TPU v7x, 1024 devices: a whole 8x8x8 slice. The times are simulated.
1024 devices in a mesh: node: 128 (over z, x, core), local: 8 (over y).
Axes of the slice: x: 8, y: 8, z: 8, core: 2. Of those that a mesh axis runs over, the one named last changes fastest.
Arguments:
- tokens: bfloat16 [2048, 4096], P('node', 'local'), may hold values from -6 to 6
- grad_out: bfloat16 [2048, 4096], P('node', 'local'), may hold values from -6 to 6
- gates: float32 [2048, 8], P('node'), may hold values from 0.1 to 1
- expert_ids: int32 [2048, 8], P('node'), may hold values from 0 to 127, all different within a row; in each aligned block of 16 rows (0 to 15, 16 to 31, ...) at most 2 rows name the same one
- w_gate: bfloat16 [128, 4096, 1024], P('node', 'local'), may hold values from -0.09375 to 0.09375
- w_up: bfloat16 [128, 4096, 1024], P('node', 'local'), may hold values from -0.09375 to 0.09375
- w_down: bfloat16 [128, 1024, 4096], P('node', None, 'local'), may hold values from -0.046875 to 0.046875
Outputs:
- grad_tokens: bfloat16 [2048, 4096], P('node', 'local')
- grad_gates: bfloat16 [2048, 8], P('node')
Inputs may be any that keep to these rules, and one draw needn't show every extreme that they name: `expert_ids`: each row names 8 different experts. Among the 16 rows of one node rank no expert is named by more than 2 rows, a bound that some block reaches.
All inputs are finite; a program needn't handle non-finite values.
Results may differ from a plain program's by a relative error of at most 0.0057.
Values may be sent and summed in bfloat16 or wider, within the bound.
No kernel may reach another device: no remote copies, remote signals or barrier semaphores. Data moves between devices by JAX's collectives and lax.ppermute only.
A program may use at most 32 MiB of HBM per device.

v0:
```python
import jax
import jax.numpy as jnp
from jax import lax
from jax.sharding import PartitionSpec as P


def local_grads(gate_pre, up_pre, back_pre, reduce_axis):
    sigmoid_gate = jax.nn.sigmoid(gate_pre)
    act = gate_pre * sigmoid_gate
    partial_gate = jnp.sum(act * up_pre * back_pre, axis=reduce_axis)
    grad_up = (back_pre * act).astype(jnp.bfloat16)
    grad_gate = (back_pre * up_pre * sigmoid_gate * (1.0 + gate_pre * (1.0 - sigmoid_gate))).astype(
        jnp.bfloat16
    )
    return (grad_gate, grad_up, partial_gate)


def on_device(tokens, grad_out, gates, expert_ids, w_gate, w_up, w_down):
    n_node = lax.axis_size("node")
    tok_rows, feature_cols = tokens.shape
    top_count = expert_ids.shape[1]
    capacity = min(tok_rows, max(2, 2 * tok_rows * top_count // n_node))
    flat_ids = expert_ids.reshape(-1)
    onehot = (flat_ids[:, None] == jnp.arange(n_node, dtype=jnp.int32)[None, :]).astype(jnp.int32)
    slot_rank = jnp.sum(onehot * (jnp.cumsum(onehot, axis=0) - 1), axis=1)
    target = flat_ids * capacity + slot_rank
    placed = (target[:, None] == jnp.arange(n_node * capacity, dtype=jnp.int32)[None, :]).astype(
        jnp.bfloat16
    )
    paired = jnp.repeat(jnp.concatenate([tokens, grad_out], axis=1), top_count, axis=0)
    outgoing = lax.dot_general(
        placed, paired, (((0,), (0,)), ((), ())), preferred_element_type=jnp.float32
    )
    outgoing = outgoing.astype(jnp.bfloat16).reshape(n_node, capacity, 2 * feature_cols)
    gate_cols = w_gate[0]
    up_cols = w_up[0]
    down_rows = w_down[0]
    incoming = lax.all_to_all(outgoing, "node", split_axis=0, concat_axis=0, tiled=True)
    sources = incoming.shape[0]
    slot_count = incoming.shape[1]
    row_count = sources * slot_count
    flat_in = incoming.reshape(row_count, 2 * feature_cols)
    x_rows = flat_in[:, :feature_cols]
    dy_rows = flat_in[:, feature_cols:]
    gate_pre = lax.dot_general(
        gate_cols, x_rows, (((0,), (1,)), ((), ())), preferred_element_type=jnp.float32
    )
    up_pre = lax.dot_general(
        up_cols, x_rows, (((0,), (1,)), ((), ())), preferred_element_type=jnp.float32
    )
    back_pre = lax.dot_general(
        down_rows, dy_rows, (((1,), (1,)), ((), ())), preferred_element_type=jnp.float32
    )
    summed = lax.psum_scatter(
        jnp.concatenate([gate_pre, up_pre, back_pre], axis=1),
        "local",
        scatter_dimension=0,
        tiled=True,
    )
    grad_gate, grad_up, partial_gate = local_grads(
        summed[:, :row_count], summed[:, row_count : 2 * row_count], summed[:, 2 * row_count :], 0
    )
    running = lax.dot_general(
        lax.all_gather(grad_gate, "local", axis=0, tiled=True),
        gate_cols,
        (((0,), (1,)), ((), ())),
        preferred_element_type=jnp.float32,
    )
    result = running + lax.dot_general(
        lax.all_gather(grad_up, "local", axis=0, tiled=True),
        up_cols,
        (((0,), (1,)), ((), ())),
        preferred_element_type=jnp.float32,
    )
    gate_total = lax.psum(partial_gate, "local").astype(jnp.bfloat16)
    sent_rows = result.astype(jnp.bfloat16).reshape(sources, slot_count, feature_cols)
    sent_gates = gate_total.reshape(sources, slot_count)
    back_rows = lax.all_to_all(sent_rows, "node", split_axis=0, concat_axis=0, tiled=True)
    back_gates = lax.all_to_all(sent_gates, "node", split_axis=0, concat_axis=0, tiled=True)
    picked = jnp.take(back_rows.reshape(n_node * capacity, feature_cols), target, axis=0)
    picked = picked.reshape(tok_rows, top_count, feature_cols).astype(jnp.float32)
    grad_tokens = jnp.sum(picked * gates[:, :, None], axis=1).astype(jnp.bfloat16)
    grad_gates = jnp.take(back_gates.reshape(-1), target, axis=0).reshape(tok_rows, top_count)
    return (grad_tokens, grad_gates)


def solution(mesh):
    in_specs = (
        P("node", "local"),
        P("node", "local"),
        P("node", None),
        P("node", None),
        P("node", "local", None),
        P("node", "local", None),
        P("node", None, "local"),
    )
    out_specs = (P("node", "local"), P("node", None))
    return jax.shard_map(
        on_device, mesh=mesh, in_specs=in_specs, out_specs=out_specs, check_vma=False
    )
```

profile of v0, /device:TPU:1, one launch (start us, length us, event | category | flops | bytes accessed | tf_op | source)
XLA Modules:
  0.0 227.1 jit_solution(8225179933572298183)
XLA Ops:
  7.2 0.0 copy-start
  7.2 0.0 reduce-scatter.2.cloned.1.call-start
  7.2 0.8 copy.17
  8.1 0.1 reshape.82
  8.2 0.1 fusion.14
  8.2 0.0 copy-start.1
  8.3 0.2 reduce_window_sum.11
  8.4 0.2 select_reduce_fusion
  8.6 0.7 pad_maximum_fusion.1
  9.4 0.4 convolution_convert_fusion
  9.8 0.2 reshape.84
  10.0 44.9 %all_to_all.20 = bf16[128,2,1024]{2,1,0:T(2,128)(2,1)} all-to-all(bf16[128,2,1024]{2,1,0:T(2,128)(2,1)S(1)} %reshape.84), channel_id=1, replica_groups=mesh['node'=128,'local'=8] {'node'}, dimensions={0} | all-to-all | bytes 1048576 | tf_op jit(solution)/shard_map/all_to_all | solution.py:38
  54.9 1.2 reshape.85
  56.2 1.7 convolution_bitcast_fusion
  57.9 0.0 copy-done.1
  57.9 0.4 convolution_bitcast_fusion.1
  58.3 0.0 copy-done
  58.3 0.4 convolution_bitcast_fusion.2
  58.8 2.1 pad_maximum_fusion
  60.8 0.0 copy-start.2
  60.8 0.0 reduce-scatter.2.cloned.1.call-update
  60.9 0.1 reduce_sum.32
  61.0 0.1 mul.73
  61.1 0.5 copy-done.2
  61.5 0.1 copy.19
  61.6 41.9 %reduce-scatter.2.cloned.1.call-done = f32[128,768]{0,1:T(8,128)} async-done(((f32[1024,768]{0,1:T(8,128)}), f32[128,768]{0,1:T(8,128)}) %reduce-scatter.2.cloned.1.call-update) | async-done | bytes 393232 | tf_op jit(solution)/shard_map/reduce_scatter | solution.py:54
  103.5 1.2 multiply_reduce_fusion.1
  104.7 20.0 %all_gather.6 = bf16[1024,256]{0,1:T(8,128)(2,1)S(1)} all-gather(bf16[128,256]{0,1:T(8,128)(2,1)S(1)} %get-tuple-element.11), channel_id=1, replica_groups=mesh['node'=128,'local'=8] {'local'}, dimensions={0}, use_global_device_ids=true | all-gather | bytes 589824 | tf_op jit(solution)/shard_map/all_gather | solution.py:64
  124.6 0.5 fusion.4
  125.1 18.2 %all_gather.7 = bf16[1024,256]{0,1:T(8,128)(2,1)S(1)} all-gather(bf16[128,256]{0,1:T(8,128)(2,1)S(1)} %get-tuple-element.12), channel_id=1, replica_groups=mesh['node'=128,'local'=8] {'local'}, dimensions={0}, use_global_device_ids=true | all-gather | bytes 589824 | tf_op jit(solution)/shard_map/all_gather | solution.py:70
  143.3 11.8 %psum.7 = bf16[256]{0:T(256)(128)(2,1)S(1)} all-reduce(f32[256]{0:T(256)S(1)} %get-tuple-element.10), channel_id=1, replica_groups=mesh['node'=128,'local'=8] {'local'}, use_global_device_ids=true, to_apply=%region_5.6 | all-reduce | flops 256 | bytes 1536 | tf_op jit(solution)/shard_map/psum | solution.py:75
  155.1 0.8 all_to_all.16
  155.9 30.0 %all-to-all-start.2 = ((bf16[128,1,2]{2,1,0:T(2,128)(2,1)}), bf16[128,1,2]{2,1,0:T(2,128)(2,1)S(1)}, u32[]{:S(2)}, u32[]{:S(2)}) async-start(bf16[128,1,2]{2,1,0:T(2,128)(2,1)} %all_to_all.16), calls=%async_computation.3 | async-start | bytes 131072 | tf_op jit(solution)/shard_map/all_to_all | solution.py:79
  185.9 0.5 fusion
  186.4 0.8 reshape.86
  187.2 10.2 %all-to-all-done.2 = bf16[128,1,2]{2,1,0:T(2,128)(2,1)S(1)} async-done(((bf16[128,1,2]{2,1,0:T(2,128)(2,1)}), bf16[128,1,2]{2,1,0:T(2,128)(2,1)S(1)}, u32[]{:S(2)}, u32[]{:S(2)}) %all-to-all-start.2) | async-done | bytes 544 | tf_op jit(solution)/shard_map/all_to_all | solution.py:79
  197.4 5.8 %all-to-all-start.1 = ((bf16[128,2,512]{2,1,0:T(2,128)(2,1)}), bf16[128,2,512]{2,1,0:T(2,128)(2,1)S(1)}, u32[]{:S(2)}, u32[]{:S(2)}) async-start(bf16[128,2,512]{2,1,0:T(2,128)(2,1)} %reshape.86), calls=%async_computation.2 | async-start | bytes 524288 | tf_op jit(solution)/shard_map/all_to_all | solution.py:78
  203.1 0.2 reduce
  203.3 0.1 reshape.88
  203.5 1.2 gather_fusion.1
  204.7 0.1 gather.15
  204.8 0.7 copy.21
  205.5 13.0 %all-to-all-done.1 = bf16[128,2,512]{2,1,0:T(2,128)(2,1)S(1)} async-done(((bf16[128,2,512]{2,1,0:T(2,128)(2,1)}), bf16[128,2,512]{2,1,0:T(2,128)(2,1)S(1)}, u32[]{:S(2)}, u32[]{:S(2)}) %all-to-all-start.1) | async-done | bytes 262176 | tf_op jit(solution)/shard_map/all_to_all | solution.py:78
  218.5 0.1 reshape.87
  218.6 0.8 gather_fusion
  219.4 0.8 multiply_reduce_fusion
  (5 shorter events, 0.0 us)
Async XLA Ops:
  7.2 51.1 %copy-start = (bf16[1,512,1024]{2,1,0:T(8,128)(2,1)S(1)}, bf16[1,512,1024]{2,1,0:T(8,128)(2,1)}, u32[]{:S(2)}) copy-start(bf16[1,512,1024]{2,1,0:T(8,128)(2,1)} %param.11) | copy-start | bytes 3145732
  7.2 96.3 %reduce-scatter.2.cloned.1.call-start = ((), (), s32[]{:S(2)}) async-start(), calls=%async_computation.4 | async-start | bytes 3538944 | tf_op jit(solution)/shard_map/reduce_scatter | solution.py:54
  8.2 49.6 %copy-start.1 = (bf16[1,512,1024]{2,1,0:T(8,128)(2,1)S(1)}, bf16[1,512,1024]{2,1,0:T(8,128)(2,1)}, u32[]{:S(2)}) copy-start(bf16[1,512,1024]{2,1,0:T(8,128)(2,1)} %param.12) | copy-start | bytes 3145732
  60.8 0.7 copy-start.2
  155.9 41.5 %all-to-all-start.2 = ((bf16[128,1,2]{2,1,0:T(2,128)(2,1)}), bf16[128,1,2]{2,1,0:T(2,128)(2,1)S(1)}, u32[]{:S(2)}, u32[]{:S(2)}) async-start(bf16[128,1,2]{2,1,0:T(2,128)(2,1)} %all_to_all.16), calls=%async_computation.3 | async-start | bytes 131072 | tf_op jit(solution)/shard_map/all_to_all | solution.py:79
  197.4 21.1 %all-to-all-start.1 = ((bf16[128,2,512]{2,1,0:T(2,128)(2,1)}), bf16[128,2,512]{2,1,0:T(2,128)(2,1)S(1)}, u32[]{:S(2)}, u32[]{:S(2)}) async-start(bf16[128,2,512]{2,1,0:T(2,128)(2,1)} %reshape.86), calls=%async_computation.2 | async-start | bytes 524288 | tf_op jit(solution)/shard_map/all_to_all | solution.py:78
Sparse Core Ops, SparseCore 0:
  61.0 42.4 reduce-scatter.1
where the time goes:
time: 228 us; the launch traced here: 227 us
  blocking collectives  94.9 us (42%)
  waiting for transfers between devices  65 us (29%)
  starting transfers between devices  35.8 us (16%)
  between operations  14.2 us (6%)
  local copies, waits for them, and re-layouts  7.76 us (3%)
  other arithmetic  5.44 us (2%)
  matrix products  3.92 us (2%)
    all_to_all x1, blocking collectives, on_device(): lax.all_to_all(outgoing, 'node', split_axis=0, concat_axis=0, tiled=True)  44.9 us
    reduce_scatter x1, waiting for transfers between devices, on_device(): lax.psum_scatter(jnp.concatenate([gate_pre, up_pre, back_pre], axis=1), '...  41.9 us
    all_to_all x1, starting transfers between devices, on_device(): lax.all_to_all(sent_gates, 'node', split_axis=0, concat_axis=0, tiled=True)  30 us
    all_gather x1, blocking collectives, on_device(): lax.all_gather(grad_gate, 'local', axis=0, tiled=True)  20 us
    all_gather x1, blocking collectives, on_device(): lax.all_gather(grad_up, 'local', axis=0, tiled=True)  18.2 us
    all_to_all x1, waiting for transfers between devices, on_device(): lax.all_to_all(sent_rows, 'node', split_axis=0, concat_axis=0, tiled=True)  13 us
    psum x1, blocking collectives, on_device(): gate_total = lax.psum(partial_gate, 'local').astype(jnp.bfloat16)  11.8 us
    all_to_all x1, waiting for transfers between devices, on_device(): lax.all_to_all(sent_gates, 'node', split_axis=0, concat_axis=0, tiled=True)  10.2 us
  transfers between devices with their start and end apart: 3, of which 3 were waited for; matrix products, arithmetic and copies ran while one was open for 2% of the time, Pallas kernels for 0%

commit v1 on v0

v1 whole, which is shorter than its diff:
```python
import functools

import jax
import jax.numpy as jnp
from jax import lax
from jax.experimental import pallas as pl
from jax.experimental.pallas import tpu as pltpu
from jax.sharding import PartitionSpec as P

BF16 = jnp.bfloat16
F32 = jnp.float32
VMEM = pl.BlockSpec(memory_space=pltpu.VMEM)
LIMIT = 40 * 1024 * 1024


def slot_choice(ids, slots, capacity):
    rows, top_count = ids.shape
    slot = lax.broadcasted_iota(jnp.int32, (rows, slots), 1)
    expert = slot // capacity
    named = jnp.zeros((rows, slots), F32)
    for k in range(top_count):
        named = named + jnp.where(ids[:, k : k + 1] == expert, 1.0, 0.0)
    before = lax.broadcasted_iota(jnp.int32, (rows, rows), 0) > lax.broadcasted_iota(
        jnp.int32, (rows, rows), 1
    )
    rank = jnp.dot(before.astype(BF16), named.astype(BF16), preferred_element_type=F32)
    return jnp.where(rank == (slot % capacity).astype(F32), named, 0.0), expert


def send_kernel(capacity, ids, tokens, grad_out, out):
    slots = out.shape[0]
    cols = tokens.shape[1]
    chosen, _ = slot_choice(ids[...], slots, capacity)
    chosen = chosen.astype(BF16)
    pick = (((0,), (0,)), ((), ()))
    out[:, :cols] = lax.dot_general(chosen, tokens[...], pick, preferred_element_type=F32).astype(BF16)
    out[:, cols:] = lax.dot_general(chosen, grad_out[...], pick, preferred_element_type=F32).astype(BF16)


def partial_kernel(n_local, index, rows_in, w_gate, w_up, w_down, *refs):
    outs, total = refs[:n_local], refs[n_local]
    cols = w_gate.shape[0]
    hidden = w_gate.shape[1]
    step = outs[0].shape[0]
    x = rows_in[:, :cols]
    dy = rows_in[:, cols:]
    total[:, :hidden] = jnp.dot(x, w_gate[...], preferred_element_type=F32)
    total[:, hidden : 2 * hidden] = jnp.dot(x, w_up[...], preferred_element_type=F32)
    total[:, 2 * hidden :] = lax.dot_general(
        dy, w_down[...], (((1,), (1,)), ((), ())), preferred_element_type=F32
    )
    me = index[0]
    for d in range(n_local):
        place = pl.multiple_of(lax.rem(me + d, n_local) * step, step)
        outs[d][...] = total[pl.ds(place, step), :].astype(outs[d].dtype)


def hidden_kernel(*refs):
    parts, out = refs[:-1], refs[-1]
    hidden = parts[0].shape[1] // 3

    def summed(start):
        value = parts[0][:, start : start + hidden].astype(F32)
        for part in parts[1:]:
            value = value + part[:, start : start + hidden].astype(F32)
        return value

    gate_pre, up_pre, back_pre = summed(0), summed(hidden), summed(2 * hidden)
    sigmoid_gate = jax.nn.sigmoid(gate_pre)
    act = gate_pre * sigmoid_gate
    grad_up = back_pre * act
    out[:, :hidden] = (
        back_pre * up_pre * sigmoid_gate * (1.0 + gate_pre * (1.0 - sigmoid_gate))
    ).astype(BF16)
    out[:, hidden : 2 * hidden] = grad_up.astype(BF16)
    gate_total = jnp.sum(grad_up * up_pre, axis=1, keepdims=True)
    extra = out.shape[1] - 2 * hidden
    out[:, 2 * hidden :] = jnp.broadcast_to(gate_total, (out.shape[0], extra)).astype(BF16)


def back_kernel(n_local, index, *refs):
    parts = refs[:n_local]
    w_gate, w_up, out, joined = refs[n_local:]
    cols, hidden = w_gate.shape
    step = parts[0].shape[0]
    me = index[0]
    for d in range(n_local):
        place = pl.multiple_of(lax.rem(me + n_local - d, n_local) * step, step)
        joined[pl.ds(place, step), :] = parts[d][...]
    across = (((1,), (1,)), ((), ()))
    result = lax.dot_general(joined[:, :hidden], w_gate[...], across, preferred_element_type=F32)
    result = result + lax.dot_general(
        joined[:, hidden : 2 * hidden], w_up[...], across, preferred_element_type=F32
    )
    out[:, :cols] = result.astype(BF16)
    out[:, cols:] = joined[:, 2 * hidden :]


def combine_kernel(capacity, ids, gates, rows_back, grad_tokens, grad_gates):
    slots = rows_back.shape[0]
    rows, cols = grad_tokens.shape
    top_count = gates.shape[1]
    named = ids[...]
    chosen, expert = slot_choice(named, slots, capacity)
    weight = jnp.zeros((rows, slots), F32)
    lane = lax.broadcasted_iota(jnp.int32, (rows, top_count), 1)
    values = jnp.zeros((rows, top_count), F32)
    for k in range(top_count):
        here = jnp.where(named[:, k : k + 1] == expert, chosen, 0.0)
        weight = weight + here * gates[:, k : k + 1]
        value = jnp.dot(here.astype(BF16), rows_back[:, cols:], preferred_element_type=F32)
        values = values + jnp.where(lane == k, value[:, :1], 0.0)
    high = weight.astype(BF16)
    rest = weight - high.astype(F32)
    middle = rest.astype(BF16)
    low = (rest - middle.astype(F32)).astype(BF16)
    total = jnp.zeros((rows, cols), F32)
    for part in (low, middle, high):
        total = total + jnp.dot(part, rows_back[:, :cols], preferred_element_type=F32)
    grad_tokens[...] = total.astype(BF16)
    grad_gates[...] = values.astype(BF16)


def on_device(tokens, grad_out, gates, expert_ids, w_gate, w_up, w_down):
    n_node = lax.axis_size("node")
    n_local = lax.axis_size("local")
    tok_rows, cols = tokens.shape
    top_count = expert_ids.shape[1]
    capacity = min(tok_rows, max(2, 2 * tok_rows * top_count // n_node))
    slots = n_node * capacity
    step = slots // n_local
    hidden = w_gate.shape[2]
    extra = 128
    shape = jax.ShapeDtypeStruct
    index = lax.axis_index("local").astype(jnp.int32).reshape(1)
    smem = pl.BlockSpec(memory_space=pltpu.SMEM)

    def build(kernel, out_shape, in_specs, flops, moved, scratch=()):
        return pl.pallas_call(
            kernel,
            out_shape=out_shape,
            in_specs=in_specs,
            out_specs=jax.tree.map(lambda _: VMEM, out_shape),
            scratch_shapes=list(scratch),
            compiler_params=pltpu.CompilerParams(vmem_limit_bytes=LIMIT),
            cost_estimate=pl.CostEstimate(flops=flops, bytes_accessed=moved, transcendentals=0),
        )

    outgoing = build(
        functools.partial(send_kernel, capacity),
        shape((slots, 2 * cols), BF16),
        [VMEM] * 3,
        2 * slots * tok_rows * 2 * cols,
        4 * slots * cols,
    )(expert_ids, tokens, grad_out)
    incoming = lax.all_to_all(
        outgoing.reshape(n_node, capacity, 2 * cols), "node", split_axis=0, concat_axis=0, tiled=True
    ).reshape(slots, 2 * cols)

    partials = build(
        functools.partial(partial_kernel, n_local),
        [shape((step, 3 * hidden), BF16) for _ in range(n_local)],
        [smem] + [VMEM] * 4,
        6 * slots * cols * hidden,
        2 * (3 * cols * hidden + slots * (2 * cols + 3 * hidden)),
        [pltpu.VMEM((slots, 3 * hidden), F32)],
    )(index, incoming, w_gate[0], w_up[0], w_down[0])

    def shifted(value, d):
        return lax.ppermute(value, "local", [(k, (k + d) % n_local) for k in range(n_local)])

    arrived = [partials[0]] + [shifted(partials[d], d) for d in range(1, n_local)]
    mine = build(
        hidden_kernel,
        shape((step, 2 * hidden + extra), BF16),
        [VMEM] * n_local,
        40 * step * hidden,
        2 * step * hidden * (3 * n_local + 2),
    )(*arrived)
    gathered = [mine] + [shifted(mine, d) for d in range(1, n_local)]
    sent = build(
        functools.partial(back_kernel, n_local),
        shape((slots, cols + extra), BF16),
        [smem] + [VMEM] * (n_local + 2),
        4 * slots * cols * hidden,
        2 * (2 * cols * hidden + slots * (2 * hidden + cols)),
        [pltpu.VMEM((slots, 2 * hidden + extra), BF16)],
    )(index, *gathered, w_gate[0], w_up[0])
    back = lax.all_to_all(
        sent.reshape(n_node, capacity, cols + extra), "node", split_axis=0, concat_axis=0, tiled=True
    ).reshape(slots, cols + extra)
    grad_tokens, grad_gates = build(
        functools.partial(combine_kernel, capacity),
        [shape((tok_rows, cols), BF16), shape((tok_rows, top_count), BF16)],
        [VMEM] * 3,
        8 * tok_rows * slots * cols,
        2 * slots * cols,
    )(expert_ids, gates, back)
    return grad_tokens, grad_gates


def solution(mesh):
    in_specs = (
        P("node", "local"),
        P("node", "local"),
        P("node", None),
        P("node", None),
        P("node", "local", None),
        P("node", "local", None),
        P("node", None, "local"),
    )
    out_specs = (P("node", "local"), P("node", None))
    return jax.shard_map(
        on_device, mesh=mesh, in_specs=in_specs, out_specs=out_specs, check_vma=False
    )
```

time: 228 us -> 170 us (0.75)
  the two profiles are of different devices: /device:TPU:1 before, /device:TPU:33 now
where the time goes in v1:
time: 170 us; the launch traced here: 169 us
  starting transfers between devices  80.4 us (47%)
  waiting for transfers between devices  78 us (46%)
  local copies, waits for them, and re-layouts  6.32 us (4%)
  Pallas kernels  3.84 us (2%)
    ppermute x14, starting transfers between devices, shifted(): lax.ppermute(value, 'local', [(k, (k + d) % n_local) for k in range(n_loc...  50.8 us
    ppermute x14, waiting for transfers between devices, shifted(): lax.ppermute(value, 'local', [(k, (k + d) % n_local) for k in range(n_loc...  40.8 us
    all_to_all x1, starting transfers between devices, on_device(): lax.all_to_all(outgoing.reshape(n_node, capacity, 2 * cols), 'node', spli...  23.7 us
    all_to_all x1, waiting for transfers between devices, on_device(): lax.all_to_all(outgoing.reshape(n_node, capacity, 2 * cols), 'node', spli...  20.6 us
    all_to_all x1, waiting for transfers between devices, on_device(): lax.all_to_all(sent.reshape(n_node, capacity, cols + extra), 'node', spli...  16.6 us
    all_to_all x1, starting transfers between devices, on_device(): lax.all_to_all(sent.reshape(n_node, capacity, cols + extra), 'node', spli...  5.86 us
    unnamed x14, local copies, waits for them, and re-layouts  3.5 us
  transfers between devices with their start and end apart: 16, of which 9 were waited for; matrix products, arithmetic and copies ran while one was open for 0% of the time, Pallas kernels for 0%

profile of v1, /device:TPU:33, one launch (start us, length us, event | category | flops | bytes accessed | tf_op | source)
XLA Modules:
  0.0 169.4 jit_solution(2070056165024090522)
XLA Ops:
  0.6 0.8 copy.10.ids
  1.4 0.0 copy-start.3
  1.4 0.7 copy-done.3
  2.1 0.0 copy-start.4
  2.1 0.7 copy-done.4
  2.8 0.5 shard_map.86
  3.4 1.0 reshape.20
  4.4 0.0 copy-start
  4.4 0.0 copy-start.1
  4.4 23.7 %all-to-all-start = ((bf16[128,2,1024]{2,1,0:T(2,128)(2,1)}), bf16[128,2,1024]{2,1,0:T(2,128)(2,1)S(1)}, u32[]{:S(2)}, u32[]{:S(2)}) async-start(bf16[128,2,1024]{2,1,0:T(2,128)(2,1)} %reshape.20), calls=%async_computation | async-start | bytes 1048576 | tf_op jit(solution)/shard_map/all_to_all | solution.py:156
  28.1 20.6 %all-to-all-done = bf16[128,2,1024]{2,1,0:T(2,128)(2,1)S(1)} async-done(((bf16[128,2,1024]{2,1,0:T(2,128)(2,1)}), bf16[128,2,1024]{2,1,0:T(2,128)(2,1)S(1)}, u32[]{:S(2)}, u32[]{:S(2)}) %all-to-all-start) | async-done | bytes 524320 | tf_op jit(solution)/shard_map/all_to_all | solution.py:156
  48.7 0.2 reshape.21.rows_in
  48.9 0.0 copy-done
  48.9 0.0 copy-done.1
  48.9 0.0 copy-start.2
  48.9 1.2 copy-done.2
  50.1 1.1 shard_map.87
  51.3 3.3 %collective-permute-start = (bf16[32,3072]{1,0:T(8,128)(2,1)S(1)}, bf16[32,3072]{1,0:T(8,128)(2,1)S(1)}, u32[]{:S(2)}, u32[]{:S(2)}) collective-permute-start(bf16[32,3072]{1,0:T(8,128)(2,1)S(1)} %get-tuple-element.11), channel_id=1, source_target_pairs={{0,1},{1,2},{2,3},{3,4},{4,5},{5,6},{6,7},{7,0},{8,9},{9,10},{10,1... | collective-permute-start | bytes 589832 | tf_op jit(solution)/shard_map/ppermute | solution.py:170
  54.6 4.8 %collective-permute-start.1 = (bf16[32,3072]{1,0:T(8,128)(2,1)S(1)}, bf16[32,3072]{1,0:T(8,128)(2,1)S(1)}, u32[]{:S(2)}, u32[]{:S(2)}) collective-permute-start(bf16[32,3072]{1,0:T(8,128)(2,1)S(1)} %get-tuple-element.12), channel_id=1, source_target_pairs={{0,2},{1,3},{2,4},{3,5},{4,6},{5,7},{6,0},{7,1},{8,10},{9,11},{10,... | collective-permute-start | bytes 589832 | tf_op jit(solution)/shard_map/ppermute | solution.py:170
  59.4 2.4 %collective-permute-start.2 = (bf16[32,3072]{1,0:T(8,128)(2,1)S(1)}, bf16[32,3072]{1,0:T(8,128)(2,1)S(1)}, u32[]{:S(2)}, u32[]{:S(2)}) collective-permute-start(bf16[32,3072]{1,0:T(8,128)(2,1)S(1)} %get-tuple-element.13), channel_id=1, source_target_pairs={{0,3},{1,4},{2,5},{3,6},{4,7},{5,0},{6,1},{7,2},{8,11},{9,12},{10,... | collective-permute-start | bytes 589832 | tf_op jit(solution)/shard_map/ppermute | solution.py:170
  61.8 6.6 %collective-permute-start.3 = (bf16[32,3072]{1,0:T(8,128)(2,1)S(1)}, bf16[32,3072]{1,0:T(8,128)(2,1)S(1)}, u32[]{:S(2)}, u32[]{:S(2)}) collective-permute-start(bf16[32,3072]{1,0:T(8,128)(2,1)S(1)} %get-tuple-element.14), channel_id=1, source_target_pairs={{0,4},{1,5},{2,6},{3,7},{4,0},{5,1},{6,2},{7,3},{8,12},{9,13},{10,... | collective-permute-start | bytes 589832 | tf_op jit(solution)/shard_map/ppermute | solution.py:170
  68.4 1.9 %collective-permute-start.4 = (bf16[32,3072]{1,0:T(8,128)(2,1)S(1)}, bf16[32,3072]{1,0:T(8,128)(2,1)S(1)}, u32[]{:S(2)}, u32[]{:S(2)}) collective-permute-start(bf16[32,3072]{1,0:T(8,128)(2,1)S(1)} %get-tuple-element.15), channel_id=1, source_target_pairs={{0,5},{1,6},{2,7},{3,0},{4,1},{5,2},{6,3},{7,4},{8,13},{9,14},{10,... | collective-permute-start | bytes 589832 | tf_op jit(solution)/shard_map/ppermute | solution.py:170
  70.3 0.0 collective-permute-done.refs_1_
  70.3 4.0 %collective-permute-start.5 = (bf16[32,3072]{1,0:T(8,128)(2,1)S(1)}, bf16[32,3072]{1,0:T(8,128)(2,1)S(1)}, u32[]{:S(2)}, u32[]{:S(2)}) collective-permute-start(bf16[32,3072]{1,0:T(8,128)(2,1)S(1)} %get-tuple-element.16), channel_id=1, source_target_pairs={{0,6},{1,7},{2,0},{3,1},{4,2},{5,3},{6,4},{7,5},{8,14},{9,15},{10,... | collective-permute-start | bytes 589832 | tf_op jit(solution)/shard_map/ppermute | solution.py:170
  74.4 0.0 collective-permute-done.1.refs_2_
  74.4 2.9 %collective-permute-start.6 = (bf16[32,3072]{1,0:T(8,128)(2,1)S(1)}, bf16[32,3072]{1,0:T(8,128)(2,1)S(1)}, u32[]{:S(2)}, u32[]{:S(2)}) collective-permute-start(bf16[32,3072]{1,0:T(8,128)(2,1)S(1)} %get-tuple-element.17), channel_id=1, source_target_pairs={{0,7},{1,0},{2,1},{3,2},{4,3},{5,4},{6,5},{7,6},{8,15},{9,8},{10,9... | collective-permute-start | bytes 589832 | tf_op jit(solution)/shard_map/ppermute | solution.py:170
  77.2 7.5 %collective-permute-done.2.refs_3_ = bf16[32,3072]{1,0:T(8,128)(2,1)S(1)} collective-permute-done((bf16[32,3072]{1,0:T(8,128)(2,1)S(1)}, bf16[32,3072]{1,0:T(8,128)(2,1)S(1)}, u32[]{:S(2)}, u32[]{:S(2)}) %collective-permute-start.2) | collective-permute-done | bytes 196640 | tf_op jit(solution)/shard_map/ppermute | solution.py:170
  84.7 8.1 %collective-permute-done.3.refs_4_ = bf16[32,3072]{1,0:T(8,128)(2,1)S(1)} collective-permute-done((bf16[32,3072]{1,0:T(8,128)(2,1)S(1)}, bf16[32,3072]{1,0:T(8,128)(2,1)S(1)}, u32[]{:S(2)}, u32[]{:S(2)}) %collective-permute-start.3) | collective-permute-done | bytes 196640 | tf_op jit(solution)/shard_map/ppermute | solution.py:170
  92.9 0.0 collective-permute-done.4.refs_5_
  92.9 6.8 %collective-permute-done.5.refs_6_ = bf16[32,3072]{1,0:T(8,128)(2,1)S(1)} collective-permute-done((bf16[32,3072]{1,0:T(8,128)(2,1)S(1)}, bf16[32,3072]{1,0:T(8,128)(2,1)S(1)}, u32[]{:S(2)}, u32[]{:S(2)}) %collective-permute-start.5) | collective-permute-done | bytes 196640 | tf_op jit(solution)/shard_map/ppermute | solution.py:170
  99.7 3.3 %collective-permute-done.6.refs_7_ = bf16[32,3072]{1,0:T(8,128)(2,1)S(1)} collective-permute-done((bf16[32,3072]{1,0:T(8,128)(2,1)S(1)}, bf16[32,3072]{1,0:T(8,128)(2,1)S(1)}, u32[]{:S(2)}, u32[]{:S(2)}) %collective-permute-start.6) | collective-permute-done | bytes 196640 | tf_op jit(solution)/shard_map/ppermute | solution.py:170
  103.0 0.3 shard_map.88.refs_0_
  103.3 2.7 %collective-permute-start.10 = (bf16[32,2176]{1,0:T(8,128)(2,1)S(1)}, bf16[32,2176]{1,0:T(8,128)(2,1)S(1)}, u32[]{:S(2)}, u32[]{:S(2)}) collective-permute-start(bf16[32,2176]{1,0:T(8,128)(2,1)S(1)} %shard_map.88.refs_0_), channel_id=1, source_target_pairs={{0,4},{1,5},{2,6},{3,7},{4,0},{5,1},{6,2},{7,3},{8,12},{9,13},{10,... | collective-permute-start | bytes 417800 | tf_op jit(solution)/shard_map/ppermute | solution.py:170
  106.0 6.5 %collective-permute-start.11 = (bf16[32,2176]{1,0:T(8,128)(2,1)S(1)}, bf16[32,2176]{1,0:T(8,128)(2,1)S(1)}, u32[]{:S(2)}, u32[]{:S(2)}) collective-permute-start(bf16[32,2176]{1,0:T(8,128)(2,1)S(1)} %shard_map.88.refs_0_), channel_id=1, source_target_pairs={{0,5},{1,6},{2,7},{3,0},{4,1},{5,2},{6,3},{7,4},{8,13},{9,14},{10,... | collective-permute-start | bytes 417800 | tf_op jit(solution)/shard_map/ppermute | solution.py:170
  112.5 3.8 %collective-permute-start.12 = (bf16[32,2176]{1,0:T(8,128)(2,1)S(1)}, bf16[32,2176]{1,0:T(8,128)(2,1)S(1)}, u32[]{:S(2)}, u32[]{:S(2)}) collective-permute-start(bf16[32,2176]{1,0:T(8,128)(2,1)S(1)} %shard_map.88.refs_0_), channel_id=1, source_target_pairs={{0,6},{1,7},{2,0},{3,1},{4,2},{5,3},{6,4},{7,5},{8,14},{9,15},{10,... | collective-permute-start | bytes 417800 | tf_op jit(solution)/shard_map/ppermute | solution.py:170
  116.3 1.9 %collective-permute-start.13 = (bf16[32,2176]{1,0:T(8,128)(2,1)S(1)}, bf16[32,2176]{1,0:T(8,128)(2,1)S(1)}, u32[]{:S(2)}, u32[]{:S(2)}) collective-permute-start(bf16[32,2176]{1,0:T(8,128)(2,1)S(1)} %shard_map.88.refs_0_), channel_id=1, source_target_pairs={{0,7},{1,0},{2,1},{3,2},{4,3},{5,4},{6,5},{7,6},{8,15},{9,8},{10,9... | collective-permute-start | bytes 417800 | tf_op jit(solution)/shard_map/ppermute | solution.py:170
  118.2 3.4 %collective-permute-start.7 = (bf16[32,2176]{1,0:T(8,128)(2,1)S(1)}, bf16[32,2176]{1,0:T(8,128)(2,1)S(1)}, u32[]{:S(2)}, u32[]{:S(2)}) collective-permute-start(bf16[32,2176]{1,0:T(8,128)(2,1)S(1)} %shard_map.88.refs_0_), channel_id=1, source_target_pairs={{0,1},{1,2},{2,3},{3,4},{4,5},{5,6},{6,7},{7,0},{8,9},{9,10},{10,1... | collective-permute-start | bytes 417800 | tf_op jit(solution)/shard_map/ppermute | solution.py:170
  121.6 0.0 collective-permute-done.10.refs_4_
  121.6 3.6 %collective-permute-start.8 = (bf16[32,2176]{1,0:T(8,128)(2,1)S(1)}, bf16[32,2176]{1,0:T(8,128)(2,1)S(1)}, u32[]{:S(2)}, u32[]{:S(2)}) collective-permute-start(bf16[32,2176]{1,0:T(8,128)(2,1)S(1)} %shard_map.88.refs_0_), channel_id=1, source_target_pairs={{0,2},{1,3},{2,4},{3,5},{4,6},{5,7},{6,0},{7,1},{8,10},{9,11},{10,... | collective-permute-start | bytes 417800 | tf_op jit(solution)/shard_map/ppermute | solution.py:170
  125.2 0.0 collective-permute-done.11.refs_5_
  125.2 3.1 %collective-permute-start.9 = (bf16[32,2176]{1,0:T(8,128)(2,1)S(1)}, bf16[32,2176]{1,0:T(8,128)(2,1)S(1)}, u32[]{:S(2)}, u32[]{:S(2)}) collective-permute-start(bf16[32,2176]{1,0:T(8,128)(2,1)S(1)} %shard_map.88.refs_0_), channel_id=1, source_target_pairs={{0,3},{1,4},{2,5},{3,6},{4,7},{5,0},{6,1},{7,2},{8,11},{9,12},{10,... | collective-permute-start | bytes 417800 | tf_op jit(solution)/shard_map/ppermute | solution.py:170
  128.4 4.7 %collective-permute-done.12.refs_6_ = bf16[32,2176]{1,0:T(8,128)(2,1)S(1)} collective-permute-done((bf16[32,2176]{1,0:T(8,128)(2,1)S(1)}, bf16[32,2176]{1,0:T(8,128)(2,1)S(1)}, u32[]{:S(2)}, u32[]{:S(2)}) %collective-permute-start.12) | collective-permute-done | bytes 139296 | tf_op jit(solution)/shard_map/ppermute | solution.py:170
  133.1 0.6 collective-permute-done.13.refs_7_
  133.6 0.0 collective-permute-done.7.refs_1_
  133.6 0.0 collective-permute-done.8.refs_2_
  133.6 9.7 %collective-permute-done.9.refs_3_ = bf16[32,2176]{1,0:T(8,128)(2,1)S(1)} collective-permute-done((bf16[32,2176]{1,0:T(8,128)(2,1)S(1)}, bf16[32,2176]{1,0:T(8,128)(2,1)S(1)}, u32[]{:S(2)}, u32[]{:S(2)}) %collective-permute-start.9) | collective-permute-done | bytes 139296 | tf_op jit(solution)/shard_map/ppermute | solution.py:170
  143.4 0.8 shard_map.89
  144.2 0.8 reshape.22
  145.0 0.0 copy-start.5
  145.0 5.9 %all-to-all-start.1 = ((bf16[128,2,640]{2,1,0:T(2,128)(2,1)}), bf16[128,2,640]{2,1,0:T(2,128)(2,1)S(1)}, u32[]{:S(2)}, u32[]{:S(2)}) async-start(bf16[128,2,640]{2,1,0:T(2,128)(2,1)} %reshape.22), calls=%async_computation.1 | async-start | bytes 655360 | tf_op jit(solution)/shard_map/all_to_all | solution.py:189
  150.9 0.0 copy-done.5
  150.9 0.1 copy.11.gates
  151.0 16.6 %all-to-all-done.1 = bf16[128,2,640]{2,1,0:T(2,128)(2,1)S(1)} async-done(((bf16[128,2,640]{2,1,0:T(2,128)(2,1)}), bf16[128,2,640]{2,1,0:T(2,128)(2,1)S(1)}, u32[]{:S(2)}, u32[]{:S(2)}) %all-to-all-start.1) | async-done | bytes 327712 | tf_op jit(solution)/shard_map/all_to_all | solution.py:189
  167.6 0.1 reshape.23.rows_back
  167.7 1.1 shard_map.90
  168.8 0.7 copy.12
Async XLA Ops:
  1.4 0.7 copy-start.3
  2.1 0.7 copy-start.4
  4.4 44.5 %copy-start = (bf16[1,512,1024]{2,1,0:T(8,128)(2,1)S(1)}, bf16[1,512,1024]{2,1,0:T(8,128)(2,1)}, u32[]{:S(2)}) copy-start(bf16[1,512,1024]{2,1,0:T(8,128)(2,1)} %param.11) | copy-start | bytes 3145732
  4.4 44.5 %copy-start.1 = (bf16[1,512,1024]{2,1,0:T(8,128)(2,1)S(1)}, bf16[1,512,1024]{2,1,0:T(8,128)(2,1)}, u32[]{:S(2)}) copy-start(bf16[1,512,1024]{2,1,0:T(8,128)(2,1)} %param.12) | copy-start | bytes 3145732
  4.4 44.3 %all-to-all-start = ((bf16[128,2,1024]{2,1,0:T(2,128)(2,1)}), bf16[128,2,1024]{2,1,0:T(2,128)(2,1)S(1)}, u32[]{:S(2)}, u32[]{:S(2)}) async-start(bf16[128,2,1024]{2,1,0:T(2,128)(2,1)} %reshape.20), calls=%async_computation | async-start | bytes 1048576 | tf_op jit(solution)/shard_map/all_to_all | solution.py:156
  48.9 1.2 copy-start.2
  51.3 19.0 %collective-permute-start = (bf16[32,3072]{1,0:T(8,128)(2,1)S(1)}, bf16[32,3072]{1,0:T(8,128)(2,1)S(1)}, u32[]{:S(2)}, u32[]{:S(2)}) collective-permute-start(bf16[32,3072]{1,0:T(8,128)(2,1)S(1)} %get-tuple-element.11), channel_id=1, source_target_pairs={{0,1},{1,2},{2,3},{3,4},{4,5},{5,6},{6,7},{7,0},{8,9},{9,10},{10,1... | collective-permute-start | bytes 589832 | tf_op jit(solution)/shard_map/ppermute | solution.py:170
  54.6 19.7 %collective-permute-start.1 = (bf16[32,3072]{1,0:T(8,128)(2,1)S(1)}, bf16[32,3072]{1,0:T(8,128)(2,1)S(1)}, u32[]{:S(2)}, u32[]{:S(2)}) collective-permute-start(bf16[32,3072]{1,0:T(8,128)(2,1)S(1)} %get-tuple-element.12), channel_id=1, source_target_pairs={{0,2},{1,3},{2,4},{3,5},{4,6},{5,7},{6,0},{7,1},{8,10},{9,11},{10,... | collective-permute-start | bytes 589832 | tf_op jit(solution)/shard_map/ppermute | solution.py:170
  59.4 25.3 %collective-permute-start.2 = (bf16[32,3072]{1,0:T(8,128)(2,1)S(1)}, bf16[32,3072]{1,0:T(8,128)(2,1)S(1)}, u32[]{:S(2)}, u32[]{:S(2)}) collective-permute-start(bf16[32,3072]{1,0:T(8,128)(2,1)S(1)} %get-tuple-element.13), channel_id=1, source_target_pairs={{0,3},{1,4},{2,5},{3,6},{4,7},{5,0},{6,1},{7,2},{8,11},{9,12},{10,... | collective-permute-start | bytes 589832 | tf_op jit(solution)/shard_map/ppermute | solution.py:170
  61.8 31.1 %collective-permute-start.3 = (bf16[32,3072]{1,0:T(8,128)(2,1)S(1)}, bf16[32,3072]{1,0:T(8,128)(2,1)S(1)}, u32[]{:S(2)}, u32[]{:S(2)}) collective-permute-start(bf16[32,3072]{1,0:T(8,128)(2,1)S(1)} %get-tuple-element.14), channel_id=1, source_target_pairs={{0,4},{1,5},{2,6},{3,7},{4,0},{5,1},{6,2},{7,3},{8,12},{9,13},{10,... | collective-permute-start | bytes 589832 | tf_op jit(solution)/shard_map/ppermute | solution.py:170
  68.4 24.5 %collective-permute-start.4 = (bf16[32,3072]{1,0:T(8,128)(2,1)S(1)}, bf16[32,3072]{1,0:T(8,128)(2,1)S(1)}, u32[]{:S(2)}, u32[]{:S(2)}) collective-permute-start(bf16[32,3072]{1,0:T(8,128)(2,1)S(1)} %get-tuple-element.15), channel_id=1, source_target_pairs={{0,5},{1,6},{2,7},{3,0},{4,1},{5,2},{6,3},{7,4},{8,13},{9,14},{10,... | collective-permute-start | bytes 589832 | tf_op jit(solution)/shard_map/ppermute | solution.py:170
  70.3 29.4 %collective-permute-start.5 = (bf16[32,3072]{1,0:T(8,128)(2,1)S(1)}, bf16[32,3072]{1,0:T(8,128)(2,1)S(1)}, u32[]{:S(2)}, u32[]{:S(2)}) collective-permute-start(bf16[32,3072]{1,0:T(8,128)(2,1)S(1)} %get-tuple-element.16), channel_id=1, source_target_pairs={{0,6},{1,7},{2,0},{3,1},{4,2},{5,3},{6,4},{7,5},{8,14},{9,15},{10,... | collective-permute-start | bytes 589832 | tf_op jit(solution)/shard_map/ppermute | solution.py:170
  74.4 28.6 %collective-permute-start.6 = (bf16[32,3072]{1,0:T(8,128)(2,1)S(1)}, bf16[32,3072]{1,0:T(8,128)(2,1)S(1)}, u32[]{:S(2)}, u32[]{:S(2)}) collective-permute-start(bf16[32,3072]{1,0:T(8,128)(2,1)S(1)} %get-tuple-element.17), channel_id=1, source_target_pairs={{0,7},{1,0},{2,1},{3,2},{4,3},{5,4},{6,5},{7,6},{8,15},{9,8},{10,9... | collective-permute-start | bytes 589832 | tf_op jit(solution)/shard_map/ppermute | solution.py:170
  103.3 18.3 %collective-permute-start.10 = (bf16[32,2176]{1,0:T(8,128)(2,1)S(1)}, bf16[32,2176]{1,0:T(8,128)(2,1)S(1)}, u32[]{:S(2)}, u32[]{:S(2)}) collective-permute-start(bf16[32,2176]{1,0:T(8,128)(2,1)S(1)} %shard_map.88.refs_0_), channel_id=1, source_target_pairs={{0,4},{1,5},{2,6},{3,7},{4,0},{5,1},{6,2},{7,3},{8,12},{9,13},{10,... | collective-permute-start | bytes 417800 | tf_op jit(solution)/shard_map/ppermute | solution.py:170
  106.0 19.3 %collective-permute-start.11 = (bf16[32,2176]{1,0:T(8,128)(2,1)S(1)}, bf16[32,2176]{1,0:T(8,128)(2,1)S(1)}, u32[]{:S(2)}, u32[]{:S(2)}) collective-permute-start(bf16[32,2176]{1,0:T(8,128)(2,1)S(1)} %shard_map.88.refs_0_), channel_id=1, source_target_pairs={{0,5},{1,6},{2,7},{3,0},{4,1},{5,2},{6,3},{7,4},{8,13},{9,14},{10,... | collective-permute-start | bytes 417800 | tf_op jit(solution)/shard_map/ppermute | solution.py:170
  112.5 20.6 %collective-permute-start.12 = (bf16[32,2176]{1,0:T(8,128)(2,1)S(1)}, bf16[32,2176]{1,0:T(8,128)(2,1)S(1)}, u32[]{:S(2)}, u32[]{:S(2)}) collective-permute-start(bf16[32,2176]{1,0:T(8,128)(2,1)S(1)} %shard_map.88.refs_0_), channel_id=1, source_target_pairs={{0,6},{1,7},{2,0},{3,1},{4,2},{5,3},{6,4},{7,5},{8,14},{9,15},{10,... | collective-permute-start | bytes 417800 | tf_op jit(solution)/shard_map/ppermute | solution.py:170
  116.3 17.3 %collective-permute-start.13 = (bf16[32,2176]{1,0:T(8,128)(2,1)S(1)}, bf16[32,2176]{1,0:T(8,128)(2,1)S(1)}, u32[]{:S(2)}, u32[]{:S(2)}) collective-permute-start(bf16[32,2176]{1,0:T(8,128)(2,1)S(1)} %shard_map.88.refs_0_), channel_id=1, source_target_pairs={{0,7},{1,0},{2,1},{3,2},{4,3},{5,4},{6,5},{7,6},{8,15},{9,8},{10,9... | collective-permute-start | bytes 417800 | tf_op jit(solution)/shard_map/ppermute | solution.py:170
  118.2 15.4 %collective-permute-start.7 = (bf16[32,2176]{1,0:T(8,128)(2,1)S(1)}, bf16[32,2176]{1,0:T(8,128)(2,1)S(1)}, u32[]{:S(2)}, u32[]{:S(2)}) collective-permute-start(bf16[32,2176]{1,0:T(8,128)(2,1)S(1)} %shard_map.88.refs_0_), channel_id=1, source_target_pairs={{0,1},{1,2},{2,3},{3,4},{4,5},{5,6},{6,7},{7,0},{8,9},{9,10},{10,1... | collective-permute-start | bytes 417800 | tf_op jit(solution)/shard_map/ppermute | solution.py:170
  121.6 12.0 %collective-permute-start.8 = (bf16[32,2176]{1,0:T(8,128)(2,1)S(1)}, bf16[32,2176]{1,0:T(8,128)(2,1)S(1)}, u32[]{:S(2)}, u32[]{:S(2)}) collective-permute-start(bf16[32,2176]{1,0:T(8,128)(2,1)S(1)} %shard_map.88.refs_0_), channel_id=1, source_target_pairs={{0,2},{1,3},{2,4},{3,5},{4,6},{5,7},{6,0},{7,1},{8,10},{9,11},{10,... | collective-permute-start | bytes 417800 | tf_op jit(solution)/shard_map/ppermute | solution.py:170
  125.2 18.1 %collective-permute-start.9 = (bf16[32,2176]{1,0:T(8,128)(2,1)S(1)}, bf16[32,2176]{1,0:T(8,128)(2,1)S(1)}, u32[]{:S(2)}, u32[]{:S(2)}) collective-permute-start(bf16[32,2176]{1,0:T(8,128)(2,1)S(1)} %shard_map.88.refs_0_), channel_id=1, source_target_pairs={{0,3},{1,4},{2,5},{3,6},{4,7},{5,0},{6,1},{7,2},{8,11},{9,12},{10,... | collective-permute-start | bytes 417800 | tf_op jit(solution)/shard_map/ppermute | solution.py:170
  145.0 5.9 %copy-start.5 = (f32[16,8]{0,1:T(8,128)S(1)}, f32[16,8]{0,1:T(8,128)}, u32[]{:S(2)}) copy-start(f32[16,8]{0,1:T(8,128)} %param.9) | copy-start | bytes 1540
  145.0 22.6 %all-to-all-start.1 = ((bf16[128,2,640]{2,1,0:T(2,128)(2,1)}), bf16[128,2,640]{2,1,0:T(2,128)(2,1)S(1)}, u32[]{:S(2)}, u32[]{:S(2)}) async-start(bf16[128,2,640]{2,1,0:T(2,128)(2,1)} %reshape.22), calls=%async_computation.1 | async-start | bytes 655360 | tf_op jit(solution)/shard_map/all_to_all | solution.py:189

commit v2 on v1

--- a/solution.py
+++ b/solution.py
@@ -14,16 +14,17 @@
 
 
 def slot_choice(ids, slots, capacity):
-    rows, top_count = ids.shape
-    slot = lax.broadcasted_iota(jnp.int32, (rows, slots), 1)
+    top_count, rows = ids.shape
+    slot = lax.broadcasted_iota(jnp.int32, (slots, rows), 0)
     expert = slot // capacity
-    named = jnp.zeros((rows, slots), F32)
+    named = jnp.zeros((slots, rows), F32)
     for k in range(top_count):
-        named = named + jnp.where(ids[:, k : k + 1] == expert, 1.0, 0.0)
-    before = lax.broadcasted_iota(jnp.int32, (rows, rows), 0) > lax.broadcasted_iota(
+        named = named + jnp.where(ids[k : k + 1, :] == expert, 1.0, 0.0)
+    before = lax.broadcasted_iota(jnp.int32, (rows, rows), 0) < lax.broadcasted_iota(
         jnp.int32, (rows, rows), 1
     )
-    rank = jnp.dot(before.astype(BF16), named.astype(BF16), preferred_element_type=F32)
+    before = jnp.where(before, 1.0, 0.0).astype(BF16)
+    rank = jnp.dot(named.astype(BF16), before, preferred_element_type=F32)
     return jnp.where(rank == (slot % capacity).astype(F32), named, 0.0), expert
 
 
@@ -32,13 +33,14 @@
     cols = tokens.shape[1]
     chosen, _ = slot_choice(ids[...], slots, capacity)
     chosen = chosen.astype(BF16)
-    pick = (((0,), (0,)), ((), ()))
-    out[:, :cols] = lax.dot_general(chosen, tokens[...], pick, preferred_element_type=F32).astype(BF16)
-    out[:, cols:] = lax.dot_general(chosen, grad_out[...], pick, preferred_element_type=F32).astype(BF16)
-
-
-def partial_kernel(n_local, index, rows_in, w_gate, w_up, w_down, *refs):
-    outs, total = refs[:n_local], refs[n_local]
+    out[:, :cols] = jnp.dot(chosen, tokens[...], preferred_element_type=F32).astype(BF16)
+    out[:, cols:] = jnp.dot(chosen, grad_out[...], preferred_element_type=F32).astype(BF16)
+
+
+def partial_kernel(order, index, rows_in, w_gate, w_up, w_down, *refs):
+    n_local = len(order)
+    outs = refs[:n_local]
+    total = refs[n_local]
     cols = w_gate.shape[0]
     hidden = w_gate.shape[1]
     step = outs[0].shape[0]
@@ -50,9 +52,9 @@
         dy, w_down[...], (((1,), (1,)), ((), ())), preferred_element_type=F32
     )
     me = index[0]
-    for d in range(n_local):
+    for d, out in zip(order, outs):
         place = pl.multiple_of(lax.rem(me + d, n_local) * step, step)
-        outs[d][...] = total[pl.ds(place, step), :].astype(outs[d].dtype)
+        out[...] = total[pl.ds(place, step), :].astype(out.dtype)
 
 
 def hidden_kernel(*refs):
@@ -78,15 +80,16 @@
     out[:, 2 * hidden :] = jnp.broadcast_to(gate_total, (out.shape[0], extra)).astype(BF16)
 
 
-def back_kernel(n_local, index, *refs):
+def back_kernel(order, index, *refs):
+    n_local = len(order)
     parts = refs[:n_local]
     w_gate, w_up, out, joined = refs[n_local:]
     cols, hidden = w_gate.shape
     step = parts[0].shape[0]
     me = index[0]
-    for d in range(n_local):
+    for d, part in zip(order, parts):
         place = pl.multiple_of(lax.rem(me + n_local - d, n_local) * step, step)
-        joined[pl.ds(place, step), :] = parts[d][...]
+        joined[pl.ds(place, step), :] = part[...]
     across = (((1,), (1,)), ((), ()))
     result = lax.dot_general(joined[:, :hidden], w_gate[...], across, preferred_element_type=F32)
     result = result + lax.dot_general(
@@ -99,26 +102,35 @@
 def combine_kernel(capacity, ids, gates, rows_back, grad_tokens, grad_gates):
     slots = rows_back.shape[0]
     rows, cols = grad_tokens.shape
-    top_count = gates.shape[1]
+    top_count = gates.shape[0]
     named = ids[...]
     chosen, expert = slot_choice(named, slots, capacity)
-    weight = jnp.zeros((rows, slots), F32)
-    lane = lax.broadcasted_iota(jnp.int32, (rows, top_count), 1)
-    values = jnp.zeros((rows, top_count), F32)
+    weight = jnp.zeros((slots, rows), F32)
+    across = (((0,), (0,)), ((), ()))
     for k in range(top_count):
-        here = jnp.where(named[:, k : k + 1] == expert, chosen, 0.0)
-        weight = weight + here * gates[:, k : k + 1]
-        value = jnp.dot(here.astype(BF16), rows_back[:, cols:], preferred_element_type=F32)
-        values = values + jnp.where(lane == k, value[:, :1], 0.0)
+        here = jnp.where(named[k : k + 1, :] == expert, chosen, 0.0)
+        weight = weight + here * gates[k : k + 1, :]
+        value = lax.dot_general(
+            rows_back[:, cols:], here.astype(BF16), across, preferred_element_type=F32
+        )
+        grad_gates[k : k + 1, :] = value[:1, :].astype(BF16)
     high = weight.astype(BF16)
     rest = weight - high.astype(F32)
     middle = rest.astype(BF16)
     low = (rest - middle.astype(F32)).astype(BF16)
     total = jnp.zeros((rows, cols), F32)
     for part in (low, middle, high):
-        total = total + jnp.dot(part, rows_back[:, :cols], preferred_element_type=F32)
+        total = total + lax.dot_general(
+            part, rows_back[:, :cols], across, preferred_element_type=F32
+        )
     grad_tokens[...] = total.astype(BF16)
-    grad_gates[...] = values.astype(BF16)
+
+
+def ring_order(n):
+    order = [0] + ([n // 2] if n % 2 == 0 and n > 1 else [])
+    for d in range((n - 1) // 2, 0, -1):
+        order += [d, n - d]
+    return order
 
 
 def on_device(tokens, grad_out, gates, expert_ids, w_gate, w_up, w_down):
@@ -134,6 +146,8 @@
     shape = jax.ShapeDtypeStruct
     index = lax.axis_index("local").astype(jnp.int32).reshape(1)
     smem = pl.BlockSpec(memory_space=pltpu.SMEM)
+    order = ring_order(n_local)
+    named = expert_ids.T
 
     def build(kernel, out_shape, in_specs, flops, moved, scratch=()):
         return pl.pallas_call(
@@ -152,13 +166,13 @@
         [VMEM] * 3,
         2 * slots * tok_rows * 2 * cols,
         4 * slots * cols,
-    )(expert_ids, tokens, grad_out)
+    )(named, tokens, grad_out)
     incoming = lax.all_to_all(
         outgoing.reshape(n_node, capacity, 2 * cols), "node", split_axis=0, concat_axis=0, tiled=True
     ).reshape(slots, 2 * cols)
 
     partials = build(
-        functools.partial(partial_kernel, n_local),
+        functools.partial(partial_kernel, order),
         [shape((step, 3 * hidden), BF16) for _ in range(n_local)],
         [smem] + [VMEM] * 4,
         6 * slots * cols * hidden,
@@ -169,7 +183,7 @@
     def shifted(value, d):
         return lax.ppermute(value, "local", [(k, (k + d) % n_local) for k in range(n_local)])
 
-    arrived = [partials[0]] + [shifted(partials[d], d) for d in range(1, n_local)]
+    arrived = [shifted(part, d) if d else part for d, part in zip(order, partials)]
     mine = build(
         hidden_kernel,
         shape((step, 2 * hidden + extra), BF16),
@@ -177,9 +191,9 @@
         40 * step * hidden,
         2 * step * hidden * (3 * n_local + 2),
     )(*arrived)
-    gathered = [mine] + [shifted(mine, d) for d in range(1, n_local)]
+    gathered = [shifted(mine, d) if d else mine for d in reversed(order)]
     sent = build(
-        functools.partial(back_kernel, n_local),
+        functools.partial(back_kernel, order[::-1]),
         shape((slots, cols + extra), BF16),
         [smem] + [VMEM] * (n_local + 2),
         4 * slots * cols * hidden,
@@ -191,12 +205,12 @@
     ).reshape(slots, cols + extra)
     grad_tokens, grad_gates = build(
         functools.partial(combine_kernel, capacity),
-        [shape((tok_rows, cols), BF16), shape((tok_rows, top_count), BF16)],
+        [shape((tok_rows, cols), BF16), shape((top_count, tok_rows), BF16)],
         [VMEM] * 3,
         8 * tok_rows * slots * cols,
         2 * slots * cols,
-    )(expert_ids, gates, back)
-    return grad_tokens, grad_gates
+    )(named, gates.T, back)
+    return grad_tokens, grad_gates.T
 
 
 def solution(mesh):

time: 170 us -> 154 us (0.906)
  the two profiles are of different devices: /device:TPU:33 before, /device:TPU:1 now
where the time goes in v2:
time: 154 us
  starting transfers between devices  80.2 us (52%)
  waiting for transfers between devices  41.2 us (27%)
  blocking collectives  22.1 us (14%)
  local copies, waits for them, and re-layouts  5.37 us (3%)
  Pallas kernels  3.88 us (3%)
    ppermute x14, starting transfers between devices, shifted(): lax.ppermute(value, 'local', [(k, (k + d) % n_local) for k in range(n_loc...  55.6 us
    all_to_all x1, starting transfers between devices, on_device(): lax.all_to_all(outgoing.reshape(n_node, capacity, 2 * cols), 'node', spli...  24.6 us
    all_to_all x1, blocking collectives, on_device(): lax.all_to_all(sent.reshape(n_node, capacity, cols + extra), 'node', spli...  22.1 us
    ppermute x14, waiting for transfers between devices, shifted(): lax.ppermute(value, 'local', [(k, (k + d) % n_local) for k in range(n_loc...  20.6 us
    all_to_all x1, waiting for transfers between devices, on_device(): lax.all_to_all(outgoing.reshape(n_node, capacity, 2 * cols), 'node', spli...  20.6 us
    unnamed x16, local copies, waits for them, and re-layouts  3.92 us
  transfers between devices with their start and end apart: 15, of which 9 were waited for; matrix products, arithmetic and copies ran while one was open for 0% of the time, Pallas kernels for 0%

profile of v2, /device:TPU:1, one launch (start us, length us, event | category | flops | bytes accessed | tf_op | source)
XLA Modules:
  0.0 153.6 jit_solution(7631718149234498494)
XLA Ops:
  0.6 0.0 copy-start.3
  0.6 0.7 copy-done.3
  1.3 0.0 copy-start.5
  1.3 0.7 copy-done.5
  2.0 0.0 copy-start.6
  2.0 0.7 copy-done.6
  2.8 0.4 shard_map.86
  3.2 1.0 reshape.20
  4.2 0.0 copy-start
  4.2 0.0 copy-start.1
  4.2 24.6 %all-to-all-start = ((bf16[128,2,1024]{2,1,0:T(2,128)(2,1)}), bf16[128,2,1024]{2,1,0:T(2,128)(2,1)S(1)}, u32[]{:S(2)}, u32[]{:S(2)}) async-start(bf16[128,2,1024]{2,1,0:T(2,128)(2,1)} %reshape.20), calls=%async_computation | async-start | bytes 1048576 | tf_op jit(solution)/shard_map/all_to_all | solution.py:170
  28.8 20.6 %all-to-all-done = bf16[128,2,1024]{2,1,0:T(2,128)(2,1)S(1)} async-done(((bf16[128,2,1024]{2,1,0:T(2,128)(2,1)}), bf16[128,2,1024]{2,1,0:T(2,128)(2,1)S(1)}, u32[]{:S(2)}, u32[]{:S(2)}) %all-to-all-start) | async-done | bytes 524320 | tf_op jit(solution)/shard_map/all_to_all | solution.py:170
  49.4 0.2 reshape.21.rows_in
  49.6 0.0 copy-done
  49.6 0.0 copy-done.1
  49.6 0.0 copy-start.2
  49.6 1.2 copy-done.2
  50.8 1.1 shard_map.87
  52.0 7.9 %collective-permute-start = (bf16[32,3072]{1,0:T(8,128)(2,1)S(1)}, bf16[32,3072]{1,0:T(8,128)(2,1)S(1)}, u32[]{:S(2)}, u32[]{:S(2)}) collective-permute-start(bf16[32,3072]{1,0:T(8,128)(2,1)S(1)} %get-tuple-element.13), channel_id=1, source_target_pairs={{0,4},{1,5},{2,6},{3,7},{4,0},{5,1},{6,2},{7,3},{8,12},{9,13},{10,... | collective-permute-start | bytes 589832 | tf_op jit(solution)/shard_map/ppermute | solution.py:184
  59.9 2.9 %collective-permute-start.1 = (bf16[32,3072]{1,0:T(8,128)(2,1)S(1)}, bf16[32,3072]{1,0:T(8,128)(2,1)S(1)}, u32[]{:S(2)}, u32[]{:S(2)}) collective-permute-start(bf16[32,3072]{1,0:T(8,128)(2,1)S(1)} %get-tuple-element.14), channel_id=1, source_target_pairs={{0,3},{1,4},{2,5},{3,6},{4,7},{5,0},{6,1},{7,2},{8,11},{9,12},{10,... | collective-permute-start | bytes 589832 | tf_op jit(solution)/shard_map/ppermute | solution.py:184
  62.8 5.4 %collective-permute-start.2 = (bf16[32,3072]{1,0:T(8,128)(2,1)S(1)}, bf16[32,3072]{1,0:T(8,128)(2,1)S(1)}, u32[]{:S(2)}, u32[]{:S(2)}) collective-permute-start(bf16[32,3072]{1,0:T(8,128)(2,1)S(1)} %get-tuple-element.15), channel_id=1, source_target_pairs={{0,5},{1,6},{2,7},{3,0},{4,1},{5,2},{6,3},{7,4},{8,13},{9,14},{10,... | collective-permute-start | bytes 589832 | tf_op jit(solution)/shard_map/ppermute | solution.py:184
  68.2 2.7 %collective-permute-start.3 = (bf16[32,3072]{1,0:T(8,128)(2,1)S(1)}, bf16[32,3072]{1,0:T(8,128)(2,1)S(1)}, u32[]{:S(2)}, u32[]{:S(2)}) collective-permute-start(bf16[32,3072]{1,0:T(8,128)(2,1)S(1)} %get-tuple-element.16), channel_id=1, source_target_pairs={{0,2},{1,3},{2,4},{3,5},{4,6},{5,7},{6,0},{7,1},{8,10},{9,11},{10,... | collective-permute-start | bytes 589832 | tf_op jit(solution)/shard_map/ppermute | solution.py:184
  70.8 4.7 %collective-permute-start.4 = (bf16[32,3072]{1,0:T(8,128)(2,1)S(1)}, bf16[32,3072]{1,0:T(8,128)(2,1)S(1)}, u32[]{:S(2)}, u32[]{:S(2)}) collective-permute-start(bf16[32,3072]{1,0:T(8,128)(2,1)S(1)} %get-tuple-element.17), channel_id=1, source_target_pairs={{0,6},{1,7},{2,0},{3,1},{4,2},{5,3},{6,4},{7,5},{8,14},{9,15},{10,... | collective-permute-start | bytes 589832 | tf_op jit(solution)/shard_map/ppermute | solution.py:184
  75.6 0.0 collective-permute-done.refs_1_
  75.6 2.4 %collective-permute-start.5 = (bf16[32,3072]{1,0:T(8,128)(2,1)S(1)}, bf16[32,3072]{1,0:T(8,128)(2,1)S(1)}, u32[]{:S(2)}, u32[]{:S(2)}) collective-permute-start(bf16[32,3072]{1,0:T(8,128)(2,1)S(1)} %get-tuple-element.18), channel_id=1, source_target_pairs={{0,1},{1,2},{2,3},{3,4},{4,5},{5,6},{6,7},{7,0},{8,9},{9,10},{10,1... | collective-permute-start | bytes 589832 | tf_op jit(solution)/shard_map/ppermute | solution.py:184
  78.0 3.3 %collective-permute-done.1.refs_2_ = bf16[32,3072]{1,0:T(8,128)(2,1)S(1)} collective-permute-done((bf16[32,3072]{1,0:T(8,128)(2,1)S(1)}, bf16[32,3072]{1,0:T(8,128)(2,1)S(1)}, u32[]{:S(2)}, u32[]{:S(2)}) %collective-permute-start.1) | collective-permute-done | bytes 196640 | tf_op jit(solution)/shard_map/ppermute | solution.py:184
  81.4 1.9 %collective-permute-start.6 = (bf16[32,3072]{1,0:T(8,128)(2,1)S(1)}, bf16[32,3072]{1,0:T(8,128)(2,1)S(1)}, u32[]{:S(2)}, u32[]{:S(2)}) collective-permute-start(bf16[32,3072]{1,0:T(8,128)(2,1)S(1)} %get-tuple-element.19), channel_id=1, source_target_pairs={{0,7},{1,0},{2,1},{3,2},{4,3},{5,4},{6,5},{7,6},{8,15},{9,8},{10,9... | collective-permute-start | bytes 589832 | tf_op jit(solution)/shard_map/ppermute | solution.py:184
  83.3 0.0 collective-permute-done.2.refs_3_
  83.3 6.4 %collective-permute-done.3.refs_4_ = bf16[32,3072]{1,0:T(8,128)(2,1)S(1)} collective-permute-done((bf16[32,3072]{1,0:T(8,128)(2,1)S(1)}, bf16[32,3072]{1,0:T(8,128)(2,1)S(1)}, u32[]{:S(2)}, u32[]{:S(2)}) %collective-permute-start.3) | collective-permute-done | bytes 196640 | tf_op jit(solution)/shard_map/ppermute | solution.py:184
  89.7 1.4 collective-permute-done.4.refs_5_
  91.2 3.4 %collective-permute-done.5.refs_6_ = bf16[32,3072]{1,0:T(8,128)(2,1)S(1)} collective-permute-done((bf16[32,3072]{1,0:T(8,128)(2,1)S(1)}, bf16[32,3072]{1,0:T(8,128)(2,1)S(1)}, u32[]{:S(2)}, u32[]{:S(2)}) %collective-permute-start.5) | collective-permute-done | bytes 196640 | tf_op jit(solution)/shard_map/ppermute | solution.py:184
  94.6 0.7 collective-permute-done.6.refs_7_
  95.3 0.3 shard_map.88.refs_7_
  95.6 5.5 %collective-permute-start.13 = (bf16[32,2176]{1,0:T(8,128)(2,1)S(1)}, bf16[32,2176]{1,0:T(8,128)(2,1)S(1)}, u32[]{:S(2)}, u32[]{:S(2)}) collective-permute-start(bf16[32,2176]{1,0:T(8,128)(2,1)S(1)} %shard_map.88.refs_7_), channel_id=1, source_target_pairs={{0,4},{1,5},{2,6},{3,7},{4,0},{5,1},{6,2},{7,3},{8,12},{9,13},{10,... | collective-permute-start | bytes 417800 | tf_op jit(solution)/shard_map/ppermute | solution.py:184
  101.1 3.6 %collective-permute-start.12 = (bf16[32,2176]{1,0:T(8,128)(2,1)S(1)}, bf16[32,2176]{1,0:T(8,128)(2,1)S(1)}, u32[]{:S(2)}, u32[]{:S(2)}) collective-permute-start(bf16[32,2176]{1,0:T(8,128)(2,1)S(1)} %shard_map.88.refs_7_), channel_id=1, source_target_pairs={{0,3},{1,4},{2,5},{3,6},{4,7},{5,0},{6,1},{7,2},{8,11},{9,12},{10,... | collective-permute-start | bytes 417800 | tf_op jit(solution)/shard_map/ppermute | solution.py:184
  104.7 4.7 %collective-permute-start.11 = (bf16[32,2176]{1,0:T(8,128)(2,1)S(1)}, bf16[32,2176]{1,0:T(8,128)(2,1)S(1)}, u32[]{:S(2)}, u32[]{:S(2)}) collective-permute-start(bf16[32,2176]{1,0:T(8,128)(2,1)S(1)} %shard_map.88.refs_7_), channel_id=1, source_target_pairs={{0,5},{1,6},{2,7},{3,0},{4,1},{5,2},{6,3},{7,4},{8,13},{9,14},{10,... | collective-permute-start | bytes 417800 | tf_op jit(solution)/shard_map/ppermute | solution.py:184
  109.4 3.6 %collective-permute-start.10 = (bf16[32,2176]{1,0:T(8,128)(2,1)S(1)}, bf16[32,2176]{1,0:T(8,128)(2,1)S(1)}, u32[]{:S(2)}, u32[]{:S(2)}) collective-permute-start(bf16[32,2176]{1,0:T(8,128)(2,1)S(1)} %shard_map.88.refs_7_), channel_id=1, source_target_pairs={{0,2},{1,3},{2,4},{3,5},{4,6},{5,7},{6,0},{7,1},{8,10},{9,11},{10,... | collective-permute-start | bytes 417800 | tf_op jit(solution)/shard_map/ppermute | solution.py:184
  113.1 3.8 %collective-permute-start.9 = (bf16[32,2176]{1,0:T(8,128)(2,1)S(1)}, bf16[32,2176]{1,0:T(8,128)(2,1)S(1)}, u32[]{:S(2)}, u32[]{:S(2)}) collective-permute-start(bf16[32,2176]{1,0:T(8,128)(2,1)S(1)} %shard_map.88.refs_7_), channel_id=1, source_target_pairs={{0,6},{1,7},{2,0},{3,1},{4,2},{5,3},{6,4},{7,5},{8,14},{9,15},{10,... | collective-permute-start | bytes 417800 | tf_op jit(solution)/shard_map/ppermute | solution.py:184
  116.8 0.0 collective-permute-done.13.refs_6_
  116.8 1.9 %collective-permute-start.8 = (bf16[32,2176]{1,0:T(8,128)(2,1)S(1)}, bf16[32,2176]{1,0:T(8,128)(2,1)S(1)}, u32[]{:S(2)}, u32[]{:S(2)}) collective-permute-start(bf16[32,2176]{1,0:T(8,128)(2,1)S(1)} %shard_map.88.refs_7_), channel_id=1, source_target_pairs={{0,1},{1,2},{2,3},{3,4},{4,5},{5,6},{6,7},{7,0},{8,9},{9,10},{10,1... | collective-permute-start | bytes 417800 | tf_op jit(solution)/shard_map/ppermute | solution.py:184
  118.8 0.0 collective-permute-done.12.refs_5_
  118.8 4.6 %collective-permute-start.7 = (bf16[32,2176]{1,0:T(8,128)(2,1)S(1)}, bf16[32,2176]{1,0:T(8,128)(2,1)S(1)}, u32[]{:S(2)}, u32[]{:S(2)}) collective-permute-start(bf16[32,2176]{1,0:T(8,128)(2,1)S(1)} %shard_map.88.refs_7_), channel_id=1, source_target_pairs={{0,7},{1,0},{2,1},{3,2},{4,3},{5,4},{6,5},{7,6},{8,15},{9,8},{10,9... | collective-permute-start | bytes 417800 | tf_op jit(solution)/shard_map/ppermute | solution.py:184
  123.3 0.0 collective-permute-done.11.refs_4_
  123.4 0.0 collective-permute-done.10.refs_3_
  123.4 2.7 %collective-permute-done.9.refs_2_ = bf16[32,2176]{1,0:T(8,128)(2,1)S(1)} collective-permute-done((bf16[32,2176]{1,0:T(8,128)(2,1)S(1)}, bf16[32,2176]{1,0:T(8,128)(2,1)S(1)}, u32[]{:S(2)}, u32[]{:S(2)}) %collective-permute-start.9) | collective-permute-done | bytes 139296 | tf_op jit(solution)/shard_map/ppermute | solution.py:184
  126.1 1.9 %collective-permute-done.8.refs_1_ = bf16[32,2176]{1,0:T(8,128)(2,1)S(1)} collective-permute-done((bf16[32,2176]{1,0:T(8,128)(2,1)S(1)}, bf16[32,2176]{1,0:T(8,128)(2,1)S(1)}, u32[]{:S(2)}, u32[]{:S(2)}) %collective-permute-start.8) | collective-permute-done | bytes 139296 | tf_op jit(solution)/shard_map/ppermute | solution.py:184
  128.0 0.7 collective-permute-done.7.refs_0_
  128.7 0.8 shard_map.89
  129.5 0.1 reshape.22
  129.6 22.1 %all_to_all.10 = bf16[128,2,640]{2,1,0:T(2,128)(2,1)S(1)} all-to-all(bf16[128,2,640]{2,1,0:T(2,128)(2,1)S(1)} %reshape.22), channel_id=1, replica_groups=mesh['node'=128,'local'=8] {'node'}, dimensions={0} | all-to-all | bytes 655360 | tf_op jit(solution)/shard_map/all_to_all | solution.py:203
  151.7 0.0 copy-start.4
  151.7 0.0 copy-start.7
  151.7 0.1 reshape.23.rows_back
  151.8 0.6 copy-done.4
  152.4 0.0 copy-done.7
  152.4 1.2 shard_map.90
Async XLA Ops:
  0.6 0.7 copy-start.3
  1.3 0.7 copy-start.5
  2.0 0.7 copy-start.6
  4.2 45.4 %copy-start = (bf16[1,512,1024]{2,1,0:T(8,128)(2,1)S(1)}, bf16[1,512,1024]{2,1,0:T(8,128)(2,1)}, u32[]{:S(2)}) copy-start(bf16[1,512,1024]{2,1,0:T(8,128)(2,1)} %param.11) | copy-start | bytes 3145732
  4.2 45.4 %copy-start.1 = (bf16[1,512,1024]{2,1,0:T(8,128)(2,1)S(1)}, bf16[1,512,1024]{2,1,0:T(8,128)(2,1)}, u32[]{:S(2)}) copy-start(bf16[1,512,1024]{2,1,0:T(8,128)(2,1)} %param.12) | copy-start | bytes 3145732
  4.2 45.2 %all-to-all-start = ((bf16[128,2,1024]{2,1,0:T(2,128)(2,1)}), bf16[128,2,1024]{2,1,0:T(2,128)(2,1)S(1)}, u32[]{:S(2)}, u32[]{:S(2)}) async-start(bf16[128,2,1024]{2,1,0:T(2,128)(2,1)} %reshape.20), calls=%async_computation | async-start | bytes 1048576 | tf_op jit(solution)/shard_map/all_to_all | solution.py:170
  49.6 1.2 copy-start.2
  52.0 23.6 %collective-permute-start = (bf16[32,3072]{1,0:T(8,128)(2,1)S(1)}, bf16[32,3072]{1,0:T(8,128)(2,1)S(1)}, u32[]{:S(2)}, u32[]{:S(2)}) collective-permute-start(bf16[32,3072]{1,0:T(8,128)(2,1)S(1)} %get-tuple-element.13), channel_id=1, source_target_pairs={{0,4},{1,5},{2,6},{3,7},{4,0},{5,1},{6,2},{7,3},{8,12},{9,13},{10,... | collective-permute-start | bytes 589832 | tf_op jit(solution)/shard_map/ppermute | solution.py:184
  59.9 21.5 %collective-permute-start.1 = (bf16[32,3072]{1,0:T(8,128)(2,1)S(1)}, bf16[32,3072]{1,0:T(8,128)(2,1)S(1)}, u32[]{:S(2)}, u32[]{:S(2)}) collective-permute-start(bf16[32,3072]{1,0:T(8,128)(2,1)S(1)} %get-tuple-element.14), channel_id=1, source_target_pairs={{0,3},{1,4},{2,5},{3,6},{4,7},{5,0},{6,1},{7,2},{8,11},{9,12},{10,... | collective-permute-start | bytes 589832 | tf_op jit(solution)/shard_map/ppermute | solution.py:184
  62.8 20.5 %collective-permute-start.2 = (bf16[32,3072]{1,0:T(8,128)(2,1)S(1)}, bf16[32,3072]{1,0:T(8,128)(2,1)S(1)}, u32[]{:S(2)}, u32[]{:S(2)}) collective-permute-start(bf16[32,3072]{1,0:T(8,128)(2,1)S(1)} %get-tuple-element.15), channel_id=1, source_target_pairs={{0,5},{1,6},{2,7},{3,0},{4,1},{5,2},{6,3},{7,4},{8,13},{9,14},{10,... | collective-permute-start | bytes 589832 | tf_op jit(solution)/shard_map/ppermute | solution.py:184
  68.2 21.6 %collective-permute-start.3 = (bf16[32,3072]{1,0:T(8,128)(2,1)S(1)}, bf16[32,3072]{1,0:T(8,128)(2,1)S(1)}, u32[]{:S(2)}, u32[]{:S(2)}) collective-permute-start(bf16[32,3072]{1,0:T(8,128)(2,1)S(1)} %get-tuple-element.16), channel_id=1, source_target_pairs={{0,2},{1,3},{2,4},{3,5},{4,6},{5,7},{6,0},{7,1},{8,10},{9,11},{10,... | collective-permute-start | bytes 589832 | tf_op jit(solution)/shard_map/ppermute | solution.py:184
  70.8 20.3 %collective-permute-start.4 = (bf16[32,3072]{1,0:T(8,128)(2,1)S(1)}, bf16[32,3072]{1,0:T(8,128)(2,1)S(1)}, u32[]{:S(2)}, u32[]{:S(2)}) collective-permute-start(bf16[32,3072]{1,0:T(8,128)(2,1)S(1)} %get-tuple-element.17), channel_id=1, source_target_pairs={{0,6},{1,7},{2,0},{3,1},{4,2},{5,3},{6,4},{7,5},{8,14},{9,15},{10,... | collective-permute-start | bytes 589832 | tf_op jit(solution)/shard_map/ppermute | solution.py:184
  75.6 19.0 %collective-permute-start.5 = (bf16[32,3072]{1,0:T(8,128)(2,1)S(1)}, bf16[32,3072]{1,0:T(8,128)(2,1)S(1)}, u32[]{:S(2)}, u32[]{:S(2)}) collective-permute-start(bf16[32,3072]{1,0:T(8,128)(2,1)S(1)} %get-tuple-element.18), channel_id=1, source_target_pairs={{0,1},{1,2},{2,3},{3,4},{4,5},{5,6},{6,7},{7,0},{8,9},{9,10},{10,1... | collective-permute-start | bytes 589832 | tf_op jit(solution)/shard_map/ppermute | solution.py:184
  81.4 13.9 %collective-permute-start.6 = (bf16[32,3072]{1,0:T(8,128)(2,1)S(1)}, bf16[32,3072]{1,0:T(8,128)(2,1)S(1)}, u32[]{:S(2)}, u32[]{:S(2)}) collective-permute-start(bf16[32,3072]{1,0:T(8,128)(2,1)S(1)} %get-tuple-element.19), channel_id=1, source_target_pairs={{0,7},{1,0},{2,1},{3,2},{4,3},{5,4},{6,5},{7,6},{8,15},{9,8},{10,9... | collective-permute-start | bytes 589832 | tf_op jit(solution)/shard_map/ppermute | solution.py:184
  95.6 21.3 %collective-permute-start.13 = (bf16[32,2176]{1,0:T(8,128)(2,1)S(1)}, bf16[32,2176]{1,0:T(8,128)(2,1)S(1)}, u32[]{:S(2)}, u32[]{:S(2)}) collective-permute-start(bf16[32,2176]{1,0:T(8,128)(2,1)S(1)} %shard_map.88.refs_7_), channel_id=1, source_target_pairs={{0,4},{1,5},{2,6},{3,7},{4,0},{5,1},{6,2},{7,3},{8,12},{9,13},{10,... | collective-permute-start | bytes 417800 | tf_op jit(solution)/shard_map/ppermute | solution.py:184
  101.1 17.7 %collective-permute-start.12 = (bf16[32,2176]{1,0:T(8,128)(2,1)S(1)}, bf16[32,2176]{1,0:T(8,128)(2,1)S(1)}, u32[]{:S(2)}, u32[]{:S(2)}) collective-permute-start(bf16[32,2176]{1,0:T(8,128)(2,1)S(1)} %shard_map.88.refs_7_), channel_id=1, source_target_pairs={{0,3},{1,4},{2,5},{3,6},{4,7},{5,0},{6,1},{7,2},{8,11},{9,12},{10,... | collective-permute-start | bytes 417800 | tf_op jit(solution)/shard_map/ppermute | solution.py:184
  104.7 18.6 %collective-permute-start.11 = (bf16[32,2176]{1,0:T(8,128)(2,1)S(1)}, bf16[32,2176]{1,0:T(8,128)(2,1)S(1)}, u32[]{:S(2)}, u32[]{:S(2)}) collective-permute-start(bf16[32,2176]{1,0:T(8,128)(2,1)S(1)} %shard_map.88.refs_7_), channel_id=1, source_target_pairs={{0,5},{1,6},{2,7},{3,0},{4,1},{5,2},{6,3},{7,4},{8,13},{9,14},{10,... | collective-permute-start | bytes 417800 | tf_op jit(solution)/shard_map/ppermute | solution.py:184
  109.4 14.0 %collective-permute-start.10 = (bf16[32,2176]{1,0:T(8,128)(2,1)S(1)}, bf16[32,2176]{1,0:T(8,128)(2,1)S(1)}, u32[]{:S(2)}, u32[]{:S(2)}) collective-permute-start(bf16[32,2176]{1,0:T(8,128)(2,1)S(1)} %shard_map.88.refs_7_), channel_id=1, source_target_pairs={{0,2},{1,3},{2,4},{3,5},{4,6},{5,7},{6,0},{7,1},{8,10},{9,11},{10,... | collective-permute-start | bytes 417800 | tf_op jit(solution)/shard_map/ppermute | solution.py:184
  113.1 13.0 %collective-permute-start.9 = (bf16[32,2176]{1,0:T(8,128)(2,1)S(1)}, bf16[32,2176]{1,0:T(8,128)(2,1)S(1)}, u32[]{:S(2)}, u32[]{:S(2)}) collective-permute-start(bf16[32,2176]{1,0:T(8,128)(2,1)S(1)} %shard_map.88.refs_7_), channel_id=1, source_target_pairs={{0,6},{1,7},{2,0},{3,1},{4,2},{5,3},{6,4},{7,5},{8,14},{9,15},{10,... | collective-permute-start | bytes 417800 | tf_op jit(solution)/shard_map/ppermute | solution.py:184
  116.8 11.2 %collective-permute-start.8 = (bf16[32,2176]{1,0:T(8,128)(2,1)S(1)}, bf16[32,2176]{1,0:T(8,128)(2,1)S(1)}, u32[]{:S(2)}, u32[]{:S(2)}) collective-permute-start(bf16[32,2176]{1,0:T(8,128)(2,1)S(1)} %shard_map.88.refs_7_), channel_id=1, source_target_pairs={{0,1},{1,2},{2,3},{3,4},{4,5},{5,6},{6,7},{7,0},{8,9},{9,10},{10,1... | collective-permute-start | bytes 417800 | tf_op jit(solution)/shard_map/ppermute | solution.py:184
  118.8 9.9 %collective-permute-start.7 = (bf16[32,2176]{1,0:T(8,128)(2,1)S(1)}, bf16[32,2176]{1,0:T(8,128)(2,1)S(1)}, u32[]{:S(2)}, u32[]{:S(2)}) collective-permute-start(bf16[32,2176]{1,0:T(8,128)(2,1)S(1)} %shard_map.88.refs_7_), channel_id=1, source_target_pairs={{0,7},{1,0},{2,1},{3,2},{4,3},{5,4},{6,5},{7,6},{8,15},{9,8},{10,9... | collective-permute-start | bytes 417800 | tf_op jit(solution)/shard_map/ppermute | solution.py:184
  151.7 0.7 copy-start.4
  151.7 0.7 copy-start.7

commit v3 on v2

--- a/solution.py
+++ b/solution.py
@@ -11,6 +11,7 @@
 F32 = jnp.float32
 VMEM = pl.BlockSpec(memory_space=pltpu.VMEM)
 LIMIT = 40 * 1024 * 1024
+RIGHT, LEFT, FAR, KEPT = (2, 4), 6, 5, (1, 3, 7)
 
 
 def slot_choice(ids, slots, capacity):
@@ -28,22 +29,32 @@
     return jnp.where(rank == (slot % capacity).astype(F32), named, 0.0), expert
 
 
-def send_kernel(capacity, ids, tokens, grad_out, out):
-    slots = out.shape[0]
+def send_kernel(capacity, ids, tokens, grad_out, out, ids_here, tokens_here, grads_here, sems):
+    slots = out.shape[0] * capacity
     cols = tokens.shape[1]
-    chosen, _ = slot_choice(ids[...], slots, capacity)
+    copies = [
+        pltpu.make_async_copy(source, target, sems.at[i])
+        for i, (source, target) in enumerate(
+            [(ids, ids_here), (tokens, tokens_here), (grad_out, grads_here)]
+        )
+    ]
+    for copy in copies:
+        copy.start()
+    copies[0].wait()
+    chosen, _ = slot_choice(ids_here[...], slots, capacity)
     chosen = chosen.astype(BF16)
-    out[:, :cols] = jnp.dot(chosen, tokens[...], preferred_element_type=F32).astype(BF16)
-    out[:, cols:] = jnp.dot(chosen, grad_out[...], preferred_element_type=F32).astype(BF16)
-
-
-def partial_kernel(order, index, rows_in, w_gate, w_up, w_down, *refs):
-    n_local = len(order)
-    outs = refs[:n_local]
-    total = refs[n_local]
-    cols = w_gate.shape[0]
-    hidden = w_gate.shape[1]
-    step = outs[0].shape[0]
+    copies[1].wait()
+    picked = jnp.dot(chosen, tokens_here[...], preferred_element_type=F32).astype(BF16)
+    out[:, :, :cols] = picked.reshape(out.shape[0], capacity, cols)
+    copies[2].wait()
+    picked = jnp.dot(chosen, grads_here[...], preferred_element_type=F32).astype(BF16)
+    out[:, :, cols:] = picked.reshape(out.shape[0], capacity, cols)
+
+
+def partial_kernel(n_local, index, rows_in, w_gate, w_up, w_down, *refs):
+    mine, kept, right, left, far, total = refs
+    cols, hidden = w_gate.shape
+    step = mine.shape[0]
     x = rows_in[:, :cols]
     dy = rows_in[:, cols:]
     total[:, :hidden] = jnp.dot(x, w_gate[...], preferred_element_type=F32)
@@ -52,9 +63,18 @@
         dy, w_down[...], (((1,), (1,)), ((), ())), preferred_element_type=F32
     )
     me = index[0]
-    for d, out in zip(order, outs):
+
+    def chunk(d):
         place = pl.multiple_of(lax.rem(me + d, n_local) * step, step)
-        out[...] = total[pl.ds(place, step), :].astype(out.dtype)
+        return total[pl.ds(place, step), :]
+
+    mine[...] = chunk(0)
+    for i, d in enumerate(KEPT):
+        kept[i * step : (i + 1) * step, :] = chunk(d)
+    for i, d in enumerate(RIGHT):
+        right[i * step : (i + 1) * step, :] = chunk(d).astype(BF16)
+    left[...] = chunk(LEFT).astype(BF16)
+    far[...] = chunk(FAR).astype(BF16)
 
 
 def hidden_kernel(*refs):
@@ -146,34 +166,48 @@
     shape = jax.ShapeDtypeStruct
     index = lax.axis_index("local").astype(jnp.int32).reshape(1)
     smem = pl.BlockSpec(memory_space=pltpu.SMEM)
+    anywhere = pl.BlockSpec(memory_space=pl.ANY)
     order = ring_order(n_local)
     named = expert_ids.T
 
-    def build(kernel, out_shape, in_specs, flops, moved, scratch=()):
+    def build(kernel, out_shape, in_specs, flops, moved, scratch=(), limit=LIMIT):
         return pl.pallas_call(
             kernel,
             out_shape=out_shape,
             in_specs=in_specs,
             out_specs=jax.tree.map(lambda _: VMEM, out_shape),
             scratch_shapes=list(scratch),
-            compiler_params=pltpu.CompilerParams(vmem_limit_bytes=LIMIT),
+            compiler_params=pltpu.CompilerParams(vmem_limit_bytes=limit),
             cost_estimate=pl.CostEstimate(flops=flops, bytes_accessed=moved, transcendentals=0),
         )
 
     outgoing = build(
         functools.partial(send_kernel, capacity),
-        shape((slots, 2 * cols), BF16),
-        [VMEM] * 3,
+        shape((n_node, capacity, 2 * cols), BF16),
+        [anywhere] * 3,
         2 * slots * tok_rows * 2 * cols,
         4 * slots * cols,
+        [
+            pltpu.VMEM((top_count, tok_rows), jnp.int32),
+            pltpu.VMEM((tok_rows, cols), BF16),
+            pltpu.VMEM((tok_rows, cols), BF16),
+            pltpu.SemaphoreType.DMA((3,)),
+        ],
+        limit=63 * 1024 * 1024,
     )(named, tokens, grad_out)
     incoming = lax.all_to_all(
-        outgoing.reshape(n_node, capacity, 2 * cols), "node", split_axis=0, concat_axis=0, tiled=True
+        outgoing, "node", split_axis=0, concat_axis=0, tiled=True
     ).reshape(slots, 2 * cols)
 
-    partials = build(
-        functools.partial(partial_kernel, order),
-        [shape((step, 3 * hidden), BF16) for _ in range(n_local)],
+    mine, kept, right, left, far = build(
+        functools.partial(partial_kernel, n_local),
+        [
+            shape((step, 3 * hidden), F32),
+            shape((len(KEPT) * step, 3 * hidden), F32),
+            shape((len(RIGHT) * step, 3 * hidden), BF16),
+            shape((step, 3 * hidden), BF16),
+            shape((step, 3 * hidden), BF16),
+        ],
         [smem] + [VMEM] * 4,
         6 * slots * cols * hidden,
         2 * (3 * cols * hidden + slots * (2 * cols + 3 * hidden)),
@@ -183,15 +217,25 @@
     def shifted(value, d):
         return lax.ppermute(value, "local", [(k, (k + d) % n_local) for k in range(n_local)])
 
-    arrived = [shifted(part, d) if d else part for d, part in zip(order, partials)]
-    mine = build(
+    def added(sent, place):
+        return (sent.astype(F32) + kept[place * step : (place + 1) * step]).astype(BF16)
+
+    from_right = shifted(left, n_local - 1)
+    from_left = shifted(right, 1)
+    arrived = [
+        shifted(far, FAR),
+        shifted(added(from_right, 2), KEPT[2]),
+        shifted(added(from_left[:step], 0), KEPT[0]),
+        shifted(added(from_left[step:], 1), KEPT[1]),
+    ]
+    hidden_grads = build(
         hidden_kernel,
         shape((step, 2 * hidden + extra), BF16),
-        [VMEM] * n_local,
+        [VMEM] * 5,
         40 * step * hidden,
         2 * step * hidden * (3 * n_local + 2),
-    )(*arrived)
-    gathered = [shifted(mine, d) if d else mine for d in reversed(order)]
+    )(mine, *arrived)
+    gathered = [shifted(hidden_grads, d) if d else hidden_grads for d in reversed(order)]
     sent = build(
         functools.partial(back_kernel, order[::-1]),
         shape((slots, cols + extra), BF16),

time: 154 us -> 147 us (0.955)
  waiting for transfers between devices: 41.2 us -> 35.8 us
  local copies, waits for them, and re-layouts: 5.37 us -> 1.69 us
  Pallas kernels: 3.88 us -> 5.56 us
    ppermute x14 -> x13, waiting for transfers between devices: 20.6 us -> 15.3 us  [shifted(): lax.ppermute(value, 'local', [(k, (k + d) % n_local) for k in range(n_loc...]
    unnamed x16 -> x10, local copies, waits for them, and re-layouts: 3.92 us -> 1.25 us
    pallas_call x3, Pallas kernels: 1.86 us -> 3.55 us  [the longest x1 2.17 us: on_device(): build(functools.partial(send_kernel, capacity), shape((n_node, capacity,...]
    ppermute x14 -> x13, starting transfers between devices: 55.6 us -> 54.8 us  [shifted(): lax.ppermute(value, 'local', [(k, (k + d) % n_local) for k in range(n_loc...]
  transfers between devices with their start and end apart: 15 -> 14, of which waited for: 9 -> 7; matrix products, arithmetic and copies ran while one was open for 0% -> 0% of each run, Pallas kernels for 0% -> 0%
where the time goes in v3:
time: 147 us; the launch traced here: 146 us
  starting transfers between devices  79.4 us (54%)
  waiting for transfers between devices  35.8 us (24%)
  blocking collectives  22.9 us (16%)
  Pallas kernels  5.56 us (4%)
  local copies, waits for them, and re-layouts  1.69 us (1%)
    ppermute x13, starting transfers between devices, shifted(): lax.ppermute(value, 'local', [(k, (k + d) % n_local) for k in range(n_loc...  54.8 us
    all_to_all x1, starting transfers between devices, on_device(): lax.all_to_all(outgoing, 'node', split_axis=0, concat_axis=0, tiled=True)  24.6 us
    all_to_all x1, blocking collectives, on_device(): lax.all_to_all(sent.reshape(n_node, capacity, cols + extra), 'node', spli...  22.9 us
    all_to_all x1, waiting for transfers between devices, on_device(): lax.all_to_all(outgoing, 'node', split_axis=0, concat_axis=0, tiled=True)  20.6 us
    ppermute x13, waiting for transfers between devices, shifted(): lax.ppermute(value, 'local', [(k, (k + d) % n_local) for k in range(n_loc...  15.3 us
  transfers between devices with their start and end apart: 14, of which 7 were waited for; matrix products, arithmetic and copies ran while one was open for 0% of the time, Pallas kernels for 0%

profile of v3, /device:TPU:1, one launch (start us, length us, event | category | flops | bytes accessed | tf_op | source)
XLA Modules:
  0.0 146.4 jit_solution(17530427795565143288)
XLA Ops:
  0.6 2.2 %shard_map.86 = bf16[128,2,1024]{2,1,0:T(2,128)(2,1)} custom-call(s32[8,16]{1,0:T(8,128)} %bitcast.12, bf16[16,512]{1,0:T(8,128)(2,1)} %tokens.1, bf16[16,512]{1,0:T(8,128)(2,1)} %grad_out.1), custom_call_target="tpu_custom_call" | custom-call | flops 8388608 | bytes 524288 | tf_op jit(solution)/shard_map/pallas_call | solution.py:184
  2.8 0.0 copy-start
  2.8 0.0 copy-start.1
  2.8 24.6 %all-to-all-start = ((bf16[128,2,1024]{2,1,0:T(2,128)(2,1)}), bf16[128,2,1024]{2,1,0:T(2,128)(2,1)S(1)}, u32[]{:S(2)}, u32[]{:S(2)}) async-start(bf16[128,2,1024]{2,1,0:T(2,128)(2,1)} %shard_map.86), calls=%async_computation | async-start | bytes 1048576 | tf_op jit(solution)/shard_map/all_to_all | solution.py:198
  27.4 20.6 %all-to-all-done = bf16[128,2,1024]{2,1,0:T(2,128)(2,1)S(1)} async-done(((bf16[128,2,1024]{2,1,0:T(2,128)(2,1)}), bf16[128,2,1024]{2,1,0:T(2,128)(2,1)S(1)}, u32[]{:S(2)}, u32[]{:S(2)}) %all-to-all-start) | async-done | bytes 524320 | tf_op jit(solution)/shard_map/all_to_all | solution.py:198
  48.0 0.2 reshape.17.rows_in
  48.2 0.0 copy-done
  48.2 0.0 copy-done.1
  48.2 0.0 copy-start.2
  48.2 1.2 copy-done.2
  49.4 1.2 shard_map.87
  50.6 3.3 %collective-permute-start.3 = (bf16[64,3072]{1,0:T(8,128)(2,1)S(1)}, bf16[64,3072]{1,0:T(8,128)(2,1)S(1)}, u32[]{:S(2)}, u32[]{:S(2)}) collective-permute-start(bf16[64,3072]{1,0:T(8,128)(2,1)S(1)} %get-tuple-element.13), channel_id=1, source_target_pairs={{0,1},{1,2},{2,3},{3,4},{4,5},{5,6},{6,7},{7,0},{8,9},{9,10},{10,1... | collective-permute-start | bytes 1179656 | tf_op jit(solution)/shard_map/ppermute | solution.py:218
  54.0 4.5 %collective-permute-start.1 = (bf16[32,3072]{1,0:T(8,128)(2,1)S(1)}, bf16[32,3072]{1,0:T(8,128)(2,1)S(1)}, u32[]{:S(2)}, u32[]{:S(2)}) collective-permute-start(bf16[32,3072]{1,0:T(8,128)(2,1)S(1)} %get-tuple-element.11), channel_id=1, source_target_pairs={{0,7},{1,0},{2,1},{3,2},{4,3},{5,4},{6,5},{7,6},{8,15},{9,8},{10,9... | collective-permute-start | bytes 589832 | tf_op jit(solution)/shard_map/ppermute | solution.py:218
  58.5 4.7 %collective-permute-start = (bf16[32,3072]{1,0:T(8,128)(2,1)S(1)}, bf16[32,3072]{1,0:T(8,128)(2,1)S(1)}, u32[]{:S(2)}, u32[]{:S(2)}) collective-permute-start(bf16[32,3072]{1,0:T(8,128)(2,1)S(1)} %get-tuple-element.10), channel_id=1, source_target_pairs={{0,5},{1,6},{2,7},{3,0},{4,1},{5,2},{6,3},{7,4},{8,13},{9,14},{10,... | collective-permute-start | bytes 589832 | tf_op jit(solution)/shard_map/ppermute | solution.py:218
  63.2 0.0 collective-permute-done.1
  63.2 2.5 %collective-permute-done.3 = bf16[64,3072]{1,0:T(8,128)(2,1)S(1)} collective-permute-done((bf16[64,3072]{1,0:T(8,128)(2,1)S(1)}, bf16[64,3072]{1,0:T(8,128)(2,1)S(1)}, u32[]{:S(2)}, u32[]{:S(2)}) %collective-permute-start.3) | collective-permute-done | bytes 393248 | tf_op jit(solution)/shard_map/ppermute | solution.py:218
  65.7 0.1 add_convert_fusion
  65.9 7.0 %collective-permute-start.5 = (bf16[32,3072]{1,0:T(8,128)(2,1)S(1)}, bf16[32,3072]{1,0:T(8,128)(2,1)S(1)}, u32[]{:S(2)}, u32[]{:S(2)}) collective-permute-start(bf16[32,3072]{1,0:T(8,128)(2,1)S(1)} %get-tuple-element.16), channel_id=1, source_target_pairs={{0,3},{1,4},{2,5},{3,6},{4,7},{5,0},{6,1},{7,2},{8,11},{9,12},{10,... | collective-permute-start | bytes 589832 | tf_op jit(solution)/shard_map/ppermute | solution.py:218
  72.9 2.2 %collective-permute-start.4 = (bf16[32,3072]{1,0:T(8,128)(2,1)S(1)}, bf16[32,3072]{1,0:T(8,128)(2,1)S(1)}, u32[]{:S(2)}, u32[]{:S(2)}) collective-permute-start(bf16[32,3072]{1,0:T(8,128)(2,1)S(1)} %get-tuple-element.17), channel_id=1, source_target_pairs={{0,1},{1,2},{2,3},{3,4},{4,5},{5,6},{6,7},{7,0},{8,9},{9,10},{10,1... | collective-permute-start | bytes 589832 | tf_op jit(solution)/shard_map/ppermute | solution.py:218
  75.1 4.3 %collective-permute-start.2 = (bf16[32,3072]{1,0:T(8,128)(2,1)S(1)}, bf16[32,3072]{1,0:T(8,128)(2,1)S(1)}, u32[]{:S(2)}, u32[]{:S(2)}) collective-permute-start(bf16[32,3072]{1,0:T(8,128)(2,1)S(1)} %get-tuple-element.18), channel_id=1, source_target_pairs={{0,7},{1,0},{2,1},{3,2},{4,3},{5,4},{6,5},{7,6},{8,15},{9,8},{10,9... | collective-permute-start | bytes 589832 | tf_op jit(solution)/shard_map/ppermute | solution.py:218
  79.4 0.0 collective-permute-done.refs_1_
  79.4 4.3 %collective-permute-done.5.refs_4_ = bf16[32,3072]{1,0:T(8,128)(2,1)S(1)} collective-permute-done((bf16[32,3072]{1,0:T(8,128)(2,1)S(1)}, bf16[32,3072]{1,0:T(8,128)(2,1)S(1)}, u32[]{:S(2)}, u32[]{:S(2)}) %collective-permute-start.5) | collective-permute-done | bytes 196640 | tf_op jit(solution)/shard_map/ppermute | solution.py:218
  83.7 4.6 %collective-permute-done.4.refs_3_ = bf16[32,3072]{1,0:T(8,128)(2,1)S(1)} collective-permute-done((bf16[32,3072]{1,0:T(8,128)(2,1)S(1)}, bf16[32,3072]{1,0:T(8,128)(2,1)S(1)}, u32[]{:S(2)}, u32[]{:S(2)}) %collective-permute-start.4) | collective-permute-done | bytes 196640 | tf_op jit(solution)/shard_map/ppermute | solution.py:218
  88.4 0.0 collective-permute-done.2.refs_2_
  88.4 0.2 shard_map.88.refs_7_
  88.6 6.6 %collective-permute-start.12 = (bf16[32,2176]{1,0:T(8,128)(2,1)S(1)}, bf16[32,2176]{1,0:T(8,128)(2,1)S(1)}, u32[]{:S(2)}, u32[]{:S(2)}) collective-permute-start(bf16[32,2176]{1,0:T(8,128)(2,1)S(1)} %shard_map.88.refs_7_), channel_id=1, source_target_pairs={{0,4},{1,5},{2,6},{3,7},{4,0},{5,1},{6,2},{7,3},{8,12},{9,13},{10,... | collective-permute-start | bytes 417800 | tf_op jit(solution)/shard_map/ppermute | solution.py:218
  95.2 1.9 %collective-permute-start.11 = (bf16[32,2176]{1,0:T(8,128)(2,1)S(1)}, bf16[32,2176]{1,0:T(8,128)(2,1)S(1)}, u32[]{:S(2)}, u32[]{:S(2)}) collective-permute-start(bf16[32,2176]{1,0:T(8,128)(2,1)S(1)} %shard_map.88.refs_7_), channel_id=1, source_target_pairs={{0,3},{1,4},{2,5},{3,6},{4,7},{5,0},{6,1},{7,2},{8,11},{9,12},{10,... | collective-permute-start | bytes 417800 | tf_op jit(solution)/shard_map/ppermute | solution.py:218
  97.2 6.4 %collective-permute-start.10 = (bf16[32,2176]{1,0:T(8,128)(2,1)S(1)}, bf16[32,2176]{1,0:T(8,128)(2,1)S(1)}, u32[]{:S(2)}, u32[]{:S(2)}) collective-permute-start(bf16[32,2176]{1,0:T(8,128)(2,1)S(1)} %shard_map.88.refs_7_), channel_id=1, source_target_pairs={{0,5},{1,6},{2,7},{3,0},{4,1},{5,2},{6,3},{7,4},{8,13},{9,14},{10,... | collective-permute-start | bytes 417800 | tf_op jit(solution)/shard_map/ppermute | solution.py:218
  103.5 1.9 %collective-permute-start.9 = (bf16[32,2176]{1,0:T(8,128)(2,1)S(1)}, bf16[32,2176]{1,0:T(8,128)(2,1)S(1)}, u32[]{:S(2)}, u32[]{:S(2)}) collective-permute-start(bf16[32,2176]{1,0:T(8,128)(2,1)S(1)} %shard_map.88.refs_7_), channel_id=1, source_target_pairs={{0,2},{1,3},{2,4},{3,5},{4,6},{5,7},{6,0},{7,1},{8,10},{9,11},{10,... | collective-permute-start | bytes 417800 | tf_op jit(solution)/shard_map/ppermute | solution.py:218
  105.5 5.5 %collective-permute-start.8 = (bf16[32,2176]{1,0:T(8,128)(2,1)S(1)}, bf16[32,2176]{1,0:T(8,128)(2,1)S(1)}, u32[]{:S(2)}, u32[]{:S(2)}) collective-permute-start(bf16[32,2176]{1,0:T(8,128)(2,1)S(1)} %shard_map.88.refs_7_), channel_id=1, source_target_pairs={{0,6},{1,7},{2,0},{3,1},{4,2},{5,3},{6,4},{7,5},{8,14},{9,15},{10,... | collective-permute-start | bytes 417800 | tf_op jit(solution)/shard_map/ppermute | solution.py:218
  111.0 0.0 collective-permute-done.12.refs_6_
  111.0 1.9 %collective-permute-start.7 = (bf16[32,2176]{1,0:T(8,128)(2,1)S(1)}, bf16[32,2176]{1,0:T(8,128)(2,1)S(1)}, u32[]{:S(2)}, u32[]{:S(2)}) collective-permute-start(bf16[32,2176]{1,0:T(8,128)(2,1)S(1)} %shard_map.88.refs_7_), channel_id=1, source_target_pairs={{0,1},{1,2},{2,3},{3,4},{4,5},{5,6},{6,7},{7,0},{8,9},{9,10},{10,1... | collective-permute-start | bytes 417800 | tf_op jit(solution)/shard_map/ppermute | solution.py:218
  112.9 0.0 collective-permute-done.11.refs_5_
  112.9 4.6 %collective-permute-start.6 = (bf16[32,2176]{1,0:T(8,128)(2,1)S(1)}, bf16[32,2176]{1,0:T(8,128)(2,1)S(1)}, u32[]{:S(2)}, u32[]{:S(2)}) collective-permute-start(bf16[32,2176]{1,0:T(8,128)(2,1)S(1)} %shard_map.88.refs_7_), channel_id=1, source_target_pairs={{0,7},{1,0},{2,1},{3,2},{4,3},{5,4},{6,5},{7,6},{8,15},{9,8},{10,9... | collective-permute-start | bytes 417800 | tf_op jit(solution)/shard_map/ppermute | solution.py:218
  117.5 0.0 collective-permute-done.10.refs_4_
  117.5 0.0 collective-permute-done.9.refs_3_
  117.5 2.1 %collective-permute-done.8.refs_2_ = bf16[32,2176]{1,0:T(8,128)(2,1)S(1)} collective-permute-done((bf16[32,2176]{1,0:T(8,128)(2,1)S(1)}, bf16[32,2176]{1,0:T(8,128)(2,1)S(1)}, u32[]{:S(2)}, u32[]{:S(2)}) %collective-permute-start.8) | collective-permute-done | bytes 139296 | tf_op jit(solution)/shard_map/ppermute | solution.py:218
  119.6 0.1 collective-permute-done.7.refs_1_
  119.7 1.5 %collective-permute-done.6.refs_0_ = bf16[32,2176]{1,0:T(8,128)(2,1)S(1)} collective-permute-done((bf16[32,2176]{1,0:T(8,128)(2,1)S(1)}, bf16[32,2176]{1,0:T(8,128)(2,1)S(1)}, u32[]{:S(2)}, u32[]{:S(2)}) %collective-permute-start.6) | collective-permute-done | bytes 139296 | tf_op jit(solution)/shard_map/ppermute | solution.py:218
  121.2 0.8 shard_map.89
  122.0 0.0 copy-start.3
  122.0 0.0 copy-start.4
  122.0 0.1 reshape.18
  122.2 22.9 %all_to_all.10 = bf16[128,2,640]{2,1,0:T(2,128)(2,1)S(1)} all-to-all(bf16[128,2,640]{2,1,0:T(2,128)(2,1)S(1)} %reshape.18), channel_id=1, replica_groups=mesh['node'=128,'local'=8] {'node'}, dimensions={0} | all-to-all | bytes 655360 | tf_op jit(solution)/shard_map/all_to_all | solution.py:247
  145.0 0.1 reshape.19.rows_back
  145.2 0.0 copy-done.3
  145.2 0.0 copy-done.4
  145.2 1.2 shard_map.90
Async XLA Ops:
  2.8 45.4 %copy-start = (bf16[1,512,1024]{2,1,0:T(8,128)(2,1)S(1)}, bf16[1,512,1024]{2,1,0:T(8,128)(2,1)}, u32[]{:S(2)}) copy-start(bf16[1,512,1024]{2,1,0:T(8,128)(2,1)} %param.11) | copy-start | bytes 3145732
  2.8 45.4 %copy-start.1 = (bf16[1,512,1024]{2,1,0:T(8,128)(2,1)S(1)}, bf16[1,512,1024]{2,1,0:T(8,128)(2,1)}, u32[]{:S(2)}) copy-start(bf16[1,512,1024]{2,1,0:T(8,128)(2,1)} %param.12) | copy-start | bytes 3145732
  2.8 45.2 %all-to-all-start = ((bf16[128,2,1024]{2,1,0:T(2,128)(2,1)}), bf16[128,2,1024]{2,1,0:T(2,128)(2,1)S(1)}, u32[]{:S(2)}, u32[]{:S(2)}) async-start(bf16[128,2,1024]{2,1,0:T(2,128)(2,1)} %shard_map.86), calls=%async_computation | async-start | bytes 1048576 | tf_op jit(solution)/shard_map/all_to_all | solution.py:198
  48.2 1.2 copy-start.2
  50.6 15.1 %collective-permute-start.3 = (bf16[64,3072]{1,0:T(8,128)(2,1)S(1)}, bf16[64,3072]{1,0:T(8,128)(2,1)S(1)}, u32[]{:S(2)}, u32[]{:S(2)}) collective-permute-start(bf16[64,3072]{1,0:T(8,128)(2,1)S(1)} %get-tuple-element.13), channel_id=1, source_target_pairs={{0,1},{1,2},{2,3},{3,4},{4,5},{5,6},{6,7},{7,0},{8,9},{9,10},{10,1... | collective-permute-start | bytes 1179656 | tf_op jit(solution)/shard_map/ppermute | solution.py:218
  54.0 9.2 %collective-permute-start.1 = (bf16[32,3072]{1,0:T(8,128)(2,1)S(1)}, bf16[32,3072]{1,0:T(8,128)(2,1)S(1)}, u32[]{:S(2)}, u32[]{:S(2)}) collective-permute-start(bf16[32,3072]{1,0:T(8,128)(2,1)S(1)} %get-tuple-element.11), channel_id=1, source_target_pairs={{0,7},{1,0},{2,1},{3,2},{4,3},{5,4},{6,5},{7,6},{8,15},{9,8},{10,9... | collective-permute-start | bytes 589832 | tf_op jit(solution)/shard_map/ppermute | solution.py:218
  58.5 20.9 %collective-permute-start = (bf16[32,3072]{1,0:T(8,128)(2,1)S(1)}, bf16[32,3072]{1,0:T(8,128)(2,1)S(1)}, u32[]{:S(2)}, u32[]{:S(2)}) collective-permute-start(bf16[32,3072]{1,0:T(8,128)(2,1)S(1)} %get-tuple-element.10), channel_id=1, source_target_pairs={{0,5},{1,6},{2,7},{3,0},{4,1},{5,2},{6,3},{7,4},{8,13},{9,14},{10,... | collective-permute-start | bytes 589832 | tf_op jit(solution)/shard_map/ppermute | solution.py:218
  65.9 17.9 %collective-permute-start.5 = (bf16[32,3072]{1,0:T(8,128)(2,1)S(1)}, bf16[32,3072]{1,0:T(8,128)(2,1)S(1)}, u32[]{:S(2)}, u32[]{:S(2)}) collective-permute-start(bf16[32,3072]{1,0:T(8,128)(2,1)S(1)} %get-tuple-element.16), channel_id=1, source_target_pairs={{0,3},{1,4},{2,5},{3,6},{4,7},{5,0},{6,1},{7,2},{8,11},{9,12},{10,... | collective-permute-start | bytes 589832 | tf_op jit(solution)/shard_map/ppermute | solution.py:218
  72.9 15.5 %collective-permute-start.4 = (bf16[32,3072]{1,0:T(8,128)(2,1)S(1)}, bf16[32,3072]{1,0:T(8,128)(2,1)S(1)}, u32[]{:S(2)}, u32[]{:S(2)}) collective-permute-start(bf16[32,3072]{1,0:T(8,128)(2,1)S(1)} %get-tuple-element.17), channel_id=1, source_target_pairs={{0,1},{1,2},{2,3},{3,4},{4,5},{5,6},{6,7},{7,0},{8,9},{9,10},{10,1... | collective-permute-start | bytes 589832 | tf_op jit(solution)/shard_map/ppermute | solution.py:218
  75.1 13.3 %collective-permute-start.2 = (bf16[32,3072]{1,0:T(8,128)(2,1)S(1)}, bf16[32,3072]{1,0:T(8,128)(2,1)S(1)}, u32[]{:S(2)}, u32[]{:S(2)}) collective-permute-start(bf16[32,3072]{1,0:T(8,128)(2,1)S(1)} %get-tuple-element.18), channel_id=1, source_target_pairs={{0,7},{1,0},{2,1},{3,2},{4,3},{5,4},{6,5},{7,6},{8,15},{9,8},{10,9... | collective-permute-start | bytes 589832 | tf_op jit(solution)/shard_map/ppermute | solution.py:218
  88.6 22.4 %collective-permute-start.12 = (bf16[32,2176]{1,0:T(8,128)(2,1)S(1)}, bf16[32,2176]{1,0:T(8,128)(2,1)S(1)}, u32[]{:S(2)}, u32[]{:S(2)}) collective-permute-start(bf16[32,2176]{1,0:T(8,128)(2,1)S(1)} %shard_map.88.refs_7_), channel_id=1, source_target_pairs={{0,4},{1,5},{2,6},{3,7},{4,0},{5,1},{6,2},{7,3},{8,12},{9,13},{10,... | collective-permute-start | bytes 417800 | tf_op jit(solution)/shard_map/ppermute | solution.py:218
  95.2 17.7 %collective-permute-start.11 = (bf16[32,2176]{1,0:T(8,128)(2,1)S(1)}, bf16[32,2176]{1,0:T(8,128)(2,1)S(1)}, u32[]{:S(2)}, u32[]{:S(2)}) collective-permute-start(bf16[32,2176]{1,0:T(8,128)(2,1)S(1)} %shard_map.88.refs_7_), channel_id=1, source_target_pairs={{0,3},{1,4},{2,5},{3,6},{4,7},{5,0},{6,1},{7,2},{8,11},{9,12},{10,... | collective-permute-start | bytes 417800 | tf_op jit(solution)/shard_map/ppermute | solution.py:218
  97.2 20.3 %collective-permute-start.10 = (bf16[32,2176]{1,0:T(8,128)(2,1)S(1)}, bf16[32,2176]{1,0:T(8,128)(2,1)S(1)}, u32[]{:S(2)}, u32[]{:S(2)}) collective-permute-start(bf16[32,2176]{1,0:T(8,128)(2,1)S(1)} %shard_map.88.refs_7_), channel_id=1, source_target_pairs={{0,5},{1,6},{2,7},{3,0},{4,1},{5,2},{6,3},{7,4},{8,13},{9,14},{10,... | collective-permute-start | bytes 417800 | tf_op jit(solution)/shard_map/ppermute | solution.py:218
  103.5 14.0 %collective-permute-start.9 = (bf16[32,2176]{1,0:T(8,128)(2,1)S(1)}, bf16[32,2176]{1,0:T(8,128)(2,1)S(1)}, u32[]{:S(2)}, u32[]{:S(2)}) collective-permute-start(bf16[32,2176]{1,0:T(8,128)(2,1)S(1)} %shard_map.88.refs_7_), channel_id=1, source_target_pairs={{0,2},{1,3},{2,4},{3,5},{4,6},{5,7},{6,0},{7,1},{8,10},{9,11},{10,... | collective-permute-start | bytes 417800 | tf_op jit(solution)/shard_map/ppermute | solution.py:218
  105.5 14.1 %collective-permute-start.8 = (bf16[32,2176]{1,0:T(8,128)(2,1)S(1)}, bf16[32,2176]{1,0:T(8,128)(2,1)S(1)}, u32[]{:S(2)}, u32[]{:S(2)}) collective-permute-start(bf16[32,2176]{1,0:T(8,128)(2,1)S(1)} %shard_map.88.refs_7_), channel_id=1, source_target_pairs={{0,6},{1,7},{2,0},{3,1},{4,2},{5,3},{6,4},{7,5},{8,14},{9,15},{10,... | collective-permute-start | bytes 417800 | tf_op jit(solution)/shard_map/ppermute | solution.py:218
  111.0 8.7 %collective-permute-start.7 = (bf16[32,2176]{1,0:T(8,128)(2,1)S(1)}, bf16[32,2176]{1,0:T(8,128)(2,1)S(1)}, u32[]{:S(2)}, u32[]{:S(2)}) collective-permute-start(bf16[32,2176]{1,0:T(8,128)(2,1)S(1)} %shard_map.88.refs_7_), channel_id=1, source_target_pairs={{0,1},{1,2},{2,3},{3,4},{4,5},{5,6},{6,7},{7,0},{8,9},{9,10},{10,1... | collective-permute-start | bytes 417800 | tf_op jit(solution)/shard_map/ppermute | solution.py:218
  112.9 8.3 %collective-permute-start.6 = (bf16[32,2176]{1,0:T(8,128)(2,1)S(1)}, bf16[32,2176]{1,0:T(8,128)(2,1)S(1)}, u32[]{:S(2)}, u32[]{:S(2)}) collective-permute-start(bf16[32,2176]{1,0:T(8,128)(2,1)S(1)} %shard_map.88.refs_7_), channel_id=1, source_target_pairs={{0,7},{1,0},{2,1},{3,2},{4,3},{5,4},{6,5},{7,6},{8,15},{9,8},{10,9... | collective-permute-start | bytes 417800 | tf_op jit(solution)/shard_map/ppermute | solution.py:218
  122.0 23.2 %copy-start.3 = (s32[16,8]{0,1:T(8,128)S(1)}, s32[16,8]{0,1:T(8,128)}, u32[]{:S(2)}) copy-start(s32[16,8]{0,1:T(8,128)} %param.10) | copy-start | bytes 1540
  122.0 23.2 %copy-start.4 = (f32[16,8]{0,1:T(8,128)S(1)}, f32[16,8]{0,1:T(8,128)}, u32[]{:S(2)}) copy-start(f32[16,8]{0,1:T(8,128)} %param.9) | copy-start | bytes 1540

commit v4 on v3

--- a/solution.py
+++ b/solution.py
@@ -11,7 +11,9 @@
 F32 = jnp.float32
 VMEM = pl.BlockSpec(memory_space=pltpu.VMEM)
 LIMIT = 40 * 1024 * 1024
-RIGHT, LEFT, FAR, KEPT = (2, 4), 6, 5, (1, 3, 7)
+RING = 8
+BY_RIGHT, BY_LEFT, KEPT = (4, 6, 1), (2, 7), (3, 5)
+FROM_HERE, FROM_LEFT, FROM_RIGHT = (0, 5, 3), (7, 4, 2), (1, 6)
 
 
 def slot_choice(ids, slots, capacity):
@@ -52,7 +54,7 @@
 
 
 def partial_kernel(n_local, index, rows_in, w_gate, w_up, w_down, *refs):
-    mine, kept, right, left, far, total = refs
+    mine, kept, right, left, total = refs
     cols, hidden = w_gate.shape
     step = mine.shape[0]
     x = rows_in[:, :cols]
@@ -69,23 +71,20 @@
         return total[pl.ds(place, step), :]
 
     mine[...] = chunk(0)
-    for i, d in enumerate(KEPT):
-        kept[i * step : (i + 1) * step, :] = chunk(d)
-    for i, d in enumerate(RIGHT):
-        right[i * step : (i + 1) * step, :] = chunk(d).astype(BF16)
-    left[...] = chunk(LEFT).astype(BF16)
-    far[...] = chunk(FAR).astype(BF16)
-
-
-def hidden_kernel(*refs):
-    parts, out = refs[:-1], refs[-1]
-    hidden = parts[0].shape[1] // 3
+    for out, distances in ((kept, KEPT), (right, BY_RIGHT), (left, BY_LEFT)):
+        for i, d in enumerate(distances):
+            out[i * step : (i + 1) * step, :] = chunk(d).astype(out.dtype)
+
+
+def hidden_kernel(mine, from_left, from_right, by_three, by_five, out):
+    hidden = mine.shape[1] // 3
+    step = out.shape[0]
 
     def summed(start):
-        value = parts[0][:, start : start + hidden].astype(F32)
-        for part in parts[1:]:
-            value = value + part[:, start : start + hidden].astype(F32)
-        return value
+        at = pl.ds(start, hidden)
+        value = mine[:, at] + from_left[2 * step : 3 * step, at].astype(F32)
+        value = value + from_right[step : 2 * step, at].astype(F32)
+        return value + by_three[:, at].astype(F32) + by_five[:, at].astype(F32)
 
     gate_pre, up_pre, back_pre = summed(0), summed(hidden), summed(2 * hidden)
     sigmoid_gate = jax.nn.sigmoid(gate_pre)
@@ -100,16 +99,21 @@
     out[:, 2 * hidden :] = jnp.broadcast_to(gate_total, (out.shape[0], extra)).astype(BF16)
 
 
-def back_kernel(order, index, *refs):
-    n_local = len(order)
-    parts = refs[:n_local]
-    w_gate, w_up, out, joined = refs[n_local:]
+def back_kernel(n_local, index, here, by_three, by_five, from_left, from_right, w_gate, w_up, out, joined):
     cols, hidden = w_gate.shape
-    step = parts[0].shape[0]
+    step = here.shape[0]
     me = index[0]
-    for d, part in zip(order, parts):
-        place = pl.multiple_of(lax.rem(me + n_local - d, n_local) * step, step)
-        joined[pl.ds(place, step), :] = part[...]
+
+    def place(d, part, i):
+        at = pl.multiple_of(lax.rem(me + d, n_local) * step, step)
+        joined[pl.ds(at, step), :] = part[i * step : (i + 1) * step, :]
+
+    for d, part in zip(FROM_HERE, (here, by_three, by_five)):
+        place(d, part, 0)
+    for i, d in enumerate(FROM_LEFT):
+        place(d, from_left, i)
+    for i, d in enumerate(FROM_RIGHT):
+        place(d, from_right, i)
     across = (((1,), (1,)), ((), ()))
     result = lax.dot_general(joined[:, :hidden], w_gate[...], across, preferred_element_type=F32)
     result = result + lax.dot_general(
@@ -144,13 +148,6 @@
             part, rows_back[:, :cols], across, preferred_element_type=F32
         )
     grad_tokens[...] = total.astype(BF16)
-
-
-def ring_order(n):
-    order = [0] + ([n // 2] if n % 2 == 0 and n > 1 else [])
-    for d in range((n - 1) // 2, 0, -1):
-        order += [d, n - d]
-    return order
 
 
 def on_device(tokens, grad_out, gates, expert_ids, w_gate, w_up, w_down):
@@ -167,7 +164,7 @@
     index = lax.axis_index("local").astype(jnp.int32).reshape(1)
     smem = pl.BlockSpec(memory_space=pltpu.SMEM)
     anywhere = pl.BlockSpec(memory_space=pl.ANY)
-    order = ring_order(n_local)
+    assert n_local == RING
     named = expert_ids.T
 
     def build(kernel, out_shape, in_specs, flops, moved, scratch=(), limit=LIMIT):
@@ -199,14 +196,13 @@
         outgoing, "node", split_axis=0, concat_axis=0, tiled=True
     ).reshape(slots, 2 * cols)
 
-    mine, kept, right, left, far = build(
+    mine, kept, right, left = build(
         functools.partial(partial_kernel, n_local),
         [
             shape((step, 3 * hidden), F32),
             shape((len(KEPT) * step, 3 * hidden), F32),
-            shape((len(RIGHT) * step, 3 * hidden), BF16),
-            shape((step, 3 * hidden), BF16),
-            shape((step, 3 * hidden), BF16),
+            shape((len(BY_RIGHT) * step, 3 * hidden), BF16),
+            shape((len(BY_LEFT) * step, 3 * hidden), BF16),
         ],
         [smem] + [VMEM] * 4,
         6 * slots * cols * hidden,
@@ -217,33 +213,30 @@
     def shifted(value, d):
         return lax.ppermute(value, "local", [(k, (k + d) % n_local) for k in range(n_local)])
 
-    def added(sent, place):
-        return (sent.astype(F32) + kept[place * step : (place + 1) * step]).astype(BF16)
-
+    from_left = shifted(right, 1)
     from_right = shifted(left, n_local - 1)
-    from_left = shifted(right, 1)
-    arrived = [
-        shifted(far, FAR),
-        shifted(added(from_right, 2), KEPT[2]),
-        shifted(added(from_left[:step], 0), KEPT[0]),
-        shifted(added(from_left[step:], 1), KEPT[1]),
-    ]
+    by_five = shifted((kept[step:] + from_left[step : 2 * step].astype(F32)).astype(BF16), 5)
+    by_three = kept[:step] + from_left[:step].astype(F32) + from_right[:step].astype(F32)
+    by_three = shifted(by_three.astype(BF16), 3)
     hidden_grads = build(
         hidden_kernel,
         shape((step, 2 * hidden + extra), BF16),
         [VMEM] * 5,
         40 * step * hidden,
         2 * step * hidden * (3 * n_local + 2),
-    )(mine, *arrived)
-    gathered = [shifted(hidden_grads, d) if d else hidden_grads for d in reversed(order)]
+    )(mine, from_left, from_right, by_three, by_five)
+    by_five = shifted(hidden_grads, 5)
+    by_three = shifted(hidden_grads, 3)
+    from_right = shifted(jnp.concatenate([hidden_grads, by_three], axis=0), n_local - 1)
+    from_left = shifted(jnp.concatenate([hidden_grads, by_three, by_five], axis=0), 1)
     sent = build(
-        functools.partial(back_kernel, order[::-1]),
+        functools.partial(back_kernel, n_local),
         shape((slots, cols + extra), BF16),
-        [smem] + [VMEM] * (n_local + 2),
+        [smem] + [VMEM] * 7,
         4 * slots * cols * hidden,
         2 * (2 * cols * hidden + slots * (2 * hidden + cols)),
         [pltpu.VMEM((slots, 2 * hidden + extra), BF16)],
-    )(index, *gathered, w_gate[0], w_up[0])
+    )(index, hidden_grads, by_three, by_five, from_left, from_right, w_gate[0], w_up[0])
     back = lax.all_to_all(
         sent.reshape(n_node, capacity, cols + extra), "node", split_axis=0, concat_axis=0, tiled=True
     ).reshape(slots, cols + extra)

time: 147 us -> 149 us (1.014)
  starting transfers between devices: 79.4 us -> 53 us
  waiting for transfers between devices: 35.8 us -> 58.5 us
  blocking collectives: 22.9 us -> 28.3 us
    ppermute x13 -> x8, starting transfers between devices: 54.8 us -> 28.5 us  [shifted(): lax.ppermute(value, 'local', [(k, (k + d) % n_local) for k in range(n_loc...]
    ppermute x13 -> x8, waiting for transfers between devices: 15.3 us -> 37.9 us  [shifted(): lax.ppermute(value, 'local', [(k, (k + d) % n_local) for k in range(n_loc...]
    all_to_all x1, blocking collectives: 22.9 us -> 28.3 us  [on_device(): lax.all_to_all(sent.reshape(n_node, capacity, cols + extra), 'node', spli...]
  transfers between devices with their start and end apart: 14 -> 9, of which waited for: 7 -> 8; matrix products, arithmetic and copies ran while one was open for 0% -> 0% of each run, Pallas kernels for 0% -> 0%
where the time goes in v4:
time: 149 us
  waiting for transfers between devices  58.5 us (39%)
  starting transfers between devices  53 us (36%)
  blocking collectives  28.3 us (19%)
  Pallas kernels  5.52 us (4%)
  local copies, waits for them, and re-layouts  2.25 us (2%)
    ppermute x8, waiting for transfers between devices, shifted(): lax.ppermute(value, 'local', [(k, (k + d) % n_local) for k in range(n_loc...  37.9 us
    ppermute x8, starting transfers between devices, shifted(): lax.ppermute(value, 'local', [(k, (k + d) % n_local) for k in range(n_loc...  28.5 us
    all_to_all x1, blocking collectives, on_device(): lax.all_to_all(sent.reshape(n_node, capacity, cols + extra), 'node', spli...  28.3 us
    all_to_all x1, starting transfers between devices, on_device(): lax.all_to_all(outgoing, 'node', split_axis=0, concat_axis=0, tiled=True)  24.6 us
    all_to_all x1, waiting for transfers between devices, on_device(): lax.all_to_all(outgoing, 'node', split_axis=0, concat_axis=0, tiled=True)  20.6 us
  transfers between devices with their start and end apart: 9, of which 8 were waited for; matrix products, arithmetic and copies ran while one was open for 0% of the time, Pallas kernels for 0%

profile of v4, /device:TPU:1, one launch (start us, length us, event | category | flops | bytes accessed | tf_op | source)
XLA Modules:
  0.0 148.5 jit_solution(2302704149566134330)
XLA Ops:
  0.6 2.1 %shard_map.86 = bf16[128,2,1024]{2,1,0:T(2,128)(2,1)} custom-call(s32[8,16]{1,0:T(8,128)} %bitcast.12, bf16[16,512]{1,0:T(8,128)(2,1)} %tokens.1, bf16[16,512]{1,0:T(8,128)(2,1)} %grad_out.1), custom_call_target="tpu_custom_call" | custom-call | flops 8388608 | bytes 524288 | tf_op jit(solution)/shard_map/pallas_call | solution.py:181
  2.8 0.0 copy-start
  2.8 0.0 copy-start.1
  2.8 24.6 %all-to-all-start = ((bf16[128,2,1024]{2,1,0:T(2,128)(2,1)}), bf16[128,2,1024]{2,1,0:T(2,128)(2,1)S(1)}, u32[]{:S(2)}, u32[]{:S(2)}) async-start(bf16[128,2,1024]{2,1,0:T(2,128)(2,1)} %shard_map.86), calls=%async_computation | async-start | bytes 1048576 | tf_op jit(solution)/shard_map/all_to_all | solution.py:195
  27.4 20.6 %all-to-all-done = bf16[128,2,1024]{2,1,0:T(2,128)(2,1)S(1)} async-done(((bf16[128,2,1024]{2,1,0:T(2,128)(2,1)}), bf16[128,2,1024]{2,1,0:T(2,128)(2,1)S(1)}, u32[]{:S(2)}, u32[]{:S(2)}) %all-to-all-start) | async-done | bytes 524320 | tf_op jit(solution)/shard_map/all_to_all | solution.py:195
  48.0 0.2 reshape.17.rows_in
  48.2 0.0 copy-done
  48.2 0.0 copy-done.1
  48.2 0.0 copy-start.2
  48.2 1.2 copy-done.2
  49.4 1.2 shard_map.87
  50.6 3.3 %collective-permute-start = (bf16[96,3072]{1,0:T(8,128)(2,1)S(1)}, bf16[96,3072]{1,0:T(8,128)(2,1)S(1)}, u32[]{:S(2)}, u32[]{:S(2)}) collective-permute-start(bf16[96,3072]{1,0:T(8,128)(2,1)S(1)} %get-tuple-element.9), channel_id=1, source_target_pairs={{0,1},{1,2},{2,3},{3,4},{4,5},{5,6},{6,7},{7,0},{8,9},{9,10},{10,1... | collective-permute-start | bytes 1769480 | tf_op jit(solution)/shard_map/ppermute | solution.py:214
  53.9 4.5 %collective-permute-start.1 = (bf16[64,3072]{1,0:T(8,128)(2,1)S(1)}, bf16[64,3072]{1,0:T(8,128)(2,1)S(1)}, u32[]{:S(2)}, u32[]{:S(2)}) collective-permute-start(bf16[64,3072]{1,0:T(8,128)(2,1)S(1)} %get-tuple-element.10), channel_id=1, source_target_pairs={{0,7},{1,0},{2,1},{3,2},{4,3},{5,4},{6,5},{7,6},{8,15},{9,8},{10,9... | collective-permute-start | bytes 1179656 | tf_op jit(solution)/shard_map/ppermute | solution.py:214
  58.4 8.9 %collective-permute-done.1.from_right = bf16[64,3072]{1,0:T(8,128)(2,1)S(1)} collective-permute-done((bf16[64,3072]{1,0:T(8,128)(2,1)S(1)}, bf16[64,3072]{1,0:T(8,128)(2,1)S(1)}, u32[]{:S(2)}, u32[]{:S(2)}) %collective-permute-start.1) | collective-permute-done | bytes 393248 | tf_op jit(solution)/shard_map/ppermute | solution.py:214
  67.3 2.6 %collective-permute-done.from_left = bf16[96,3072]{1,0:T(8,128)(2,1)S(1)} collective-permute-done((bf16[96,3072]{1,0:T(8,128)(2,1)S(1)}, bf16[96,3072]{1,0:T(8,128)(2,1)S(1)}, u32[]{:S(2)}, u32[]{:S(2)}) %collective-permute-start) | collective-permute-done | bytes 589856 | tf_op jit(solution)/shard_map/ppermute | solution.py:214
  69.9 0.1 add_convert_fusion
  70.0 5.1 %collective-permute-start.3 = (bf16[32,3072]{1,0:T(8,128)(2,1)S(1)}, bf16[32,3072]{1,0:T(8,128)(2,1)S(1)}, u32[]{:S(2)}, u32[]{:S(2)}) collective-permute-start(bf16[32,3072]{1,0:T(8,128)(2,1)S(1)} %get-tuple-element.14), channel_id=1, source_target_pairs={{0,5},{1,6},{2,7},{3,0},{4,1},{5,2},{6,3},{7,4},{8,13},{9,14},{10,... | collective-permute-start | bytes 589832 | tf_op jit(solution)/shard_map/ppermute | solution.py:214
  75.1 2.0 %collective-permute-start.2 = (bf16[32,3072]{1,0:T(8,128)(2,1)S(1)}, bf16[32,3072]{1,0:T(8,128)(2,1)S(1)}, u32[]{:S(2)}, u32[]{:S(2)}) collective-permute-start(bf16[32,3072]{1,0:T(8,128)(2,1)S(1)} %get-tuple-element.15), channel_id=1, source_target_pairs={{0,3},{1,4},{2,5},{3,6},{4,7},{5,0},{6,1},{7,2},{8,11},{9,12},{10,... | collective-permute-start | bytes 589832 | tf_op jit(solution)/shard_map/ppermute | solution.py:214
  77.1 11.2 %collective-permute-done.3.by_five = bf16[32,3072]{1,0:T(8,128)(2,1)S(1)} collective-permute-done((bf16[32,3072]{1,0:T(8,128)(2,1)S(1)}, bf16[32,3072]{1,0:T(8,128)(2,1)S(1)}, u32[]{:S(2)}, u32[]{:S(2)}) %collective-permute-start.3) | collective-permute-done | bytes 196640 | tf_op jit(solution)/shard_map/ppermute | solution.py:214
  88.2 5.7 %collective-permute-done.2.by_three = bf16[32,3072]{1,0:T(8,128)(2,1)S(1)} collective-permute-done((bf16[32,3072]{1,0:T(8,128)(2,1)S(1)}, bf16[32,3072]{1,0:T(8,128)(2,1)S(1)}, u32[]{:S(2)}, u32[]{:S(2)}) %collective-permute-start.2) | collective-permute-done | bytes 196640 | tf_op jit(solution)/shard_map/ppermute | solution.py:214
  94.0 0.2 shard_map.88.here
  94.2 3.8 %collective-permute-start.5 = (bf16[32,2176]{1,0:T(8,128)(2,1)S(1)}, bf16[32,2176]{1,0:T(8,128)(2,1)S(1)}, u32[]{:S(2)}, u32[]{:S(2)}) collective-permute-start(bf16[32,2176]{1,0:T(8,128)(2,1)S(1)} %shard_map.88.here), channel_id=1, source_target_pairs={{0,5},{1,6},{2,7},{3,0},{4,1},{5,2},{6,3},{7,4},{8,13},{9,14},{10,... | collective-permute-start | bytes 417800 | tf_op jit(solution)/shard_map/ppermute | solution.py:214
  98.0 3.2 %collective-permute-start.4 = (bf16[32,2176]{1,0:T(8,128)(2,1)S(1)}, bf16[32,2176]{1,0:T(8,128)(2,1)S(1)}, u32[]{:S(2)}, u32[]{:S(2)}) collective-permute-start(bf16[32,2176]{1,0:T(8,128)(2,1)S(1)} %shard_map.88.here), channel_id=1, source_target_pairs={{0,3},{1,4},{2,5},{3,6},{4,7},{5,0},{6,1},{7,2},{8,11},{9,12},{10,... | collective-permute-start | bytes 417800 | tf_op jit(solution)/shard_map/ppermute | solution.py:214
  101.3 2.6 %collective-permute-done.5.by_five = bf16[32,2176]{1,0:T(8,128)(2,1)S(1)} collective-permute-done((bf16[32,2176]{1,0:T(8,128)(2,1)S(1)}, bf16[32,2176]{1,0:T(8,128)(2,1)S(1)}, u32[]{:S(2)}, u32[]{:S(2)}) %collective-permute-start.5) | collective-permute-done | bytes 139296 | tf_op jit(solution)/shard_map/ppermute | solution.py:214
  103.9 3.5 %collective-permute-done.4.by_three = bf16[32,2176]{1,0:T(8,128)(2,1)S(1)} collective-permute-done((bf16[32,2176]{1,0:T(8,128)(2,1)S(1)}, bf16[32,2176]{1,0:T(8,128)(2,1)S(1)}, u32[]{:S(2)}, u32[]{:S(2)}) %collective-permute-start.4) | collective-permute-done | bytes 139296 | tf_op jit(solution)/shard_map/ppermute | solution.py:214
  107.4 1.9 %collective-permute-start.6 = (bf16[96,2176]{1,0:T(8,128)(2,1)S(1)}, bf16[96,2176]{1,0:T(8,128)(2,1)S(1)}, u32[]{:S(2)}, u32[]{:S(2)}) collective-permute-start(bf16[96,2176]{1,0:T(8,128)(2,1)S(1)} %pad_maximum_fusion), channel_id=1, source_target_pairs={{0,1},{1,2},{2,3},{3,4},{4,5},{5,6},{6,7},{7,0},{8,9},{9,10},{10,1... | collective-permute-start | bytes 1253384 | tf_op jit(solution)/shard_map/ppermute | solution.py:214
  109.3 4.6 %collective-permute-start.7 = (bf16[64,2176]{1,0:T(8,128)(2,1)S(1)}, bf16[64,2176]{1,0:T(8,128)(2,1)S(1)}, u32[]{:S(2)}, u32[]{:S(2)}) collective-permute-start(bf16[64,2176]{1,0:T(8,128)(2,1)S(1)} %pad_maximum_fusion.1), channel_id=1, source_target_pairs={{0,7},{1,0},{2,1},{3,2},{4,3},{5,4},{6,5},{7,6},{8,15},{9,8},{10,9... | collective-permute-start | bytes 835592 | tf_op jit(solution)/shard_map/ppermute | solution.py:214
  113.9 3.5 %collective-permute-done.7.from_right = bf16[64,2176]{1,0:T(8,128)(2,1)S(1)} collective-permute-done((bf16[64,2176]{1,0:T(8,128)(2,1)S(1)}, bf16[64,2176]{1,0:T(8,128)(2,1)S(1)}, u32[]{:S(2)}, u32[]{:S(2)}) %collective-permute-start.7) | collective-permute-done | bytes 278560 | tf_op jit(solution)/shard_map/ppermute | solution.py:214
  117.4 0.0 collective-permute-done.6.from_left
  117.4 0.8 shard_map.89
  118.1 0.1 reshape.18
  118.3 28.3 %all_to_all.10 = bf16[128,2,640]{2,1,0:T(2,128)(2,1)S(1)} all-to-all(bf16[128,2,640]{2,1,0:T(2,128)(2,1)S(1)} %reshape.18), channel_id=1, replica_groups=mesh['node'=128,'local'=8] {'node'}, dimensions={0} | all-to-all | bytes 655360 | tf_op jit(solution)/shard_map/all_to_all | solution.py:240
  146.6 0.0 copy-start.3
  146.6 0.0 copy-start.4
  146.6 0.1 reshape.19.rows_back
  146.7 0.6 copy-done.3
  147.3 0.0 copy-done.4
  147.3 1.2 shard_map.90
  (2 shorter events, 0.1 us)
Async XLA Ops:
  2.8 45.4 %copy-start = (bf16[1,512,1024]{2,1,0:T(8,128)(2,1)S(1)}, bf16[1,512,1024]{2,1,0:T(8,128)(2,1)}, u32[]{:S(2)}) copy-start(bf16[1,512,1024]{2,1,0:T(8,128)(2,1)} %param.11) | copy-start | bytes 3145732
  2.8 45.4 %copy-start.1 = (bf16[1,512,1024]{2,1,0:T(8,128)(2,1)S(1)}, bf16[1,512,1024]{2,1,0:T(8,128)(2,1)}, u32[]{:S(2)}) copy-start(bf16[1,512,1024]{2,1,0:T(8,128)(2,1)} %param.12) | copy-start | bytes 3145732
  2.8 45.2 %all-to-all-start = ((bf16[128,2,1024]{2,1,0:T(2,128)(2,1)}), bf16[128,2,1024]{2,1,0:T(2,128)(2,1)S(1)}, u32[]{:S(2)}, u32[]{:S(2)}) async-start(bf16[128,2,1024]{2,1,0:T(2,128)(2,1)} %shard_map.86), calls=%async_computation | async-start | bytes 1048576 | tf_op jit(solution)/shard_map/all_to_all | solution.py:195
  48.2 1.2 copy-start.2
  50.6 19.3 %collective-permute-start = (bf16[96,3072]{1,0:T(8,128)(2,1)S(1)}, bf16[96,3072]{1,0:T(8,128)(2,1)S(1)}, u32[]{:S(2)}, u32[]{:S(2)}) collective-permute-start(bf16[96,3072]{1,0:T(8,128)(2,1)S(1)} %get-tuple-element.9), channel_id=1, source_target_pairs={{0,1},{1,2},{2,3},{3,4},{4,5},{5,6},{6,7},{7,0},{8,9},{9,10},{10,1... | collective-permute-start | bytes 1769480 | tf_op jit(solution)/shard_map/ppermute | solution.py:214
  53.9 13.4 %collective-permute-start.1 = (bf16[64,3072]{1,0:T(8,128)(2,1)S(1)}, bf16[64,3072]{1,0:T(8,128)(2,1)S(1)}, u32[]{:S(2)}, u32[]{:S(2)}) collective-permute-start(bf16[64,3072]{1,0:T(8,128)(2,1)S(1)} %get-tuple-element.10), channel_id=1, source_target_pairs={{0,7},{1,0},{2,1},{3,2},{4,3},{5,4},{6,5},{7,6},{8,15},{9,8},{10,9... | collective-permute-start | bytes 1179656 | tf_op jit(solution)/shard_map/ppermute | solution.py:214
  70.0 18.2 %collective-permute-start.3 = (bf16[32,3072]{1,0:T(8,128)(2,1)S(1)}, bf16[32,3072]{1,0:T(8,128)(2,1)S(1)}, u32[]{:S(2)}, u32[]{:S(2)}) collective-permute-start(bf16[32,3072]{1,0:T(8,128)(2,1)S(1)} %get-tuple-element.14), channel_id=1, source_target_pairs={{0,5},{1,6},{2,7},{3,0},{4,1},{5,2},{6,3},{7,4},{8,13},{9,14},{10,... | collective-permute-start | bytes 589832 | tf_op jit(solution)/shard_map/ppermute | solution.py:214
  75.1 18.9 %collective-permute-start.2 = (bf16[32,3072]{1,0:T(8,128)(2,1)S(1)}, bf16[32,3072]{1,0:T(8,128)(2,1)S(1)}, u32[]{:S(2)}, u32[]{:S(2)}) collective-permute-start(bf16[32,3072]{1,0:T(8,128)(2,1)S(1)} %get-tuple-element.15), channel_id=1, source_target_pairs={{0,3},{1,4},{2,5},{3,6},{4,7},{5,0},{6,1},{7,2},{8,11},{9,12},{10,... | collective-permute-start | bytes 589832 | tf_op jit(solution)/shard_map/ppermute | solution.py:214
  94.2 9.6 %collective-permute-start.5 = (bf16[32,2176]{1,0:T(8,128)(2,1)S(1)}, bf16[32,2176]{1,0:T(8,128)(2,1)S(1)}, u32[]{:S(2)}, u32[]{:S(2)}) collective-permute-start(bf16[32,2176]{1,0:T(8,128)(2,1)S(1)} %shard_map.88.here), channel_id=1, source_target_pairs={{0,5},{1,6},{2,7},{3,0},{4,1},{5,2},{6,3},{7,4},{8,13},{9,14},{10,... | collective-permute-start | bytes 417800 | tf_op jit(solution)/shard_map/ppermute | solution.py:214
  98.0 9.3 %collective-permute-start.4 = (bf16[32,2176]{1,0:T(8,128)(2,1)S(1)}, bf16[32,2176]{1,0:T(8,128)(2,1)S(1)}, u32[]{:S(2)}, u32[]{:S(2)}) collective-permute-start(bf16[32,2176]{1,0:T(8,128)(2,1)S(1)} %shard_map.88.here), channel_id=1, source_target_pairs={{0,3},{1,4},{2,5},{3,6},{4,7},{5,0},{6,1},{7,2},{8,11},{9,12},{10,... | collective-permute-start | bytes 417800 | tf_op jit(solution)/shard_map/ppermute | solution.py:214
  107.4 10.0 %collective-permute-start.6 = (bf16[96,2176]{1,0:T(8,128)(2,1)S(1)}, bf16[96,2176]{1,0:T(8,128)(2,1)S(1)}, u32[]{:S(2)}, u32[]{:S(2)}) collective-permute-start(bf16[96,2176]{1,0:T(8,128)(2,1)S(1)} %pad_maximum_fusion), channel_id=1, source_target_pairs={{0,1},{1,2},{2,3},{3,4},{4,5},{5,6},{6,7},{7,0},{8,9},{9,10},{10,1... | collective-permute-start | bytes 1253384 | tf_op jit(solution)/shard_map/ppermute | solution.py:214
  109.3 8.1 %collective-permute-start.7 = (bf16[64,2176]{1,0:T(8,128)(2,1)S(1)}, bf16[64,2176]{1,0:T(8,128)(2,1)S(1)}, u32[]{:S(2)}, u32[]{:S(2)}) collective-permute-start(bf16[64,2176]{1,0:T(8,128)(2,1)S(1)} %pad_maximum_fusion.1), channel_id=1, source_target_pairs={{0,7},{1,0},{2,1},{3,2},{4,3},{5,4},{6,5},{7,6},{8,15},{9,8},{10,9... | collective-permute-start | bytes 835592 | tf_op jit(solution)/shard_map/ppermute | solution.py:214
  146.6 0.7 copy-start.3
  146.6 0.7 copy-start.4

commit v5 on v3

--- a/solution.py
+++ b/solution.py
@@ -91,25 +91,21 @@
     sigmoid_gate = jax.nn.sigmoid(gate_pre)
     act = gate_pre * sigmoid_gate
     grad_up = back_pre * act
-    out[:, :hidden] = (
+    grad_gate = (
         back_pre * up_pre * sigmoid_gate * (1.0 + gate_pre * (1.0 - sigmoid_gate))
     ).astype(BF16)
-    out[:, hidden : 2 * hidden] = grad_up.astype(BF16)
+    grad_up_sent = grad_up.astype(BF16)
     gate_total = jnp.sum(grad_up * up_pre, axis=1, keepdims=True)
-    extra = out.shape[1] - 2 * hidden
-    out[:, 2 * hidden :] = jnp.broadcast_to(gate_total, (out.shape[0], extra)).astype(BF16)
-
-
-def back_kernel(order, index, *refs):
-    n_local = len(order)
-    parts = refs[:n_local]
-    w_gate, w_up, out, joined = refs[n_local:]
+    copies, step, width = out.shape
+    gate_total = jnp.broadcast_to(gate_total, (step, width - 2 * hidden)).astype(BF16)
+    for i in range(copies):
+        out[i, :, :hidden] = grad_gate
+        out[i, :, hidden : 2 * hidden] = grad_up_sent
+        out[i, :, 2 * hidden :] = gate_total
+
+
+def back_kernel(joined, w_gate, w_up, out):
     cols, hidden = w_gate.shape
-    step = parts[0].shape[0]
-    me = index[0]
-    for d, part in zip(order, parts):
-        place = pl.multiple_of(lax.rem(me + n_local - d, n_local) * step, step)
-        joined[pl.ds(place, step), :] = part[...]
     across = (((1,), (1,)), ((), ()))
     result = lax.dot_general(joined[:, :hidden], w_gate[...], across, preferred_element_type=F32)
     result = result + lax.dot_general(
@@ -119,38 +115,33 @@
     out[:, cols:] = joined[:, 2 * hidden :]
 
 
-def combine_kernel(capacity, ids, gates, rows_back, grad_tokens, grad_gates):
-    slots = rows_back.shape[0]
-    rows, cols = grad_tokens.shape
-    top_count = gates.shape[0]
+def weight_kernel(capacity, ids, gates, weights, places):
+    slots = weights.shape[0]
+    top_count, rows = gates.shape
     named = ids[...]
     chosen, expert = slot_choice(named, slots, capacity)
     weight = jnp.zeros((slots, rows), F32)
-    across = (((0,), (0,)), ((), ()))
     for k in range(top_count):
         here = jnp.where(named[k : k + 1, :] == expert, chosen, 0.0)
         weight = weight + here * gates[k : k + 1, :]
-        value = lax.dot_general(
-            rows_back[:, cols:], here.astype(BF16), across, preferred_element_type=F32
-        )
-        grad_gates[k : k + 1, :] = value[:1, :].astype(BF16)
+        places[:, k * rows : (k + 1) * rows] = here.astype(BF16)
     high = weight.astype(BF16)
     rest = weight - high.astype(F32)
     middle = rest.astype(BF16)
     low = (rest - middle.astype(F32)).astype(BF16)
-    total = jnp.zeros((rows, cols), F32)
-    for part in (low, middle, high):
-        total = total + lax.dot_general(
-            part, rows_back[:, :cols], across, preferred_element_type=F32
-        )
+    for i, part in enumerate((low, middle, high)):
+        weights[:, i * rows : (i + 1) * rows] = part
+
+
+def combine_kernel(weights, places, rows_back, grad_tokens, grad_gates):
+    rows, cols = grad_tokens.shape
+    across = (((0,), (0,)), ((), ()))
+    values = lax.dot_general(rows_back[:, cols:], places[...], across, preferred_element_type=F32)
+    for k in range(grad_gates.shape[0]):
+        grad_gates[k : k + 1, :] = values[:1, k * rows : (k + 1) * rows].astype(BF16)
+    parts = lax.dot_general(weights[...], rows_back[:, :cols], across, preferred_element_type=F32)
+    total = parts[:rows] + parts[rows : 2 * rows] + parts[2 * rows :]
     grad_tokens[...] = total.astype(BF16)
-
-
-def ring_order(n):
-    order = [0] + ([n // 2] if n % 2 == 0 and n > 1 else [])
-    for d in range((n - 1) // 2, 0, -1):
-        order += [d, n - d]
-    return order
 
 
 def on_device(tokens, grad_out, gates, expert_ids, w_gate, w_up, w_down):
@@ -167,7 +158,7 @@
     index = lax.axis_index("local").astype(jnp.int32).reshape(1)
     smem = pl.BlockSpec(memory_space=pltpu.SMEM)
     anywhere = pl.BlockSpec(memory_space=pl.ANY)
-    order = ring_order(n_local)
+    assert n_local == 8
     named = expert_ids.T
 
     def build(kernel, out_shape, in_specs, flops, moved, scratch=(), limit=LIMIT):
@@ -195,6 +186,13 @@
         ],
         limit=63 * 1024 * 1024,
     )(named, tokens, grad_out)
+    weights, places = build(
+        functools.partial(weight_kernel, capacity),
+        [shape((slots, 3 * tok_rows), BF16), shape((slots, top_count * tok_rows), BF16)],
+        [VMEM] * 2,
+        100 * slots * tok_rows * top_count,
+        2 * slots * tok_rows * (top_count + 3),
+    )(named, gates.T)
     incoming = lax.all_to_all(
         outgoing, "node", split_axis=0, concat_axis=0, tiled=True
     ).reshape(slots, 2 * cols)
@@ -224,36 +222,35 @@
     from_left = shifted(right, 1)
     arrived = [
         shifted(far, FAR),
+        shifted(added(from_left[step:], 1), KEPT[1]),
+        shifted(added(from_left[:step], 0), KEPT[0]),
         shifted(added(from_right, 2), KEPT[2]),
-        shifted(added(from_left[:step], 0), KEPT[0]),
-        shifted(added(from_left[step:], 1), KEPT[1]),
     ]
-    hidden_grads = build(
+    copies = build(
         hidden_kernel,
-        shape((step, 2 * hidden + extra), BF16),
+        shape((n_local, step, 2 * hidden + extra), BF16),
         [VMEM] * 5,
         40 * step * hidden,
-        2 * step * hidden * (3 * n_local + 2),
+        2 * step * hidden * (3 * n_local + 2 * n_local),
     )(mine, *arrived)
-    gathered = [shifted(hidden_grads, d) if d else hidden_grads for d in reversed(order)]
+    gathered = lax.all_to_all(copies, "local", split_axis=0, concat_axis=0, tiled=True)
     sent = build(
-        functools.partial(back_kernel, order[::-1]),
+        back_kernel,
         shape((slots, cols + extra), BF16),
-        [smem] + [VMEM] * (n_local + 2),
+        [VMEM] * 3,
         4 * slots * cols * hidden,
         2 * (2 * cols * hidden + slots * (2 * hidden + cols)),
-        [pltpu.VMEM((slots, 2 * hidden + extra), BF16)],
-    )(index, *gathered, w_gate[0], w_up[0])
+    )(gathered.reshape(slots, 2 * hidden + extra), w_gate[0], w_up[0])
     back = lax.all_to_all(
         sent.reshape(n_node, capacity, cols + extra), "node", split_axis=0, concat_axis=0, tiled=True
     ).reshape(slots, cols + extra)
     grad_tokens, grad_gates = build(
-        functools.partial(combine_kernel, capacity),
+        combine_kernel,
         [shape((tok_rows, cols), BF16), shape((top_count, tok_rows), BF16)],
         [VMEM] * 3,
         8 * tok_rows * slots * cols,
         2 * slots * cols,
-    )(named, gates.T, back)
+    )(weights, places, back)
     return grad_tokens, grad_gates.T
 
 

time: 147 us -> 150 us (1.020)
  starting transfers between devices: 79.4 us -> 58.1 us
  waiting for transfers between devices: 35.8 us -> 48.2 us
  blocking collectives: 22.9 us -> 34.6 us
    ppermute x13 -> x6, starting transfers between devices: 54.8 us -> 26 us  [shifted(): lax.ppermute(value, 'local', [(k, (k + d) % n_local) for k in range(n_loc...]
    all_to_all x0 -> x1, waiting for transfers between devices: none -> 16.1 us  [on_device(): lax.all_to_all(sent.reshape(n_node, capacity, cols + extra), 'node', spli...]
    all_to_all x1, blocking collectives: 22.9 us -> 34.6 us  [on_device(): lax.all_to_all(copies, 'local', split_axis=0, concat_axis=0, tiled=True)]
    all_to_all x0 -> x1, starting transfers between devices: none -> 7.47 us  [on_device(): lax.all_to_all(sent.reshape(n_node, capacity, cols + extra), 'node', spli...]
    ppermute x13 -> x6, waiting for transfers between devices: 15.3 us -> 11.5 us  [shifted(): lax.ppermute(value, 'local', [(k, (k + d) % n_local) for k in range(n_loc...]
  transfers between devices with their start and end apart: 14 -> 8, of which waited for: 7 -> 5; matrix products, arithmetic and copies ran while one was open for 0% -> 0% of each run, Pallas kernels for 0% -> 0%
where the time goes in v5:
time: 150 us
  starting transfers between devices  58.1 us (39%)
  waiting for transfers between devices  48.2 us (32%)
  blocking collectives  34.6 us (23%)
  Pallas kernels  5.68 us (4%)
  local copies, waits for them, and re-layouts  2.42 us (2%)
    all_to_all x1, blocking collectives, on_device(): lax.all_to_all(copies, 'local', split_axis=0, concat_axis=0, tiled=True)  34.6 us
    ppermute x6, starting transfers between devices, shifted(): lax.ppermute(value, 'local', [(k, (k + d) % n_local) for k in range(n_loc...  26 us
    all_to_all x1, starting transfers between devices, on_device(): lax.all_to_all(outgoing, 'node', split_axis=0, concat_axis=0, tiled=True)  24.6 us
    all_to_all x1, waiting for transfers between devices, on_device(): lax.all_to_all(outgoing, 'node', split_axis=0, concat_axis=0, tiled=True)  20.6 us
    all_to_all x1, waiting for transfers between devices, on_device(): lax.all_to_all(sent.reshape(n_node, capacity, cols + extra), 'node', spli...  16.1 us
    ppermute x6, waiting for transfers between devices, shifted(): lax.ppermute(value, 'local', [(k, (k + d) % n_local) for k in range(n_loc...  11.5 us
    all_to_all x1, starting transfers between devices, on_device(): lax.all_to_all(sent.reshape(n_node, capacity, cols + extra), 'node', spli...  7.47 us
  transfers between devices with their start and end apart: 8, of which 5 were waited for; matrix products, arithmetic and copies ran while one was open for 0% of the time, Pallas kernels for 0%

profile of v5, /device:TPU:1, one launch (start us, length us, event | category | flops | bytes accessed | tf_op | source)
XLA Modules:
  0.0 149.9 jit_solution(1699634818375346526)
XLA Ops:
  0.6 2.2 %shard_map.87 = bf16[128,2,1024]{2,1,0:T(2,128)(2,1)} custom-call(s32[8,16]{1,0:T(8,128)} %bitcast.14, bf16[16,512]{1,0:T(8,128)(2,1)} %tokens.1, bf16[16,512]{1,0:T(8,128)(2,1)} %grad_out.1), custom_call_target="tpu_custom_call" | custom-call | flops 8388608 | bytes 524288 | tf_op jit(solution)/shard_map/pallas_call | solution.py:175
  2.8 0.0 copy-start
  2.8 0.0 copy-start.1
  2.8 24.6 %all-to-all-start = ((bf16[128,2,1024]{2,1,0:T(2,128)(2,1)}), bf16[128,2,1024]{2,1,0:T(2,128)(2,1)S(1)}, u32[]{:S(2)}, u32[]{:S(2)}) async-start(bf16[128,2,1024]{2,1,0:T(2,128)(2,1)} %shard_map.87), calls=%async_computation | async-start | bytes 1048576 | tf_op jit(solution)/shard_map/all_to_all | solution.py:196
  27.4 20.6 %all-to-all-done = bf16[128,2,1024]{2,1,0:T(2,128)(2,1)S(1)} async-done(((bf16[128,2,1024]{2,1,0:T(2,128)(2,1)}), bf16[128,2,1024]{2,1,0:T(2,128)(2,1)S(1)}, u32[]{:S(2)}, u32[]{:S(2)}) %all-to-all-start) | async-done | bytes 524320 | tf_op jit(solution)/shard_map/all_to_all | solution.py:196
  48.0 0.2 reshape.20.rows_in
  48.2 0.0 copy-done
  48.2 0.0 copy-done.1
  48.2 0.0 copy-start.2
  48.2 1.2 copy-done.2
  49.4 1.2 shard_map.88
  50.6 3.3 %collective-permute-start.1 = (bf16[64,3072]{1,0:T(8,128)(2,1)S(1)}, bf16[64,3072]{1,0:T(8,128)(2,1)S(1)}, u32[]{:S(2)}, u32[]{:S(2)}) collective-permute-start(bf16[64,3072]{1,0:T(8,128)(2,1)S(1)} %get-tuple-element.15), channel_id=1, source_target_pairs={{0,1},{1,2},{2,3},{3,4},{4,5},{5,6},{6,7},{7,0},{8,9},{9,10},{10,1... | collective-permute-start | bytes 1179656 | tf_op jit(solution)/shard_map/ppermute | solution.py:216
  53.9 4.5 %collective-permute-start.4 = (bf16[32,3072]{1,0:T(8,128)(2,1)S(1)}, bf16[32,3072]{1,0:T(8,128)(2,1)S(1)}, u32[]{:S(2)}, u32[]{:S(2)}) collective-permute-start(bf16[32,3072]{1,0:T(8,128)(2,1)S(1)} %get-tuple-element.17), channel_id=1, source_target_pairs={{0,7},{1,0},{2,1},{3,2},{4,3},{5,4},{6,5},{7,6},{8,15},{9,8},{10,9... | collective-permute-start | bytes 589832 | tf_op jit(solution)/shard_map/ppermute | solution.py:216
  58.4 4.7 %collective-permute-start = (bf16[32,3072]{1,0:T(8,128)(2,1)S(1)}, bf16[32,3072]{1,0:T(8,128)(2,1)S(1)}, u32[]{:S(2)}, u32[]{:S(2)}) collective-permute-start(bf16[32,3072]{1,0:T(8,128)(2,1)S(1)} %get-tuple-element.14), channel_id=1, source_target_pairs={{0,5},{1,6},{2,7},{3,0},{4,1},{5,2},{6,3},{7,4},{8,13},{9,14},{10,... | collective-permute-start | bytes 589832 | tf_op jit(solution)/shard_map/ppermute | solution.py:216
  63.2 0.0 collective-permute-done.4
  63.2 2.5 %collective-permute-done.1 = bf16[64,3072]{1,0:T(8,128)(2,1)S(1)} collective-permute-done((bf16[64,3072]{1,0:T(8,128)(2,1)S(1)}, bf16[64,3072]{1,0:T(8,128)(2,1)S(1)}, u32[]{:S(2)}, u32[]{:S(2)}) %collective-permute-start.1) | collective-permute-done | bytes 393248 | tf_op jit(solution)/shard_map/ppermute | solution.py:216
  65.7 0.1 add_convert_fusion.1
  65.8 7.0 %collective-permute-start.2 = (bf16[32,3072]{1,0:T(8,128)(2,1)S(1)}, bf16[32,3072]{1,0:T(8,128)(2,1)S(1)}, u32[]{:S(2)}, u32[]{:S(2)}) collective-permute-start(bf16[32,3072]{1,0:T(8,128)(2,1)S(1)} %get-tuple-element.21), channel_id=1, source_target_pairs={{0,3},{1,4},{2,5},{3,6},{4,7},{5,0},{6,1},{7,2},{8,11},{9,12},{10,... | collective-permute-start | bytes 589832 | tf_op jit(solution)/shard_map/ppermute | solution.py:216
  72.9 2.2 %collective-permute-start.3 = (bf16[32,3072]{1,0:T(8,128)(2,1)S(1)}, bf16[32,3072]{1,0:T(8,128)(2,1)S(1)}, u32[]{:S(2)}, u32[]{:S(2)}) collective-permute-start(bf16[32,3072]{1,0:T(8,128)(2,1)S(1)} %get-tuple-element.20), channel_id=1, source_target_pairs={{0,1},{1,2},{2,3},{3,4},{4,5},{5,6},{6,7},{7,0},{8,9},{9,10},{10,1... | collective-permute-start | bytes 589832 | tf_op jit(solution)/shard_map/ppermute | solution.py:216
  75.0 4.3 %collective-permute-start.5 = (bf16[32,3072]{1,0:T(8,128)(2,1)S(1)}, bf16[32,3072]{1,0:T(8,128)(2,1)S(1)}, u32[]{:S(2)}, u32[]{:S(2)}) collective-permute-start(bf16[32,3072]{1,0:T(8,128)(2,1)S(1)} %get-tuple-element.22), channel_id=1, source_target_pairs={{0,7},{1,0},{2,1},{3,2},{4,3},{5,4},{6,5},{7,6},{8,15},{9,8},{10,9... | collective-permute-start | bytes 589832 | tf_op jit(solution)/shard_map/ppermute | solution.py:216
  79.4 0.0 collective-permute-done.refs_1_
  79.4 4.3 %collective-permute-done.2.refs_2_ = bf16[32,3072]{1,0:T(8,128)(2,1)S(1)} collective-permute-done((bf16[32,3072]{1,0:T(8,128)(2,1)S(1)}, bf16[32,3072]{1,0:T(8,128)(2,1)S(1)}, u32[]{:S(2)}, u32[]{:S(2)}) %collective-permute-start.2) | collective-permute-done | bytes 196640 | tf_op jit(solution)/shard_map/ppermute | solution.py:216
  83.7 4.6 %collective-permute-done.3.refs_3_ = bf16[32,3072]{1,0:T(8,128)(2,1)S(1)} collective-permute-done((bf16[32,3072]{1,0:T(8,128)(2,1)S(1)}, bf16[32,3072]{1,0:T(8,128)(2,1)S(1)}, u32[]{:S(2)}, u32[]{:S(2)}) %collective-permute-start.3) | collective-permute-done | bytes 196640 | tf_op jit(solution)/shard_map/ppermute | solution.py:216
  88.3 0.0 collective-permute-done.5.refs_4_
  88.3 0.2 shard_map.89
  88.6 34.6 %all_to_all.15 = bf16[8,32,2176]{2,1,0:T(8,128)(2,1)S(1)} all-to-all(bf16[8,32,2176]{2,1,0:T(8,128)(2,1)S(1)} %shard_map.89), channel_id=1, replica_groups=mesh['node'=128,'local'=8] {'local'}, dimensions={0} | all-to-all | bytes 2228224 | tf_op jit(solution)/shard_map/all_to_all | solution.py:236
  123.2 0.7 shard_map.90
  123.9 0.0 copy-start.3
  124.0 0.0 copy-start.4
  124.0 0.8 reshape.22
  124.8 7.5 %all-to-all-start.2 = ((bf16[128,2,640]{2,1,0:T(2,128)(2,1)}), bf16[128,2,640]{2,1,0:T(2,128)(2,1)S(1)}, u32[]{:S(2)}, u32[]{:S(2)}) async-start(bf16[128,2,640]{2,1,0:T(2,128)(2,1)} %reshape.22), calls=%async_computation.2 | async-start | bytes 655360 | tf_op jit(solution)/shard_map/all_to_all | solution.py:244
  132.3 0.0 copy-done.3
  132.3 0.0 copy-done.4
  132.3 0.5 shard_map.86
  132.9 16.1 %all-to-all-done.2 = bf16[128,2,640]{2,1,0:T(2,128)(2,1)S(1)} async-done(((bf16[128,2,640]{2,1,0:T(2,128)(2,1)}), bf16[128,2,640]{2,1,0:T(2,128)(2,1)S(1)}, u32[]{:S(2)}, u32[]{:S(2)}) %all-to-all-start.2) | async-done | bytes 327712 | tf_op jit(solution)/shard_map/all_to_all | solution.py:244
  149.0 0.1 reshape.23.rows_back
  149.1 0.8 shard_map.91
Async XLA Ops:
  2.8 45.4 %copy-start = (bf16[1,512,1024]{2,1,0:T(8,128)(2,1)S(1)}, bf16[1,512,1024]{2,1,0:T(8,128)(2,1)}, u32[]{:S(2)}) copy-start(bf16[1,512,1024]{2,1,0:T(8,128)(2,1)} %param.11) | copy-start | bytes 3145732
  2.8 45.4 %copy-start.1 = (bf16[1,512,1024]{2,1,0:T(8,128)(2,1)S(1)}, bf16[1,512,1024]{2,1,0:T(8,128)(2,1)}, u32[]{:S(2)}) copy-start(bf16[1,512,1024]{2,1,0:T(8,128)(2,1)} %param.12) | copy-start | bytes 3145732
  2.8 45.2 %all-to-all-start = ((bf16[128,2,1024]{2,1,0:T(2,128)(2,1)}), bf16[128,2,1024]{2,1,0:T(2,128)(2,1)S(1)}, u32[]{:S(2)}, u32[]{:S(2)}) async-start(bf16[128,2,1024]{2,1,0:T(2,128)(2,1)} %shard_map.87), calls=%async_computation | async-start | bytes 1048576 | tf_op jit(solution)/shard_map/all_to_all | solution.py:196
  48.2 1.2 copy-start.2
  50.6 15.1 %collective-permute-start.1 = (bf16[64,3072]{1,0:T(8,128)(2,1)S(1)}, bf16[64,3072]{1,0:T(8,128)(2,1)S(1)}, u32[]{:S(2)}, u32[]{:S(2)}) collective-permute-start(bf16[64,3072]{1,0:T(8,128)(2,1)S(1)} %get-tuple-element.15), channel_id=1, source_target_pairs={{0,1},{1,2},{2,3},{3,4},{4,5},{5,6},{6,7},{7,0},{8,9},{9,10},{10,1... | collective-permute-start | bytes 1179656 | tf_op jit(solution)/shard_map/ppermute | solution.py:216
  53.9 9.2 %collective-permute-start.4 = (bf16[32,3072]{1,0:T(8,128)(2,1)S(1)}, bf16[32,3072]{1,0:T(8,128)(2,1)S(1)}, u32[]{:S(2)}, u32[]{:S(2)}) collective-permute-start(bf16[32,3072]{1,0:T(8,128)(2,1)S(1)} %get-tuple-element.17), channel_id=1, source_target_pairs={{0,7},{1,0},{2,1},{3,2},{4,3},{5,4},{6,5},{7,6},{8,15},{9,8},{10,9... | collective-permute-start | bytes 589832 | tf_op jit(solution)/shard_map/ppermute | solution.py:216
  58.4 20.9 %collective-permute-start = (bf16[32,3072]{1,0:T(8,128)(2,1)S(1)}, bf16[32,3072]{1,0:T(8,128)(2,1)S(1)}, u32[]{:S(2)}, u32[]{:S(2)}) collective-permute-start(bf16[32,3072]{1,0:T(8,128)(2,1)S(1)} %get-tuple-element.14), channel_id=1, source_target_pairs={{0,5},{1,6},{2,7},{3,0},{4,1},{5,2},{6,3},{7,4},{8,13},{9,14},{10,... | collective-permute-start | bytes 589832 | tf_op jit(solution)/shard_map/ppermute | solution.py:216
  65.8 17.9 %collective-permute-start.2 = (bf16[32,3072]{1,0:T(8,128)(2,1)S(1)}, bf16[32,3072]{1,0:T(8,128)(2,1)S(1)}, u32[]{:S(2)}, u32[]{:S(2)}) collective-permute-start(bf16[32,3072]{1,0:T(8,128)(2,1)S(1)} %get-tuple-element.21), channel_id=1, source_target_pairs={{0,3},{1,4},{2,5},{3,6},{4,7},{5,0},{6,1},{7,2},{8,11},{9,12},{10,... | collective-permute-start | bytes 589832 | tf_op jit(solution)/shard_map/ppermute | solution.py:216
  72.9 15.5 %collective-permute-start.3 = (bf16[32,3072]{1,0:T(8,128)(2,1)S(1)}, bf16[32,3072]{1,0:T(8,128)(2,1)S(1)}, u32[]{:S(2)}, u32[]{:S(2)}) collective-permute-start(bf16[32,3072]{1,0:T(8,128)(2,1)S(1)} %get-tuple-element.20), channel_id=1, source_target_pairs={{0,1},{1,2},{2,3},{3,4},{4,5},{5,6},{6,7},{7,0},{8,9},{9,10},{10,1... | collective-permute-start | bytes 589832 | tf_op jit(solution)/shard_map/ppermute | solution.py:216
  75.0 13.3 %collective-permute-start.5 = (bf16[32,3072]{1,0:T(8,128)(2,1)S(1)}, bf16[32,3072]{1,0:T(8,128)(2,1)S(1)}, u32[]{:S(2)}, u32[]{:S(2)}) collective-permute-start(bf16[32,3072]{1,0:T(8,128)(2,1)S(1)} %get-tuple-element.22), channel_id=1, source_target_pairs={{0,7},{1,0},{2,1},{3,2},{4,3},{5,4},{6,5},{7,6},{8,15},{9,8},{10,9... | collective-permute-start | bytes 589832 | tf_op jit(solution)/shard_map/ppermute | solution.py:216
  123.9 8.3 %copy-start.3 = (s32[16,8]{0,1:T(8,128)S(1)}, s32[16,8]{0,1:T(8,128)}, u32[]{:S(2)}) copy-start(s32[16,8]{0,1:T(8,128)} %param.10) | copy-start | bytes 1540
  124.0 8.3 %copy-start.4 = (f32[16,8]{0,1:T(8,128)S(1)}, f32[16,8]{0,1:T(8,128)}, u32[]{:S(2)}) copy-start(f32[16,8]{0,1:T(8,128)} %param.9) | copy-start | bytes 1540
  124.8 24.2 %all-to-all-start.2 = ((bf16[128,2,640]{2,1,0:T(2,128)(2,1)}), bf16[128,2,640]{2,1,0:T(2,128)(2,1)S(1)}, u32[]{:S(2)}, u32[]{:S(2)}) async-start(bf16[128,2,640]{2,1,0:T(2,128)(2,1)} %reshape.22), calls=%async_computation.2 | async-start | bytes 655360 | tf_op jit(solution)/shard_map/all_to_all | solution.py:244

commit v6 on v5

--- a/solution.py
+++ b/solution.py
@@ -12,6 +12,7 @@
 VMEM = pl.BlockSpec(memory_space=pltpu.VMEM)
 LIMIT = 40 * 1024 * 1024
 RIGHT, LEFT, FAR, KEPT = (2, 4), 6, 5, (1, 3, 7)
+FROM_HERE, FROM_LEFT, FROM_RIGHT = (0, 5, 3), (7, 4, 2), (1, 6)
 
 
 def slot_choice(ids, slots, capacity):
@@ -51,7 +52,8 @@
     out[:, :, cols:] = picked.reshape(out.shape[0], capacity, cols)
 
 
-def partial_kernel(n_local, index, rows_in, w_gate, w_up, w_down, *refs):
+def partial_kernel(n_local, index, rows_in, w_gate, w_up, w_down, first, *refs):
+    del first
     mine, kept, right, left, far, total = refs
     cols, hidden = w_gate.shape
     step = mine.shape[0]
@@ -91,21 +93,30 @@
     sigmoid_gate = jax.nn.sigmoid(gate_pre)
     act = gate_pre * sigmoid_gate
     grad_up = back_pre * act
-    grad_gate = (
+    out[:, :hidden] = (
         back_pre * up_pre * sigmoid_gate * (1.0 + gate_pre * (1.0 - sigmoid_gate))
     ).astype(BF16)
-    grad_up_sent = grad_up.astype(BF16)
+    out[:, hidden : 2 * hidden] = grad_up.astype(BF16)
     gate_total = jnp.sum(grad_up * up_pre, axis=1, keepdims=True)
-    copies, step, width = out.shape
-    gate_total = jnp.broadcast_to(gate_total, (step, width - 2 * hidden)).astype(BF16)
-    for i in range(copies):
-        out[i, :, :hidden] = grad_gate
-        out[i, :, hidden : 2 * hidden] = grad_up_sent
-        out[i, :, 2 * hidden :] = gate_total
-
-
-def back_kernel(joined, w_gate, w_up, out):
+    extra = out.shape[1] - 2 * hidden
+    out[:, 2 * hidden :] = jnp.broadcast_to(gate_total, (out.shape[0], extra)).astype(BF16)
+
+
+def back_kernel(n_local, index, here, by_three, by_five, from_left, from_right, w_gate, w_up, out, joined):
     cols, hidden = w_gate.shape
+    step = here.shape[0]
+    me = index[0]
+
+    def place(d, part, i):
+        at = pl.multiple_of(lax.rem(me + d, n_local) * step, step)
+        joined[pl.ds(at, step), :] = part[i * step : (i + 1) * step, :]
+
+    for d, part in zip(FROM_HERE, (here, by_three, by_five)):
+        place(d, part, 0)
+    for i, d in enumerate(FROM_LEFT):
+        place(d, from_left, i)
+    for i, d in enumerate(FROM_RIGHT):
+        place(d, from_right, i)
     across = (((1,), (1,)), ((), ()))
     result = lax.dot_general(joined[:, :hidden], w_gate[...], across, preferred_element_type=F32)
     result = result + lax.dot_general(
@@ -206,11 +217,11 @@
             shape((step, 3 * hidden), BF16),
             shape((step, 3 * hidden), BF16),
         ],
-        [smem] + [VMEM] * 4,
+        [smem] + [VMEM] * 4 + [anywhere],
         6 * slots * cols * hidden,
         2 * (3 * cols * hidden + slots * (2 * cols + 3 * hidden)),
         [pltpu.VMEM((slots, 3 * hidden), F32)],
-    )(index, incoming, w_gate[0], w_up[0], w_down[0])
+    )(index, incoming, w_gate[0], w_up[0], w_down[0], weights)
 
     def shifted(value, d):
         return lax.ppermute(value, "local", [(k, (k + d) % n_local) for k in range(n_local)])
@@ -222,25 +233,29 @@
     from_left = shifted(right, 1)
     arrived = [
         shifted(far, FAR),
+        shifted(added(from_left[:step], 0), KEPT[0]),
         shifted(added(from_left[step:], 1), KEPT[1]),
-        shifted(added(from_left[:step], 0), KEPT[0]),
         shifted(added(from_right, 2), KEPT[2]),
     ]
-    copies = build(
+    hidden_grads = build(
         hidden_kernel,
-        shape((n_local, step, 2 * hidden + extra), BF16),
+        shape((step, 2 * hidden + extra), BF16),
         [VMEM] * 5,
         40 * step * hidden,
-        2 * step * hidden * (3 * n_local + 2 * n_local),
+        2 * step * hidden * (3 * n_local + 2),
     )(mine, *arrived)
-    gathered = lax.all_to_all(copies, "local", split_axis=0, concat_axis=0, tiled=True)
+    by_five = shifted(hidden_grads, 5)
+    by_three = shifted(hidden_grads, 3)
+    from_right = shifted(jnp.concatenate([hidden_grads, by_three], axis=0), n_local - 1)
+    from_left = shifted(jnp.concatenate([hidden_grads, by_three, by_five], axis=0), 1)
     sent = build(
-        back_kernel,
+        functools.partial(back_kernel, n_local),
         shape((slots, cols + extra), BF16),
-        [VMEM] * 3,
+        [smem] + [VMEM] * 7,
         4 * slots * cols * hidden,
         2 * (2 * cols * hidden + slots * (2 * hidden + cols)),
-    )(gathered.reshape(slots, 2 * hidden + extra), w_gate[0], w_up[0])
+        [pltpu.VMEM((slots, 2 * hidden + extra), BF16)],
+    )(index, hidden_grads, by_three, by_five, from_left, from_right, w_gate[0], w_up[0])
     back = lax.all_to_all(
         sent.reshape(n_node, capacity, cols + extra), "node", split_axis=0, concat_axis=0, tiled=True
     ).reshape(slots, cols + extra)

time: 150 us -> 146 us (0.973)
  blocking collectives: 34.6 us -> 27.6 us
  starting transfers between devices: 58.1 us -> 64.3 us
  waiting for transfers between devices: 48.2 us -> 45.1 us
    all_to_all x1 -> x0, waiting for transfers between devices: 16.1 us -> none  [on_device(): lax.all_to_all(sent.reshape(n_node, capacity, cols + extra), 'node', spli...]
    ppermute x6 -> x10, starting transfers between devices: 26 us -> 39.7 us  [shifted(): lax.ppermute(value, 'local', [(k, (k + d) % n_local) for k in range(n_loc...]
    ppermute x6 -> x10, waiting for transfers between devices: 11.5 us -> 25.1 us  [shifted(): lax.ppermute(value, 'local', [(k, (k + d) % n_local) for k in range(n_loc...]
    all_to_all x1 -> x0, starting transfers between devices: 7.47 us -> none  [on_device(): lax.all_to_all(sent.reshape(n_node, capacity, cols + extra), 'node', spli...]
    all_to_all x1, blocking collectives: 34.6 us -> 27.6 us  [on_device(): lax.all_to_all(sent.reshape(n_node, capacity, cols + extra), 'node', spli...]
  transfers between devices with their start and end apart: 8 -> 11, of which waited for: 5 -> 7; matrix products, arithmetic and copies ran while one was open for 0% -> 0% of each run, Pallas kernels for 0% -> 0%
where the time goes in v6:
time: 146 us
  starting transfers between devices  64.3 us (44%)
  waiting for transfers between devices  45.1 us (31%)
  blocking collectives  27.6 us (19%)
  Pallas kernels  5.74 us (4%)
  local copies, waits for them, and re-layouts  1.69 us (1%)
    ppermute x10, starting transfers between devices, shifted(): lax.ppermute(value, 'local', [(k, (k + d) % n_local) for k in range(n_loc...  39.7 us
    all_to_all x1, blocking collectives, on_device(): lax.all_to_all(sent.reshape(n_node, capacity, cols + extra), 'node', spli...  27.6 us
    ppermute x10, waiting for transfers between devices, shifted(): lax.ppermute(value, 'local', [(k, (k + d) % n_local) for k in range(n_loc...  25.1 us
    all_to_all x1, starting transfers between devices, on_device(): lax.all_to_all(outgoing, 'node', split_axis=0, concat_axis=0, tiled=True)  24.6 us
    all_to_all x1, waiting for transfers between devices, on_device(): lax.all_to_all(outgoing, 'node', split_axis=0, concat_axis=0, tiled=True)  20 us
  transfers between devices with their start and end apart: 11, of which 7 were waited for; matrix products, arithmetic and copies ran while one was open for 0% of the time, Pallas kernels for 0%

profile of v6, /device:TPU:1, one launch (start us, length us, event | category | flops | bytes accessed | tf_op | source)
XLA Modules:
  0.0 145.6 jit_solution(3784135821963139550)
XLA Ops:
  0.6 0.0 copy-start.3
  0.6 0.0 copy-start.4
  0.7 2.2 %shard_map.87 = bf16[128,2,1024]{2,1,0:T(2,128)(2,1)} custom-call(s32[8,16]{1,0:T(8,128)} %bitcast.12, bf16[16,512]{1,0:T(8,128)(2,1)} %tokens.1, bf16[16,512]{1,0:T(8,128)(2,1)} %grad_out.1), custom_call_target="tpu_custom_call" | custom-call | flops 8388608 | bytes 524288 | tf_op jit(solution)/shard_map/pallas_call | solution.py:186
  2.9 0.0 copy-start
  2.9 0.0 copy-start.1
  2.9 24.6 %all-to-all-start = ((bf16[128,2,1024]{2,1,0:T(2,128)(2,1)}), bf16[128,2,1024]{2,1,0:T(2,128)(2,1)S(1)}, u32[]{:S(2)}, u32[]{:S(2)}) async-start(bf16[128,2,1024]{2,1,0:T(2,128)(2,1)} %shard_map.87), calls=%async_computation | async-start | bytes 1048576 | tf_op jit(solution)/shard_map/all_to_all | solution.py:207
  27.5 0.0 copy-done.3
  27.5 0.0 copy-done.4
  27.5 0.5 shard_map.86
  28.0 20.0 %all-to-all-done = bf16[128,2,1024]{2,1,0:T(2,128)(2,1)S(1)} async-done(((bf16[128,2,1024]{2,1,0:T(2,128)(2,1)}), bf16[128,2,1024]{2,1,0:T(2,128)(2,1)S(1)}, u32[]{:S(2)}, u32[]{:S(2)}) %all-to-all-start) | async-done | bytes 524320 | tf_op jit(solution)/shard_map/all_to_all | solution.py:207
  48.1 0.2 reshape.17.rows_in
  48.3 0.0 copy-done
  48.3 0.0 copy-done.1
  48.3 0.0 copy-start.2
  48.3 1.2 copy-done.2
  49.5 1.2 shard_map.88
  50.7 3.3 %collective-permute-start.1 = (bf16[64,3072]{1,0:T(8,128)(2,1)S(1)}, bf16[64,3072]{1,0:T(8,128)(2,1)S(1)}, u32[]{:S(2)}, u32[]{:S(2)}) collective-permute-start(bf16[64,3072]{1,0:T(8,128)(2,1)S(1)} %get-tuple-element.15), channel_id=1, source_target_pairs={{0,1},{1,2},{2,3},{3,4},{4,5},{5,6},{6,7},{7,0},{8,9},{9,10},{10,1... | collective-permute-start | bytes 1179656 | tf_op jit(solution)/shard_map/ppermute | solution.py:227
  54.0 4.5 %collective-permute-start.4 = (bf16[32,3072]{1,0:T(8,128)(2,1)S(1)}, bf16[32,3072]{1,0:T(8,128)(2,1)S(1)}, u32[]{:S(2)}, u32[]{:S(2)}) collective-permute-start(bf16[32,3072]{1,0:T(8,128)(2,1)S(1)} %get-tuple-element.17), channel_id=1, source_target_pairs={{0,7},{1,0},{2,1},{3,2},{4,3},{5,4},{6,5},{7,6},{8,15},{9,8},{10,9... | collective-permute-start | bytes 589832 | tf_op jit(solution)/shard_map/ppermute | solution.py:227
  58.5 4.7 %collective-permute-start = (bf16[32,3072]{1,0:T(8,128)(2,1)S(1)}, bf16[32,3072]{1,0:T(8,128)(2,1)S(1)}, u32[]{:S(2)}, u32[]{:S(2)}) collective-permute-start(bf16[32,3072]{1,0:T(8,128)(2,1)S(1)} %get-tuple-element.14), channel_id=1, source_target_pairs={{0,5},{1,6},{2,7},{3,0},{4,1},{5,2},{6,3},{7,4},{8,13},{9,14},{10,... | collective-permute-start | bytes 589832 | tf_op jit(solution)/shard_map/ppermute | solution.py:227
  63.2 0.0 collective-permute-done.4
  63.2 2.6 %collective-permute-done.1 = bf16[64,3072]{1,0:T(8,128)(2,1)S(1)} collective-permute-done((bf16[64,3072]{1,0:T(8,128)(2,1)S(1)}, bf16[64,3072]{1,0:T(8,128)(2,1)S(1)}, u32[]{:S(2)}, u32[]{:S(2)}) %collective-permute-start.1) | collective-permute-done | bytes 393248 | tf_op jit(solution)/shard_map/ppermute | solution.py:227
  65.8 0.1 add_convert_fusion.1
  65.9 7.0 %collective-permute-start.3 = (bf16[32,3072]{1,0:T(8,128)(2,1)S(1)}, bf16[32,3072]{1,0:T(8,128)(2,1)S(1)}, u32[]{:S(2)}, u32[]{:S(2)}) collective-permute-start(bf16[32,3072]{1,0:T(8,128)(2,1)S(1)} %get-tuple-element.20), channel_id=1, source_target_pairs={{0,3},{1,4},{2,5},{3,6},{4,7},{5,0},{6,1},{7,2},{8,11},{9,12},{10,... | collective-permute-start | bytes 589832 | tf_op jit(solution)/shard_map/ppermute | solution.py:227
  73.0 2.1 %collective-permute-start.2 = (bf16[32,3072]{1,0:T(8,128)(2,1)S(1)}, bf16[32,3072]{1,0:T(8,128)(2,1)S(1)}, u32[]{:S(2)}, u32[]{:S(2)}) collective-permute-start(bf16[32,3072]{1,0:T(8,128)(2,1)S(1)} %get-tuple-element.21), channel_id=1, source_target_pairs={{0,1},{1,2},{2,3},{3,4},{4,5},{5,6},{6,7},{7,0},{8,9},{9,10},{10,1... | collective-permute-start | bytes 589832 | tf_op jit(solution)/shard_map/ppermute | solution.py:227
  75.1 4.3 %collective-permute-start.5 = (bf16[32,3072]{1,0:T(8,128)(2,1)S(1)}, bf16[32,3072]{1,0:T(8,128)(2,1)S(1)}, u32[]{:S(2)}, u32[]{:S(2)}) collective-permute-start(bf16[32,3072]{1,0:T(8,128)(2,1)S(1)} %get-tuple-element.22), channel_id=1, source_target_pairs={{0,7},{1,0},{2,1},{3,2},{4,3},{5,4},{6,5},{7,6},{8,15},{9,8},{10,9... | collective-permute-start | bytes 589832 | tf_op jit(solution)/shard_map/ppermute | solution.py:227
  79.5 0.0 collective-permute-done.refs_1_
  79.5 4.3 %collective-permute-done.3.refs_3_ = bf16[32,3072]{1,0:T(8,128)(2,1)S(1)} collective-permute-done((bf16[32,3072]{1,0:T(8,128)(2,1)S(1)}, bf16[32,3072]{1,0:T(8,128)(2,1)S(1)}, u32[]{:S(2)}, u32[]{:S(2)}) %collective-permute-start.3) | collective-permute-done | bytes 196640 | tf_op jit(solution)/shard_map/ppermute | solution.py:227
  83.8 4.6 %collective-permute-done.2.refs_2_ = bf16[32,3072]{1,0:T(8,128)(2,1)S(1)} collective-permute-done((bf16[32,3072]{1,0:T(8,128)(2,1)S(1)}, bf16[32,3072]{1,0:T(8,128)(2,1)S(1)}, u32[]{:S(2)}, u32[]{:S(2)}) %collective-permute-start.2) | collective-permute-done | bytes 196640 | tf_op jit(solution)/shard_map/ppermute | solution.py:227
  88.4 0.0 collective-permute-done.5.refs_4_
  88.4 0.2 shard_map.89.here
  88.6 4.3 %collective-permute-start.7 = (bf16[32,2176]{1,0:T(8,128)(2,1)S(1)}, bf16[32,2176]{1,0:T(8,128)(2,1)S(1)}, u32[]{:S(2)}, u32[]{:S(2)}) collective-permute-start(bf16[32,2176]{1,0:T(8,128)(2,1)S(1)} %shard_map.89.here), channel_id=1, source_target_pairs={{0,5},{1,6},{2,7},{3,0},{4,1},{5,2},{6,3},{7,4},{8,13},{9,14},{10,... | collective-permute-start | bytes 417800 | tf_op jit(solution)/shard_map/ppermute | solution.py:227
  92.9 2.8 %collective-permute-start.6 = (bf16[32,2176]{1,0:T(8,128)(2,1)S(1)}, bf16[32,2176]{1,0:T(8,128)(2,1)S(1)}, u32[]{:S(2)}, u32[]{:S(2)}) collective-permute-start(bf16[32,2176]{1,0:T(8,128)(2,1)S(1)} %shard_map.89.here), channel_id=1, source_target_pairs={{0,3},{1,4},{2,5},{3,6},{4,7},{5,0},{6,1},{7,2},{8,11},{9,12},{10,... | collective-permute-start | bytes 417800 | tf_op jit(solution)/shard_map/ppermute | solution.py:227
  95.7 1.4 collective-permute-done.7.by_five
  97.2 7.9 %collective-permute-done.6.by_three = bf16[32,2176]{1,0:T(8,128)(2,1)S(1)} collective-permute-done((bf16[32,2176]{1,0:T(8,128)(2,1)S(1)}, bf16[32,2176]{1,0:T(8,128)(2,1)S(1)}, u32[]{:S(2)}, u32[]{:S(2)}) %collective-permute-start.6) | collective-permute-done | bytes 139296 | tf_op jit(solution)/shard_map/ppermute | solution.py:227
  105.1 2.5 %collective-permute-start.8 = (bf16[96,2176]{1,0:T(8,128)(2,1)S(1)}, bf16[96,2176]{1,0:T(8,128)(2,1)S(1)}, u32[]{:S(2)}, u32[]{:S(2)}) collective-permute-start(bf16[96,2176]{1,0:T(8,128)(2,1)S(1)} %pad_maximum_fusion), channel_id=1, source_target_pairs={{0,1},{1,2},{2,3},{3,4},{4,5},{5,6},{6,7},{7,0},{8,9},{9,10},{10,1... | collective-permute-start | bytes 1253384 | tf_op jit(solution)/shard_map/ppermute | solution.py:227
  107.7 4.1 %collective-permute-start.9 = (bf16[64,2176]{1,0:T(8,128)(2,1)S(1)}, bf16[64,2176]{1,0:T(8,128)(2,1)S(1)}, u32[]{:S(2)}, u32[]{:S(2)}) collective-permute-start(bf16[64,2176]{1,0:T(8,128)(2,1)S(1)} %pad_maximum_fusion.1), channel_id=1, source_target_pairs={{0,7},{1,0},{2,1},{3,2},{4,3},{5,4},{6,5},{7,6},{8,15},{9,8},{10,9... | collective-permute-start | bytes 835592 | tf_op jit(solution)/shard_map/ppermute | solution.py:227
  111.8 4.3 %collective-permute-done.9.from_right = bf16[64,2176]{1,0:T(8,128)(2,1)S(1)} collective-permute-done((bf16[64,2176]{1,0:T(8,128)(2,1)S(1)}, bf16[64,2176]{1,0:T(8,128)(2,1)S(1)}, u32[]{:S(2)}, u32[]{:S(2)}) %collective-permute-start.9) | collective-permute-done | bytes 278560 | tf_op jit(solution)/shard_map/ppermute | solution.py:227
  116.1 0.0 collective-permute-done.8.from_left
  116.1 0.8 shard_map.90
  116.9 0.1 reshape.18
  117.0 27.6 %all_to_all.10 = bf16[128,2,640]{2,1,0:T(2,128)(2,1)S(1)} all-to-all(bf16[128,2,640]{2,1,0:T(2,128)(2,1)S(1)} %reshape.18), channel_id=1, replica_groups=mesh['node'=128,'local'=8] {'node'}, dimensions={0} | all-to-all | bytes 655360 | tf_op jit(solution)/shard_map/all_to_all | solution.py:259
  144.6 0.1 reshape.19.rows_back
  144.7 0.8 shard_map.91
  (2 shorter events, 0.1 us)
Async XLA Ops:
  0.6 26.9 %copy-start.3 = (s32[16,8]{0,1:T(8,128)S(1)}, s32[16,8]{0,1:T(8,128)}, u32[]{:S(2)}) copy-start(s32[16,8]{0,1:T(8,128)} %param.10) | copy-start | bytes 1540
  0.6 26.9 %copy-start.4 = (f32[16,8]{0,1:T(8,128)S(1)}, f32[16,8]{0,1:T(8,128)}, u32[]{:S(2)}) copy-start(f32[16,8]{0,1:T(8,128)} %param.9) | copy-start | bytes 1540
  2.9 45.4 %copy-start = (bf16[1,512,1024]{2,1,0:T(8,128)(2,1)S(1)}, bf16[1,512,1024]{2,1,0:T(8,128)(2,1)}, u32[]{:S(2)}) copy-start(bf16[1,512,1024]{2,1,0:T(8,128)(2,1)} %param.11) | copy-start | bytes 3145732
  2.9 45.4 %copy-start.1 = (bf16[1,512,1024]{2,1,0:T(8,128)(2,1)S(1)}, bf16[1,512,1024]{2,1,0:T(8,128)(2,1)}, u32[]{:S(2)}) copy-start(bf16[1,512,1024]{2,1,0:T(8,128)(2,1)} %param.12) | copy-start | bytes 3145732
  2.9 45.2 %all-to-all-start = ((bf16[128,2,1024]{2,1,0:T(2,128)(2,1)}), bf16[128,2,1024]{2,1,0:T(2,128)(2,1)S(1)}, u32[]{:S(2)}, u32[]{:S(2)}) async-start(bf16[128,2,1024]{2,1,0:T(2,128)(2,1)} %shard_map.87), calls=%async_computation | async-start | bytes 1048576 | tf_op jit(solution)/shard_map/all_to_all | solution.py:207
  48.3 1.2 copy-start.2
  50.7 15.1 %collective-permute-start.1 = (bf16[64,3072]{1,0:T(8,128)(2,1)S(1)}, bf16[64,3072]{1,0:T(8,128)(2,1)S(1)}, u32[]{:S(2)}, u32[]{:S(2)}) collective-permute-start(bf16[64,3072]{1,0:T(8,128)(2,1)S(1)} %get-tuple-element.15), channel_id=1, source_target_pairs={{0,1},{1,2},{2,3},{3,4},{4,5},{5,6},{6,7},{7,0},{8,9},{9,10},{10,1... | collective-permute-start | bytes 1179656 | tf_op jit(solution)/shard_map/ppermute | solution.py:227
  54.0 9.2 %collective-permute-start.4 = (bf16[32,3072]{1,0:T(8,128)(2,1)S(1)}, bf16[32,3072]{1,0:T(8,128)(2,1)S(1)}, u32[]{:S(2)}, u32[]{:S(2)}) collective-permute-start(bf16[32,3072]{1,0:T(8,128)(2,1)S(1)} %get-tuple-element.17), channel_id=1, source_target_pairs={{0,7},{1,0},{2,1},{3,2},{4,3},{5,4},{6,5},{7,6},{8,15},{9,8},{10,9... | collective-permute-start | bytes 589832 | tf_op jit(solution)/shard_map/ppermute | solution.py:227
  58.5 21.0 %collective-permute-start = (bf16[32,3072]{1,0:T(8,128)(2,1)S(1)}, bf16[32,3072]{1,0:T(8,128)(2,1)S(1)}, u32[]{:S(2)}, u32[]{:S(2)}) collective-permute-start(bf16[32,3072]{1,0:T(8,128)(2,1)S(1)} %get-tuple-element.14), channel_id=1, source_target_pairs={{0,5},{1,6},{2,7},{3,0},{4,1},{5,2},{6,3},{7,4},{8,13},{9,14},{10,... | collective-permute-start | bytes 589832 | tf_op jit(solution)/shard_map/ppermute | solution.py:227
  65.9 17.9 %collective-permute-start.3 = (bf16[32,3072]{1,0:T(8,128)(2,1)S(1)}, bf16[32,3072]{1,0:T(8,128)(2,1)S(1)}, u32[]{:S(2)}, u32[]{:S(2)}) collective-permute-start(bf16[32,3072]{1,0:T(8,128)(2,1)S(1)} %get-tuple-element.20), channel_id=1, source_target_pairs={{0,3},{1,4},{2,5},{3,6},{4,7},{5,0},{6,1},{7,2},{8,11},{9,12},{10,... | collective-permute-start | bytes 589832 | tf_op jit(solution)/shard_map/ppermute | solution.py:227
  73.0 15.4 %collective-permute-start.2 = (bf16[32,3072]{1,0:T(8,128)(2,1)S(1)}, bf16[32,3072]{1,0:T(8,128)(2,1)S(1)}, u32[]{:S(2)}, u32[]{:S(2)}) collective-permute-start(bf16[32,3072]{1,0:T(8,128)(2,1)S(1)} %get-tuple-element.21), channel_id=1, source_target_pairs={{0,1},{1,2},{2,3},{3,4},{4,5},{5,6},{6,7},{7,0},{8,9},{9,10},{10,1... | collective-permute-start | bytes 589832 | tf_op jit(solution)/shard_map/ppermute | solution.py:227
  75.1 13.3 %collective-permute-start.5 = (bf16[32,3072]{1,0:T(8,128)(2,1)S(1)}, bf16[32,3072]{1,0:T(8,128)(2,1)S(1)}, u32[]{:S(2)}, u32[]{:S(2)}) collective-permute-start(bf16[32,3072]{1,0:T(8,128)(2,1)S(1)} %get-tuple-element.22), channel_id=1, source_target_pairs={{0,7},{1,0},{2,1},{3,2},{4,3},{5,4},{6,5},{7,6},{8,15},{9,8},{10,9... | collective-permute-start | bytes 589832 | tf_op jit(solution)/shard_map/ppermute | solution.py:227
  88.6 8.5 %collective-permute-start.7 = (bf16[32,2176]{1,0:T(8,128)(2,1)S(1)}, bf16[32,2176]{1,0:T(8,128)(2,1)S(1)}, u32[]{:S(2)}, u32[]{:S(2)}) collective-permute-start(bf16[32,2176]{1,0:T(8,128)(2,1)S(1)} %shard_map.89.here), channel_id=1, source_target_pairs={{0,5},{1,6},{2,7},{3,0},{4,1},{5,2},{6,3},{7,4},{8,13},{9,14},{10,... | collective-permute-start | bytes 417800 | tf_op jit(solution)/shard_map/ppermute | solution.py:227
  92.9 12.1 %collective-permute-start.6 = (bf16[32,2176]{1,0:T(8,128)(2,1)S(1)}, bf16[32,2176]{1,0:T(8,128)(2,1)S(1)}, u32[]{:S(2)}, u32[]{:S(2)}) collective-permute-start(bf16[32,2176]{1,0:T(8,128)(2,1)S(1)} %shard_map.89.here), channel_id=1, source_target_pairs={{0,3},{1,4},{2,5},{3,6},{4,7},{5,0},{6,1},{7,2},{8,11},{9,12},{10,... | collective-permute-start | bytes 417800 | tf_op jit(solution)/shard_map/ppermute | solution.py:227
  105.1 11.0 %collective-permute-start.8 = (bf16[96,2176]{1,0:T(8,128)(2,1)S(1)}, bf16[96,2176]{1,0:T(8,128)(2,1)S(1)}, u32[]{:S(2)}, u32[]{:S(2)}) collective-permute-start(bf16[96,2176]{1,0:T(8,128)(2,1)S(1)} %pad_maximum_fusion), channel_id=1, source_target_pairs={{0,1},{1,2},{2,3},{3,4},{4,5},{5,6},{6,7},{7,0},{8,9},{9,10},{10,1... | collective-permute-start | bytes 1253384 | tf_op jit(solution)/shard_map/ppermute | solution.py:227
  107.7 8.4 %collective-permute-start.9 = (bf16[64,2176]{1,0:T(8,128)(2,1)S(1)}, bf16[64,2176]{1,0:T(8,128)(2,1)S(1)}, u32[]{:S(2)}, u32[]{:S(2)}) collective-permute-start(bf16[64,2176]{1,0:T(8,128)(2,1)S(1)} %pad_maximum_fusion.1), channel_id=1, source_target_pairs={{0,7},{1,0},{2,1},{3,2},{4,3},{5,4},{6,5},{7,6},{8,15},{9,8},{10,9... | collective-permute-start | bytes 835592 | tf_op jit(solution)/shard_map/ppermute | solution.py:227

commit v7 on v6

--- a/solution.py
+++ b/solution.py
@@ -11,8 +11,8 @@
 F32 = jnp.float32
 VMEM = pl.BlockSpec(memory_space=pltpu.VMEM)
 LIMIT = 40 * 1024 * 1024
-RIGHT, LEFT, FAR, KEPT = (2, 4), 6, 5, (1, 3, 7)
-FROM_HERE, FROM_LEFT, FROM_RIGHT = (0, 5, 3), (7, 4, 2), (1, 6)
+RIGHT, LEFT, FAR, KEPT_RIGHT, KEPT_LEFT = (2, 4), 6, 5, (1, 3), 7
+FROM_HERE, FROM_LEFT, FROM_RIGHT, FROM_RIGHT_LATE = (0, 5, 3), (7, 2), (1, 4), 6
 
 
 def slot_choice(ids, slots, capacity):
@@ -54,7 +54,7 @@
 
 def partial_kernel(n_local, index, rows_in, w_gate, w_up, w_down, first, *refs):
     del first
-    mine, kept, right, left, far, total = refs
+    mine, kept_right, kept_left, right, left, far, total = refs
     cols, hidden = w_gate.shape
     step = mine.shape[0]
     x = rows_in[:, :cols]
@@ -71,8 +71,9 @@
         return total[pl.ds(place, step), :]
 
     mine[...] = chunk(0)
-    for i, d in enumerate(KEPT):
-        kept[i * step : (i + 1) * step, :] = chunk(d)
+    for i, d in enumerate(KEPT_RIGHT):
+        kept_right[i * step : (i + 1) * step, :] = chunk(d)
+    kept_left[...] = chunk(KEPT_LEFT)
     for i, d in enumerate(RIGHT):
         right[i * step : (i + 1) * step, :] = chunk(d).astype(BF16)
     left[...] = chunk(LEFT).astype(BF16)
@@ -102,7 +103,7 @@
     out[:, 2 * hidden :] = jnp.broadcast_to(gate_total, (out.shape[0], extra)).astype(BF16)
 
 
-def back_kernel(n_local, index, here, by_three, by_five, from_left, from_right, w_gate, w_up, out, joined):
+def back_kernel(n_local, index, here, by_three, by_five, from_left, from_right, late, w_gate, w_up, out, joined):
     cols, hidden = w_gate.shape
     step = here.shape[0]
     me = index[0]
@@ -117,6 +118,7 @@
         place(d, from_left, i)
     for i, d in enumerate(FROM_RIGHT):
         place(d, from_right, i)
+    place(FROM_RIGHT_LATE, late, 0)
     across = (((1,), (1,)), ((), ()))
     result = lax.dot_general(joined[:, :hidden], w_gate[...], across, preferred_element_type=F32)
     result = result + lax.dot_general(
@@ -208,11 +210,12 @@
         outgoing, "node", split_axis=0, concat_axis=0, tiled=True
     ).reshape(slots, 2 * cols)
 
-    mine, kept, right, left, far = build(
+    mine, kept_right, kept_left, right, left, far = build(
         functools.partial(partial_kernel, n_local),
         [
             shape((step, 3 * hidden), F32),
-            shape((len(KEPT) * step, 3 * hidden), F32),
+            shape((len(KEPT_RIGHT) * step, 3 * hidden), F32),
+            shape((step, 3 * hidden), F32),
             shape((len(RIGHT) * step, 3 * hidden), BF16),
             shape((step, 3 * hidden), BF16),
             shape((step, 3 * hidden), BF16),
@@ -226,16 +229,16 @@
     def shifted(value, d):
         return lax.ppermute(value, "local", [(k, (k + d) % n_local) for k in range(n_local)])
 
-    def added(sent, place):
-        return (sent.astype(F32) + kept[place * step : (place + 1) * step]).astype(BF16)
-
+    def added(sent, kept):
+        return (sent.astype(F32) + kept).astype(BF16)
+
+    from_left = shifted(right, 1)
     from_right = shifted(left, n_local - 1)
-    from_left = shifted(right, 1)
     arrived = [
         shifted(far, FAR),
-        shifted(added(from_left[:step], 0), KEPT[0]),
-        shifted(added(from_left[step:], 1), KEPT[1]),
-        shifted(added(from_right, 2), KEPT[2]),
+        shifted(added(from_left[:step], kept_right[:step]), KEPT_RIGHT[0]),
+        shifted(added(from_left[step:], kept_right[step:]), KEPT_RIGHT[1]),
+        shifted(added(from_right, kept_left), KEPT_LEFT),
     ]
     hidden_grads = build(
         hidden_kernel,
@@ -246,16 +249,18 @@
     )(mine, *arrived)
     by_five = shifted(hidden_grads, 5)
     by_three = shifted(hidden_grads, 3)
-    from_right = shifted(jnp.concatenate([hidden_grads, by_three], axis=0), n_local - 1)
-    from_left = shifted(jnp.concatenate([hidden_grads, by_three, by_five], axis=0), 1)
+    both = jnp.concatenate([hidden_grads, by_five], axis=0)
+    gathered_left = shifted(both, 1)
+    gathered_right = shifted(both, n_local - 1)
+    late = shifted(by_three, n_local - 1)
     sent = build(
         functools.partial(back_kernel, n_local),
         shape((slots, cols + extra), BF16),
-        [smem] + [VMEM] * 7,
+        [smem] + [VMEM] * 8,
         4 * slots * cols * hidden,
         2 * (2 * cols * hidden + slots * (2 * hidden + cols)),
         [pltpu.VMEM((slots, 2 * hidden + extra), BF16)],
-    )(index, hidden_grads, by_three, by_five, from_left, from_right, w_gate[0], w_up[0])
+    )(index, hidden_grads, by_three, by_five, gathered_left, gathered_right, late, w_gate[0], w_up[0])
     back = lax.all_to_all(
         sent.reshape(n_node, capacity, cols + extra), "node", split_axis=0, concat_axis=0, tiled=True
     ).reshape(slots, cols + extra)

time: 146 us -> 149 us (1.021)
  waiting for transfers between devices: 45.1 us -> 53.6 us
  blocking collectives: 27.6 us -> 22.5 us
    ppermute x10 -> x11, waiting for transfers between devices: 25.1 us -> 33.6 us  [shifted(): lax.ppermute(value, 'local', [(k, (k + d) % n_local) for k in range(n_loc...]
    all_to_all x1, blocking collectives: 27.6 us -> 22.5 us  [on_device(): lax.all_to_all(sent.reshape(n_node, capacity, cols + extra), 'node', spli...]
    ppermute x10 -> x11, starting transfers between devices: 39.7 us -> 39.2 us  [shifted(): lax.ppermute(value, 'local', [(k, (k + d) % n_local) for k in range(n_loc...]
  transfers between devices with their start and end apart: 11 -> 12, of which waited for: 7 -> 8; matrix products, arithmetic and copies ran while one was open for 0% -> 0% of each run, Pallas kernels for 0% -> 0%
where the time goes in v7:
time: 149 us; the launch traced here: 148 us
  starting transfers between devices  63.8 us (43%)
  waiting for transfers between devices  53.6 us (36%)
  blocking collectives  22.5 us (15%)
  Pallas kernels  5.74 us (4%)
  local copies, waits for them, and re-layouts  1.69 us (1%)
    ppermute x11, starting transfers between devices, shifted(): lax.ppermute(value, 'local', [(k, (k + d) % n_local) for k in range(n_loc...  39.2 us
    ppermute x11, waiting for transfers between devices, shifted(): lax.ppermute(value, 'local', [(k, (k + d) % n_local) for k in range(n_loc...  33.6 us
    all_to_all x1, starting transfers between devices, on_device(): lax.all_to_all(outgoing, 'node', split_axis=0, concat_axis=0, tiled=True)  24.6 us
    all_to_all x1, blocking collectives, on_device(): lax.all_to_all(sent.reshape(n_node, capacity, cols + extra), 'node', spli...  22.5 us
    all_to_all x1, waiting for transfers between devices, on_device(): lax.all_to_all(outgoing, 'node', split_axis=0, concat_axis=0, tiled=True)  20 us
  transfers between devices with their start and end apart: 12, of which 8 were waited for; matrix products, arithmetic and copies ran while one was open for 0% of the time, Pallas kernels for 0%

profile of v7, /device:TPU:1, one launch (start us, length us, event | category | flops | bytes accessed | tf_op | source)
XLA Modules:
  0.0 148.4 jit_solution(15174256462372383185)
XLA Ops:
  0.6 0.0 copy-start.3
  0.6 0.0 copy-start.4
  0.7 2.2 %shard_map.87 = bf16[128,2,1024]{2,1,0:T(2,128)(2,1)} custom-call(s32[8,16]{1,0:T(8,128)} %bitcast.12, bf16[16,512]{1,0:T(8,128)(2,1)} %tokens.1, bf16[16,512]{1,0:T(8,128)(2,1)} %grad_out.1), custom_call_target="tpu_custom_call" | custom-call | flops 8388608 | bytes 524288 | tf_op jit(solution)/shard_map/pallas_call | solution.py:188
  2.9 0.0 copy-start
  2.9 0.0 copy-start.1
  2.9 24.6 %all-to-all-start = ((bf16[128,2,1024]{2,1,0:T(2,128)(2,1)}), bf16[128,2,1024]{2,1,0:T(2,128)(2,1)S(1)}, u32[]{:S(2)}, u32[]{:S(2)}) async-start(bf16[128,2,1024]{2,1,0:T(2,128)(2,1)} %shard_map.87), calls=%async_computation | async-start | bytes 1048576 | tf_op jit(solution)/shard_map/all_to_all | solution.py:209
  27.5 0.0 copy-done.3
  27.5 0.0 copy-done.4
  27.5 0.5 shard_map.86
  28.1 20.0 %all-to-all-done = bf16[128,2,1024]{2,1,0:T(2,128)(2,1)S(1)} async-done(((bf16[128,2,1024]{2,1,0:T(2,128)(2,1)}), bf16[128,2,1024]{2,1,0:T(2,128)(2,1)S(1)}, u32[]{:S(2)}, u32[]{:S(2)}) %all-to-all-start) | async-done | bytes 524320 | tf_op jit(solution)/shard_map/all_to_all | solution.py:209
  48.1 0.2 reshape.17.rows_in
  48.3 0.0 copy-done
  48.3 0.0 copy-done.1
  48.3 0.0 copy-start.2
  48.3 1.2 copy-done.2
  49.5 1.2 shard_map.88
  50.7 5.9 %collective-permute-start.4 = (bf16[32,3072]{1,0:T(8,128)(2,1)S(1)}, bf16[32,3072]{1,0:T(8,128)(2,1)S(1)}, u32[]{:S(2)}, u32[]{:S(2)}) collective-permute-start(bf16[32,3072]{1,0:T(8,128)(2,1)S(1)} %get-tuple-element.18), channel_id=1, source_target_pairs={{0,7},{1,0},{2,1},{3,2},{4,3},{5,4},{6,5},{7,6},{8,15},{9,8},{10,9... | collective-permute-start | bytes 589832 | tf_op jit(solution)/shard_map/ppermute | solution.py:230
  56.6 4.2 %collective-permute-start = (bf16[32,3072]{1,0:T(8,128)(2,1)S(1)}, bf16[32,3072]{1,0:T(8,128)(2,1)S(1)}, u32[]{:S(2)}, u32[]{:S(2)}) collective-permute-start(bf16[32,3072]{1,0:T(8,128)(2,1)S(1)} %get-tuple-element.15), channel_id=1, source_target_pairs={{0,5},{1,6},{2,7},{3,0},{4,1},{5,2},{6,3},{7,4},{8,13},{9,14},{10,... | collective-permute-start | bytes 589832 | tf_op jit(solution)/shard_map/ppermute | solution.py:230
  60.8 2.4 %collective-permute-start.1 = (bf16[64,3072]{1,0:T(8,128)(2,1)S(1)}, bf16[64,3072]{1,0:T(8,128)(2,1)S(1)}, u32[]{:S(2)}, u32[]{:S(2)}) collective-permute-start(bf16[64,3072]{1,0:T(8,128)(2,1)S(1)} %get-tuple-element.16), channel_id=1, source_target_pairs={{0,1},{1,2},{2,3},{3,4},{4,5},{5,6},{6,7},{7,0},{8,9},{9,10},{10,1... | collective-permute-start | bytes 1179656 | tf_op jit(solution)/shard_map/ppermute | solution.py:230
  63.2 0.0 collective-permute-done.4
  63.3 0.1 add_convert_fusion
  63.3 4.1 %collective-permute-start.5 = (bf16[32,3072]{1,0:T(8,128)(2,1)S(1)}, bf16[32,3072]{1,0:T(8,128)(2,1)S(1)}, u32[]{:S(2)}, u32[]{:S(2)}) collective-permute-start(bf16[32,3072]{1,0:T(8,128)(2,1)S(1)} %add_convert_fusion), channel_id=1, source_target_pairs={{0,7},{1,0},{2,1},{3,2},{4,3},{5,4},{6,5},{7,6},{8,15},{9,8},{10,9... | collective-permute-start | bytes 589832 | tf_op jit(solution)/shard_map/ppermute | solution.py:230
  67.4 7.1 %collective-permute-done.1 = bf16[64,3072]{1,0:T(8,128)(2,1)S(1)} collective-permute-done((bf16[64,3072]{1,0:T(8,128)(2,1)S(1)}, bf16[64,3072]{1,0:T(8,128)(2,1)S(1)}, u32[]{:S(2)}, u32[]{:S(2)}) %collective-permute-start.1) | collective-permute-done | bytes 393248 | tf_op jit(solution)/shard_map/ppermute | solution.py:230
  74.5 0.1 add_convert_fusion.1
  74.6 1.9 %collective-permute-start.3 = (bf16[32,3072]{1,0:T(8,128)(2,1)S(1)}, bf16[32,3072]{1,0:T(8,128)(2,1)S(1)}, u32[]{:S(2)}, u32[]{:S(2)}) collective-permute-start(bf16[32,3072]{1,0:T(8,128)(2,1)S(1)} %get-tuple-element.22), channel_id=1, source_target_pairs={{0,3},{1,4},{2,5},{3,6},{4,7},{5,0},{6,1},{7,2},{8,11},{9,12},{10,... | collective-permute-start | bytes 589832 | tf_op jit(solution)/shard_map/ppermute | solution.py:230
  76.5 3.1 %collective-permute-start.2 = (bf16[32,3072]{1,0:T(8,128)(2,1)S(1)}, bf16[32,3072]{1,0:T(8,128)(2,1)S(1)}, u32[]{:S(2)}, u32[]{:S(2)}) collective-permute-start(bf16[32,3072]{1,0:T(8,128)(2,1)S(1)} %get-tuple-element.23), channel_id=1, source_target_pairs={{0,1},{1,2},{2,3},{3,4},{4,5},{5,6},{6,7},{7,0},{8,9},{9,10},{10,1... | collective-permute-start | bytes 589832 | tf_op jit(solution)/shard_map/ppermute | solution.py:230
  79.6 0.0 collective-permute-done.refs_1_
  79.6 0.0 collective-permute-done.5.refs_4_
  79.7 12.7 %collective-permute-done.3.refs_3_ = bf16[32,3072]{1,0:T(8,128)(2,1)S(1)} collective-permute-done((bf16[32,3072]{1,0:T(8,128)(2,1)S(1)}, bf16[32,3072]{1,0:T(8,128)(2,1)S(1)}, u32[]{:S(2)}, u32[]{:S(2)}) %collective-permute-start.3) | collective-permute-done | bytes 196640 | tf_op jit(solution)/shard_map/ppermute | solution.py:230
  92.4 3.1 %collective-permute-done.2.refs_2_ = bf16[32,3072]{1,0:T(8,128)(2,1)S(1)} collective-permute-done((bf16[32,3072]{1,0:T(8,128)(2,1)S(1)}, bf16[32,3072]{1,0:T(8,128)(2,1)S(1)}, u32[]{:S(2)}, u32[]{:S(2)}) %collective-permute-start.2) | collective-permute-done | bytes 196640 | tf_op jit(solution)/shard_map/ppermute | solution.py:230
  95.5 0.2 shard_map.89.here
  95.7 2.8 %collective-permute-start.7 = (bf16[32,2176]{1,0:T(8,128)(2,1)S(1)}, bf16[32,2176]{1,0:T(8,128)(2,1)S(1)}, u32[]{:S(2)}, u32[]{:S(2)}) collective-permute-start(bf16[32,2176]{1,0:T(8,128)(2,1)S(1)} %shard_map.89.here), channel_id=1, source_target_pairs={{0,5},{1,6},{2,7},{3,0},{4,1},{5,2},{6,3},{7,4},{8,13},{9,14},{10,... | collective-permute-start | bytes 417800 | tf_op jit(solution)/shard_map/ppermute | solution.py:230
  98.5 4.2 %collective-permute-start.6 = (bf16[32,2176]{1,0:T(8,128)(2,1)S(1)}, bf16[32,2176]{1,0:T(8,128)(2,1)S(1)}, u32[]{:S(2)}, u32[]{:S(2)}) collective-permute-start(bf16[32,2176]{1,0:T(8,128)(2,1)S(1)} %shard_map.89.here), channel_id=1, source_target_pairs={{0,3},{1,4},{2,5},{3,6},{4,7},{5,0},{6,1},{7,2},{8,11},{9,12},{10,... | collective-permute-start | bytes 417800 | tf_op jit(solution)/shard_map/ppermute | solution.py:230
  102.8 6.0 %collective-permute-done.7.by_five = bf16[32,2176]{1,0:T(8,128)(2,1)S(1)} collective-permute-done((bf16[32,2176]{1,0:T(8,128)(2,1)S(1)}, bf16[32,2176]{1,0:T(8,128)(2,1)S(1)}, u32[]{:S(2)}, u32[]{:S(2)}) %collective-permute-start.7) | collective-permute-done | bytes 139296 | tf_op jit(solution)/shard_map/ppermute | solution.py:230
  108.8 2.9 %collective-permute-start.9 = (bf16[64,2176]{1,0:T(8,128)(2,1)S(1)}, bf16[64,2176]{1,0:T(8,128)(2,1)S(1)}, u32[]{:S(2)}, u32[]{:S(2)}) collective-permute-start(bf16[64,2176]{1,0:T(8,128)(2,1)S(1)} %pad_maximum_fusion), channel_id=1, source_target_pairs={{0,7},{1,0},{2,1},{3,2},{4,3},{5,4},{6,5},{7,6},{8,15},{9,8},{10,9... | collective-permute-start | bytes 835592 | tf_op jit(solution)/shard_map/ppermute | solution.py:230
  111.7 2.4 %collective-permute-start.8 = (bf16[64,2176]{1,0:T(8,128)(2,1)S(1)}, bf16[64,2176]{1,0:T(8,128)(2,1)S(1)}, u32[]{:S(2)}, u32[]{:S(2)}) collective-permute-start(bf16[64,2176]{1,0:T(8,128)(2,1)S(1)} %pad_maximum_fusion), channel_id=1, source_target_pairs={{0,1},{1,2},{2,3},{3,4},{4,5},{5,6},{6,7},{7,0},{8,9},{9,10},{10,1... | collective-permute-start | bytes 835592 | tf_op jit(solution)/shard_map/ppermute | solution.py:230
  114.1 0.4 collective-permute-done.6.by_three
  114.5 5.2 %collective-permute-start.10 = (bf16[32,2176]{1,0:T(8,128)(2,1)S(1)}, bf16[32,2176]{1,0:T(8,128)(2,1)S(1)}, u32[]{:S(2)}, u32[]{:S(2)}) collective-permute-start(bf16[32,2176]{1,0:T(8,128)(2,1)S(1)} %collective-permute-done.6.by_three), channel_id=1, source_target_pairs={{0,7},{1,0},{2,1},{3,2},{4,3},{5,4},{6,5},{7,6},{8,15},{9,8},{10,9... | collective-permute-start | bytes 417800 | tf_op jit(solution)/shard_map/ppermute | solution.py:230
  119.7 2.2 %collective-permute-done.10.late = bf16[32,2176]{1,0:T(8,128)(2,1)S(1)} collective-permute-done((bf16[32,2176]{1,0:T(8,128)(2,1)S(1)}, bf16[32,2176]{1,0:T(8,128)(2,1)S(1)}, u32[]{:S(2)}, u32[]{:S(2)}) %collective-permute-start.10) | collective-permute-done | bytes 139296 | tf_op jit(solution)/shard_map/ppermute | solution.py:230
  121.9 0.0 collective-permute-done.9.from_right
  121.9 2.1 %collective-permute-done.8.from_left = bf16[64,2176]{1,0:T(8,128)(2,1)S(1)} collective-permute-done((bf16[64,2176]{1,0:T(8,128)(2,1)S(1)}, bf16[64,2176]{1,0:T(8,128)(2,1)S(1)}, u32[]{:S(2)}, u32[]{:S(2)}) %collective-permute-start.8) | collective-permute-done | bytes 278560 | tf_op jit(solution)/shard_map/ppermute | solution.py:230
  124.0 0.8 shard_map.90
  124.8 0.1 reshape.18
  124.9 22.5 %all_to_all.10 = bf16[128,2,640]{2,1,0:T(2,128)(2,1)S(1)} all-to-all(bf16[128,2,640]{2,1,0:T(2,128)(2,1)S(1)} %reshape.18), channel_id=1, replica_groups=mesh['node'=128,'local'=8] {'node'}, dimensions={0} | all-to-all | bytes 655360 | tf_op jit(solution)/shard_map/all_to_all | solution.py:264
  147.4 0.1 reshape.19.rows_back
  147.6 0.8 shard_map.91
  (1 shorter events, 0.0 us)
Async XLA Ops:
  0.6 26.9 %copy-start.3 = (s32[16,8]{0,1:T(8,128)S(1)}, s32[16,8]{0,1:T(8,128)}, u32[]{:S(2)}) copy-start(s32[16,8]{0,1:T(8,128)} %param.10) | copy-start | bytes 1540
  0.6 26.9 %copy-start.4 = (f32[16,8]{0,1:T(8,128)S(1)}, f32[16,8]{0,1:T(8,128)}, u32[]{:S(2)}) copy-start(f32[16,8]{0,1:T(8,128)} %param.9) | copy-start | bytes 1540
  2.9 45.4 %copy-start = (bf16[1,512,1024]{2,1,0:T(8,128)(2,1)S(1)}, bf16[1,512,1024]{2,1,0:T(8,128)(2,1)}, u32[]{:S(2)}) copy-start(bf16[1,512,1024]{2,1,0:T(8,128)(2,1)} %param.11) | copy-start | bytes 3145732
  2.9 45.4 %copy-start.1 = (bf16[1,512,1024]{2,1,0:T(8,128)(2,1)S(1)}, bf16[1,512,1024]{2,1,0:T(8,128)(2,1)}, u32[]{:S(2)}) copy-start(bf16[1,512,1024]{2,1,0:T(8,128)(2,1)} %param.12) | copy-start | bytes 3145732
  2.9 45.2 %all-to-all-start = ((bf16[128,2,1024]{2,1,0:T(2,128)(2,1)}), bf16[128,2,1024]{2,1,0:T(2,128)(2,1)S(1)}, u32[]{:S(2)}, u32[]{:S(2)}) async-start(bf16[128,2,1024]{2,1,0:T(2,128)(2,1)} %shard_map.87), calls=%async_computation | async-start | bytes 1048576 | tf_op jit(solution)/shard_map/all_to_all | solution.py:209
  48.3 1.2 copy-start.2
  50.7 12.5 %collective-permute-start.4 = (bf16[32,3072]{1,0:T(8,128)(2,1)S(1)}, bf16[32,3072]{1,0:T(8,128)(2,1)S(1)}, u32[]{:S(2)}, u32[]{:S(2)}) collective-permute-start(bf16[32,3072]{1,0:T(8,128)(2,1)S(1)} %get-tuple-element.18), channel_id=1, source_target_pairs={{0,7},{1,0},{2,1},{3,2},{4,3},{5,4},{6,5},{7,6},{8,15},{9,8},{10,9... | collective-permute-start | bytes 589832 | tf_op jit(solution)/shard_map/ppermute | solution.py:230
  56.6 23.0 %collective-permute-start = (bf16[32,3072]{1,0:T(8,128)(2,1)S(1)}, bf16[32,3072]{1,0:T(8,128)(2,1)S(1)}, u32[]{:S(2)}, u32[]{:S(2)}) collective-permute-start(bf16[32,3072]{1,0:T(8,128)(2,1)S(1)} %get-tuple-element.15), channel_id=1, source_target_pairs={{0,5},{1,6},{2,7},{3,0},{4,1},{5,2},{6,3},{7,4},{8,13},{9,14},{10,... | collective-permute-start | bytes 589832 | tf_op jit(solution)/shard_map/ppermute | solution.py:230
  60.8 13.7 %collective-permute-start.1 = (bf16[64,3072]{1,0:T(8,128)(2,1)S(1)}, bf16[64,3072]{1,0:T(8,128)(2,1)S(1)}, u32[]{:S(2)}, u32[]{:S(2)}) collective-permute-start(bf16[64,3072]{1,0:T(8,128)(2,1)S(1)} %get-tuple-element.16), channel_id=1, source_target_pairs={{0,1},{1,2},{2,3},{3,4},{4,5},{5,6},{6,7},{7,0},{8,9},{9,10},{10,1... | collective-permute-start | bytes 1179656 | tf_op jit(solution)/shard_map/ppermute | solution.py:230
  63.3 16.3 %collective-permute-start.5 = (bf16[32,3072]{1,0:T(8,128)(2,1)S(1)}, bf16[32,3072]{1,0:T(8,128)(2,1)S(1)}, u32[]{:S(2)}, u32[]{:S(2)}) collective-permute-start(bf16[32,3072]{1,0:T(8,128)(2,1)S(1)} %add_convert_fusion), channel_id=1, source_target_pairs={{0,7},{1,0},{2,1},{3,2},{4,3},{5,4},{6,5},{7,6},{8,15},{9,8},{10,9... | collective-permute-start | bytes 589832 | tf_op jit(solution)/shard_map/ppermute | solution.py:230
  74.6 17.8 %collective-permute-start.3 = (bf16[32,3072]{1,0:T(8,128)(2,1)S(1)}, bf16[32,3072]{1,0:T(8,128)(2,1)S(1)}, u32[]{:S(2)}, u32[]{:S(2)}) collective-permute-start(bf16[32,3072]{1,0:T(8,128)(2,1)S(1)} %get-tuple-element.22), channel_id=1, source_target_pairs={{0,3},{1,4},{2,5},{3,6},{4,7},{5,0},{6,1},{7,2},{8,11},{9,12},{10,... | collective-permute-start | bytes 589832 | tf_op jit(solution)/shard_map/ppermute | solution.py:230
  76.5 19.0 %collective-permute-start.2 = (bf16[32,3072]{1,0:T(8,128)(2,1)S(1)}, bf16[32,3072]{1,0:T(8,128)(2,1)S(1)}, u32[]{:S(2)}, u32[]{:S(2)}) collective-permute-start(bf16[32,3072]{1,0:T(8,128)(2,1)S(1)} %get-tuple-element.23), channel_id=1, source_target_pairs={{0,1},{1,2},{2,3},{3,4},{4,5},{5,6},{6,7},{7,0},{8,9},{9,10},{10,1... | collective-permute-start | bytes 589832 | tf_op jit(solution)/shard_map/ppermute | solution.py:230
  95.7 13.0 %collective-permute-start.7 = (bf16[32,2176]{1,0:T(8,128)(2,1)S(1)}, bf16[32,2176]{1,0:T(8,128)(2,1)S(1)}, u32[]{:S(2)}, u32[]{:S(2)}) collective-permute-start(bf16[32,2176]{1,0:T(8,128)(2,1)S(1)} %shard_map.89.here), channel_id=1, source_target_pairs={{0,5},{1,6},{2,7},{3,0},{4,1},{5,2},{6,3},{7,4},{8,13},{9,14},{10,... | collective-permute-start | bytes 417800 | tf_op jit(solution)/shard_map/ppermute | solution.py:230
  98.5 15.9 %collective-permute-start.6 = (bf16[32,2176]{1,0:T(8,128)(2,1)S(1)}, bf16[32,2176]{1,0:T(8,128)(2,1)S(1)}, u32[]{:S(2)}, u32[]{:S(2)}) collective-permute-start(bf16[32,2176]{1,0:T(8,128)(2,1)S(1)} %shard_map.89.here), channel_id=1, source_target_pairs={{0,3},{1,4},{2,5},{3,6},{4,7},{5,0},{6,1},{7,2},{8,11},{9,12},{10,... | collective-permute-start | bytes 417800 | tf_op jit(solution)/shard_map/ppermute | solution.py:230
  108.8 13.1 %collective-permute-start.9 = (bf16[64,2176]{1,0:T(8,128)(2,1)S(1)}, bf16[64,2176]{1,0:T(8,128)(2,1)S(1)}, u32[]{:S(2)}, u32[]{:S(2)}) collective-permute-start(bf16[64,2176]{1,0:T(8,128)(2,1)S(1)} %pad_maximum_fusion), channel_id=1, source_target_pairs={{0,7},{1,0},{2,1},{3,2},{4,3},{5,4},{6,5},{7,6},{8,15},{9,8},{10,9... | collective-permute-start | bytes 835592 | tf_op jit(solution)/shard_map/ppermute | solution.py:230
  111.7 12.3 %collective-permute-start.8 = (bf16[64,2176]{1,0:T(8,128)(2,1)S(1)}, bf16[64,2176]{1,0:T(8,128)(2,1)S(1)}, u32[]{:S(2)}, u32[]{:S(2)}) collective-permute-start(bf16[64,2176]{1,0:T(8,128)(2,1)S(1)} %pad_maximum_fusion), channel_id=1, source_target_pairs={{0,1},{1,2},{2,3},{3,4},{4,5},{5,6},{6,7},{7,0},{8,9},{9,10},{10,1... | collective-permute-start | bytes 835592 | tf_op jit(solution)/shard_map/ppermute | solution.py:230
  114.5 7.4 %collective-permute-start.10 = (bf16[32,2176]{1,0:T(8,128)(2,1)S(1)}, bf16[32,2176]{1,0:T(8,128)(2,1)S(1)}, u32[]{:S(2)}, u32[]{:S(2)}) collective-permute-start(bf16[32,2176]{1,0:T(8,128)(2,1)S(1)} %collective-permute-done.6.by_three), channel_id=1, source_target_pairs={{0,7},{1,0},{2,1},{3,2},{4,3},{5,4},{6,5},{7,6},{8,15},{9,8},{10,9... | collective-permute-start | bytes 417800 | tf_op jit(solution)/shard_map/ppermute | solution.py:230
